TPU v7x, 32 devices: a whole 2x2x4 slice. The times are simulated.
32 devices in a mesh: section: 2 (over y), dp: 16 (over z, x, core).
Axes of the slice: x: 2, y: 2, z: 4, core: 2. Of those that a mesh axis runs over, the one named last changes fastest.
Arguments:
- features: bfloat16 [32, 1024, 512], P('dp', None, 'section'), may hold values from -6 to 6
- conv_weight: bfloat16 [1024, 512], P(('section', 'dp')), may hold values from -0.1875 to 0.1875
- ln0_gain: bfloat16 [512], P(('section', 'dp')), may hold values from 0.25 to 1.75
- ln0_bias: bfloat16 [512], P(('section', 'dp')), may hold values from -1.75 to 1.75
- proj0_weight: bfloat16 [512, 768], P(('section', 'dp')), may hold values from -0.25 to 0.25
- proj0_bias: bfloat16 [768], P(('section', 'dp')), may hold values from -1.75 to 1.75
- mask_emb: bfloat16 [768], P(('section', 'dp')), may hold values from -6 to 6
- qkv_weight: bfloat16 [768, 2304], P(('section', 'dp')), may hold values from -0.21875 to 0.21875
- qv_bias: bfloat16 [1536], P(('section', 'dp')), may hold values from -1.75 to 1.75
- out_weight: bfloat16 [768, 768], P(('section', 'dp')), may hold values from -1.75 to 1.75
- out_bias: bfloat16 [768], P(('section', 'dp')), may hold values from -1.75 to 1.75
- ln1_gain: bfloat16 [768], P(('section', 'dp')), may hold values from 0.25 to 1.75
- ln1_bias: bfloat16 [768], P(('section', 'dp')), may hold values from -1.75 to 1.75
- up_weight: bfloat16 [768, 3072], P(('section', 'dp')), may hold values from -0.21875 to 0.21875
- up_bias: bfloat16 [3072], P(('section', 'dp')), may hold values from -1.75 to 1.75
- down_weight: bfloat16 [3072, 768], P(('section', 'dp')), may hold values from -0.109375 to 0.109375
- down_bias: bfloat16 [768], P(('section', 'dp')), may hold values from -1.75 to 1.75
- ln2_gain: bfloat16 [768], P(('section', 'dp')), may hold values from 0.25 to 1.75
- ln2_bias: bfloat16 [768], P(('section', 'dp')), may hold values from -1.75 to 1.75
- final_weight: bfloat16 [768, 256], P(('section', 'dp')), may hold values from -0.21875 to 0.21875
- final_bias: bfloat16 [256], P(('section', 'dp')), may hold values from -1.75 to 1.75
- codebook: bfloat16 [2, 320, 128], replicated, may hold values from -6 to 6
- lengths: int32 [32, 3], P('dp'), may hold values from 32 to 384, as said below
- mask_pos: int32 [32, 256], P('dp'), may hold values from 0 to 511, as said below
- distractors: int32 [32, 256, 100], P('dp'), may hold values from 0 to 511, as said below
- target_ids: int32 [32, 2, 512], P('dp'), may hold values from 0 to 319
Outputs:
- loss: float32 [32], P('dp')
- features_grad: float32 [32, 1024, 512], P('dp', None, 'section')
- conv_weight_grad: float32 [1024, 512], P(('section', 'dp'))
- ln0_gain_grad: float32 [512], P(('section', 'dp'))
- ln0_bias_grad: float32 [512], P(('section', 'dp'))
- proj0_weight_grad: float32 [512, 768], P(('section', 'dp'))
- proj0_bias_grad: float32 [768], P(('section', 'dp'))
- mask_emb_grad: float32 [768], P(('section', 'dp'))
- qkv_weight_grad: float32 [768, 2304], P(('section', 'dp'))
- qv_bias_grad: float32 [1536], P(('section', 'dp'))
- out_weight_grad: float32 [768, 768], P(('section', 'dp'))
- out_bias_grad: float32 [768], P(('section', 'dp'))
- ln1_gain_grad: float32 [768], P(('section', 'dp'))
- ln1_bias_grad: float32 [768], P(('section', 'dp'))
- up_weight_grad: float32 [768, 3072], P(('section', 'dp'))
- up_bias_grad: float32 [3072], P(('section', 'dp'))
- down_weight_grad: float32 [3072, 768], P(('section', 'dp'))
- down_bias_grad: float32 [768], P(('section', 'dp'))
- ln2_gain_grad: float32 [768], P(('section', 'dp'))
- ln2_bias_grad: float32 [768], P(('section', 'dp'))
- final_weight_grad: float32 [768, 256], P(('section', 'dp'))
- final_bias_grad: float32 [256], P(('section', 'dp'))
Inputs may be any that keep to these rules, and one draw needn't show every extreme that they name: Each row holds the lengths of the 3 utterances of one micro-batch in frame order; they sum to 512. `mask_pos`: each row holds 256 distinct frames of one micro-batch. distractors[b, k] are frames of the utterance of mask_pos[b, k], never that frame itself.
All inputs are finite; a program needn't handle non-finite values.
Results may differ from a plain program's by a relative error of at most 0.022.
Values may be sent and summed in bfloat16 or wider, within the bound.
No kernel may reach another device: no remote copies, remote signals or barrier semaphores. Data moves between devices by JAX's collectives and lax.ppermute only.
A program may use at most 320 MiB of HBM per device.

v0:
```python
import math

import jax
import jax.numpy as jnp
from jax import lax
from jax.sharding import PartitionSpec as P

D = 768
H = 12
HD = 64
C = 512
UTTS = 3
MB_DEV = 2
FMB = 512


norm_eps = 1e-05
unit_eps = 1e-06
sharpness_divisor = 0.1
masked_score = -1000000000.0
precise = lax.Precision.HIGHEST


def shifted(value, axis, steps):
    count = lax.axis_size(axis)
    leading, last = (max(0, -steps), min(count, count - steps))
    return lax.ppermute(value, axis, [(source, source + steps) for source in range(leading, last)])


def plain_dot(left_side, right_side):
    return jnp.dot(left_side, right_side, preferred_element_type=jnp.float32)


def left_dot(left_side, right_side):
    return lax.dot_general(
        left_side, right_side, (((0,), (0,)), ((), ())), preferred_element_type=jnp.float32
    )


def right_dot(left_side, right_side):
    return lax.dot_general(
        left_side, right_side, (((1,), (1,)), ((), ())), preferred_element_type=jnp.float32
    )


def layer_normalize(values, norm_gain, norm_shift):
    center = values - jnp.mean(values, axis=-1, keepdims=True)
    spread = jnp.mean(center * center, axis=-1, keepdims=True)
    return center * lax.rsqrt(spread + norm_eps) * norm_gain + norm_shift


def exact_gelu(values):
    return jax.nn.gelu(values, approximate=False)


def front_norm(conv_out, norm_gain, norm_shift):
    return layer_normalize(exact_gelu(conv_out), norm_gain, norm_shift)


def contrastive(projected, code_table, target_rows, positions, chosen):
    entries = jnp.arange(code_table.shape[1], dtype=jnp.int32)
    first_pick = (target_rows[0][:, None] == entries[None, :]).astype(jnp.float32)
    second_pick = (target_rows[1][:, None] == entries[None, :]).astype(jnp.float32)
    targets = jnp.concatenate(
        [
            jnp.dot(
                first_pick, code_table[0], precision=precise, preferred_element_type=jnp.float32
            ),
            jnp.dot(
                second_pick, code_table[1], precision=precise, preferred_element_type=jnp.float32
            ),
        ],
        axis=1,
    )
    targets = targets * lax.rsqrt(jnp.sum(targets * targets, axis=1, keepdims=True) + unit_eps)
    picked = jnp.take(projected, positions, axis=0)
    picked = picked * lax.rsqrt(jnp.sum(picked * picked, axis=1, keepdims=True) + unit_eps)
    angular_agreement = jnp.dot(
        picked, targets.T, precision=precise, preferred_element_type=jnp.float32
    )
    contender_entries = jnp.concatenate([positions[:, None], chosen], axis=1)
    agreement_scores_raw = (
        jnp.take_along_axis(angular_agreement, contender_entries, axis=1) / sharpness_divisor
    )
    return jnp.mean(jax.nn.logsumexp(agreement_scores_raw, axis=1) - agreement_scores_raw[:, 0])


def joined_sum(grads):
    return (
        lax.psum_scatter(grads[0], ("section", "dp"), scatter_dimension=0, tiled=True),
        lax.psum_scatter(grads[1], ("section", "dp"), scatter_dimension=0, tiled=True),
        lax.psum_scatter(grads[2], ("section", "dp"), scatter_dimension=0, tiled=True),
        lax.psum_scatter(grads[3], ("section", "dp"), scatter_dimension=0, tiled=True),
        lax.psum_scatter(grads[4], ("section", "dp"), scatter_dimension=0, tiled=True),
        lax.psum_scatter(grads[5], ("section", "dp"), scatter_dimension=0, tiled=True),
        lax.psum_scatter(grads[6], ("section", "dp"), scatter_dimension=0, tiled=True),
        lax.psum_scatter(grads[7], ("section", "dp"), scatter_dimension=0, tiled=True),
        lax.psum_scatter(grads[8], ("section", "dp"), scatter_dimension=0, tiled=True),
        lax.psum_scatter(grads[9], ("section", "dp"), scatter_dimension=0, tiled=True),
        lax.psum_scatter(grads[10], ("section", "dp"), scatter_dimension=0, tiled=True),
        lax.psum_scatter(grads[11], ("section", "dp"), scatter_dimension=0, tiled=True),
        lax.psum_scatter(grads[12], ("section", "dp"), scatter_dimension=0, tiled=True),
        lax.psum_scatter(grads[13], ("section", "dp"), scatter_dimension=0, tiled=True),
        lax.psum_scatter(grads[14], ("section", "dp"), scatter_dimension=0, tiled=True),
        lax.psum_scatter(grads[15], ("section", "dp"), scatter_dimension=0, tiled=True),
        lax.psum_scatter(grads[16], ("section", "dp"), scatter_dimension=0, tiled=True),
        lax.psum_scatter(grads[17], ("section", "dp"), scatter_dimension=0, tiled=True),
        lax.psum_scatter(grads[18], ("section", "dp"), scatter_dimension=0, tiled=True),
        lax.psum_scatter(grads[19], ("section", "dp"), scatter_dimension=0, tiled=True),
    )


def body(
    features,
    conv_weight,
    ln0_gain,
    ln0_bias,
    proj0_weight,
    proj0_bias,
    mask_emb,
    qkv_weight,
    qv_bias,
    out_weight,
    out_bias,
    ln1_gain,
    ln1_bias,
    up_weight,
    up_bias,
    down_weight,
    down_bias,
    ln2_gain,
    ln2_bias,
    final_weight,
    final_bias,
    codebook,
    lengths,
    mask_pos,
    distractors,
    target_ids,
):
    section_index = lax.axis_index("section")
    gathered = (
        lax.all_gather(conv_weight, ("section", "dp"), axis=0, tiled=True),
        lax.all_gather(ln0_gain, ("section", "dp"), axis=0, tiled=True),
        lax.all_gather(ln0_bias, ("section", "dp"), axis=0, tiled=True),
        lax.all_gather(proj0_weight, ("section", "dp"), axis=0, tiled=True),
        lax.all_gather(proj0_bias, ("section", "dp"), axis=0, tiled=True),
        lax.all_gather(mask_emb, ("section", "dp"), axis=0, tiled=True),
        lax.all_gather(qkv_weight, ("section", "dp"), axis=0, tiled=True),
        lax.all_gather(qv_bias, ("section", "dp"), axis=0, tiled=True),
        lax.all_gather(out_weight, ("section", "dp"), axis=0, tiled=True),
        lax.all_gather(out_bias, ("section", "dp"), axis=0, tiled=True),
        lax.all_gather(ln1_gain, ("section", "dp"), axis=0, tiled=True),
        lax.all_gather(ln1_bias, ("section", "dp"), axis=0, tiled=True),
        lax.all_gather(up_weight, ("section", "dp"), axis=0, tiled=True),
        lax.all_gather(up_bias, ("section", "dp"), axis=0, tiled=True),
        lax.all_gather(down_weight, ("section", "dp"), axis=0, tiled=True),
        lax.all_gather(down_bias, ("section", "dp"), axis=0, tiled=True),
        lax.all_gather(ln2_gain, ("section", "dp"), axis=0, tiled=True),
        lax.all_gather(ln2_bias, ("section", "dp"), axis=0, tiled=True),
        lax.all_gather(final_weight, ("section", "dp"), axis=0, tiled=True),
        lax.all_gather(final_bias, ("section", "dp"), axis=0, tiled=True),
    )
    (
        conv_full,
        gain_zero,
        shift_zero,
        proj_full,
        proj_shift,
        mask_full,
        qkv_full,
        qv_full,
        out_full,
        out_shift,
        gain_one,
        shift_one,
        up_full,
        up_shift,
        down_full,
        down_shift,
        gain_two,
        shift_two,
        final_full,
        final_shift,
    ) = gathered
    gain_zero = gain_zero.astype(jnp.float32)
    shift_zero = shift_zero.astype(jnp.float32)
    proj_shift = proj_shift.astype(jnp.float32)
    qv_full = qv_full.astype(jnp.float32)
    out_shift = out_shift.astype(jnp.float32)
    gain_one = gain_one.astype(jnp.float32)
    shift_one = shift_one.astype(jnp.float32)
    up_shift = up_shift.astype(jnp.float32)
    down_shift = down_shift.astype(jnp.float32)
    gain_two = gain_two.astype(jnp.float32)
    shift_two = shift_two.astype(jnp.float32)
    final_shift = final_shift.astype(jnp.float32)
    bias_three = jnp.concatenate([qv_full[:D], jnp.zeros((D,), jnp.float32), qv_full[D:]])
    code_table = codebook.astype(jnp.float32)
    frames_in = lax.all_gather(features, "section", axis=2, tiled=True)
    score_scale = 1.0 / math.sqrt(HD)
    frame_ids = jnp.arange(FMB, dtype=jnp.int32)
    front_members = gathered[:5]
    block_members = gathered[5:]

    def front_forward(feature_rows):
        frame_pairs = feature_rows.reshape(FMB, 2 * C)
        conv_out = plain_dot(frame_pairs, conv_full)
        normed = front_norm(conv_out, gain_zero, shift_zero).astype(jnp.bfloat16)
        encoded = (plain_dot(normed, proj_full) + proj_shift).astype(jnp.bfloat16)
        return (encoded, conv_out)

    def front_blank(feature_rows):
        return (jnp.zeros((FMB, D), jnp.bfloat16), jnp.zeros((FMB, C), jnp.float32))

    def attention_scores(queries, key_rows, same_utt):
        raw_scores = (
            jnp.einsum("qhd,khd->hqk", queries, key_rows, preferred_element_type=jnp.float32)
            * score_scale
        )
        return jnp.where(same_utt, raw_scores, masked_score)

    def block_step(operands):
        received, utterance_lens, positions, chosen, target_rows = operands
        mask_rows = jnp.any(frame_ids[:, None] == positions[None, :], axis=1)[:, None]
        stop_positions = jnp.cumsum(utterance_lens)
        segment = jnp.sum(
            (frame_ids[:, None] >= stop_positions[None, : UTTS - 1]).astype(jnp.int32), axis=1
        )
        same_utt = (segment[:, None] == segment[None, :])[None]
        inputs = jnp.where(mask_rows, mask_full[None, :], received)
        qkv_rows = (plain_dot(inputs, qkv_full) + bias_three).astype(jnp.bfloat16)
        queries = qkv_rows[:, :D].reshape(FMB, H, HD)
        key_rows = qkv_rows[:, D : 2 * D].reshape(FMB, H, HD)
        value_rows = qkv_rows[:, 2 * D :].reshape(FMB, H, HD)
        scores = attention_scores(queries, key_rows, same_utt)
        top_score = jnp.max(scores, axis=-1, keepdims=True)
        exp_scores = jnp.exp(scores - top_score)
        row_total = jnp.sum(exp_scores, axis=-1, keepdims=True)
        log_total = top_score + jnp.log(row_total)
        attention = (exp_scores / row_total).astype(jnp.bfloat16)
        mixed_heads = (
            jnp.einsum("hqk,khd->qhd", attention, value_rows, preferred_element_type=jnp.float32)
            .reshape(FMB, D)
            .astype(jnp.bfloat16)
        )
        attn_out = plain_dot(mixed_heads, out_full) + out_shift
        first_norm, leading_reverse_pass = jax.vjp(
            layer_normalize, inputs.astype(jnp.float32) + attn_out, gain_one, shift_one
        )
        first_low = first_norm.astype(jnp.bfloat16)
        hidden_pre = plain_dot(first_low, up_full) + up_shift
        hidden_act, gelu_back = jax.vjp(exact_gelu, hidden_pre)
        hidden_low = hidden_act.astype(jnp.bfloat16)
        ffn_out = plain_dot(hidden_low, down_full) + down_shift
        second_norm, second_back = jax.vjp(
            layer_normalize, first_low.astype(jnp.float32) + ffn_out, gain_two, shift_two
        )
        second_low = second_norm.astype(jnp.bfloat16)
        projected = plain_dot(second_low, final_full) + final_shift

        def objective(proj_rows):
            return contrastive(proj_rows, code_table, target_rows, positions, chosen)

        loss_value, loss_back = jax.vjp(objective, projected)
        (d_projected,) = loss_back(jnp.ones((), jnp.float32))
        d_proj_low = d_projected.astype(jnp.bfloat16)
        grad_final = left_dot(second_low, d_proj_low)
        grad_final_shift = jnp.sum(d_proj_low.astype(jnp.float32), axis=0)
        d_second_res, grad_gain_two, grad_shift_two = second_back(right_dot(d_proj_low, final_full))
        d_ffn_low = d_second_res.astype(jnp.bfloat16)
        grad_down = left_dot(hidden_low, d_ffn_low)
        grad_down_shift = jnp.sum(d_ffn_low.astype(jnp.float32), axis=0)
        (d_hidden_pre,) = gelu_back(right_dot(d_ffn_low, down_full))
        d_pre_low = d_hidden_pre.astype(jnp.bfloat16)
        grad_up = left_dot(first_low, d_pre_low)
        grad_up_shift = jnp.sum(d_pre_low.astype(jnp.float32), axis=0)
        d_first_res, grad_gain_one, grad_shift_one = leading_reverse_pass(
            right_dot(d_pre_low, up_full) + d_second_res
        )
        d_attn_low = d_first_res.astype(jnp.bfloat16)
        grad_out = left_dot(mixed_heads, d_attn_low)
        grad_out_shift = jnp.sum(d_attn_low.astype(jnp.float32), axis=0)
        d_mixed = right_dot(d_attn_low, out_full).astype(jnp.bfloat16).reshape(FMB, H, HD)
        again = jnp.exp(attention_scores(queries, key_rows, same_utt) - log_total)
        d_values = jnp.einsum(
            "hqk,qhd->khd", again.astype(jnp.bfloat16), d_mixed, preferred_element_type=jnp.float32
        )
        d_attention = jnp.einsum(
            "qhd,khd->hqk", d_mixed, value_rows, preferred_element_type=jnp.float32
        )
        d_scores = (
            again * (d_attention - jnp.sum(again * d_attention, axis=-1, keepdims=True))
        ).astype(jnp.bfloat16)
        d_queries = (
            jnp.einsum("hqk,khd->qhd", d_scores, key_rows, preferred_element_type=jnp.float32)
            * score_scale
        )
        d_keys = (
            jnp.einsum("hqk,qhd->khd", d_scores, queries, preferred_element_type=jnp.float32)
            * score_scale
        )
        d_qkv = jnp.concatenate(
            [d_queries.reshape(FMB, D), d_keys.reshape(FMB, D), d_values.reshape(FMB, D)], axis=1
        ).astype(jnp.bfloat16)
        grad_qkv = left_dot(inputs, d_qkv)
        qkv_sums = jnp.sum(d_qkv.astype(jnp.float32), axis=0)
        grad_qv = jnp.concatenate([qkv_sums[:D], qkv_sums[2 * D :]])
        d_inputs = right_dot(d_qkv, qkv_full) + d_first_res
        grad_mask = jnp.sum(jnp.where(mask_rows, d_inputs, 0.0), axis=0)
        d_send = jnp.where(mask_rows, 0.0, d_inputs).astype(jnp.bfloat16)
        return (
            d_send,
            (
                grad_mask,
                grad_qkv,
                grad_qv,
                grad_out,
                grad_out_shift,
                grad_gain_one,
                grad_shift_one,
                grad_up,
                grad_up_shift,
                grad_down,
                grad_down_shift,
                grad_gain_two,
                grad_shift_two,
                grad_final,
                grad_final_shift,
            ),
            loss_value,
        )

    def block_blank(operands):
        return (
            jnp.zeros((FMB, D), jnp.bfloat16),
            tuple((jnp.zeros(member.shape, jnp.float32) for member in block_members)),
            jnp.zeros((), jnp.float32),
        )

    def front_backward(operands):
        d_encoded, conv_out, feature_rows = operands
        frame_pairs = feature_rows.reshape(FMB, 2 * C)
        normed, norm_back = jax.vjp(front_norm, conv_out, gain_zero, shift_zero)
        normed_low = normed.astype(jnp.bfloat16)
        grad_proj = left_dot(normed_low, d_encoded)
        grad_proj_shift = jnp.sum(d_encoded.astype(jnp.float32), axis=0)
        d_conv, grad_gain_zero, grad_shift_zero = norm_back(right_dot(d_encoded, proj_full))
        d_conv_low = d_conv.astype(jnp.bfloat16)
        grad_conv = left_dot(frame_pairs, d_conv_low)
        d_frames = right_dot(d_conv_low, conv_full).reshape(2 * FMB, C)
        return ((grad_conv, grad_gain_zero, grad_shift_zero, grad_proj, grad_proj_shift), d_frames)

    def front_rest(operands):
        return (
            tuple((jnp.zeros(member.shape, jnp.float32) for member in front_members)),
            jnp.zeros((2 * FMB, C), jnp.float32),
        )

    summed = tuple((jnp.zeros(member.shape, jnp.float32) for member in gathered))
    micro_losses = []
    frame_grads = []
    for micro_index in range(MB_DEV):
        feature_rows = frames_in[micro_index]
        encoded, conv_out = lax.cond(section_index == 0, front_forward, front_blank, feature_rows)
        received = shifted(encoded, "section", 1)
        operands = (
            received,
            lengths[micro_index],
            mask_pos[micro_index],
            distractors[micro_index],
            target_ids[micro_index],
        )
        d_send, block_grads, loss_value = lax.cond(
            section_index == 1, block_step, block_blank, operands
        )
        d_encoded = shifted(d_send, "section", -1)
        front_grads, d_frames = lax.cond(
            section_index == 0, front_backward, front_rest, (d_encoded, conv_out, feature_rows)
        )
        micro_grads = front_grads + block_grads
        micro_losses.append(loss_value)
        frame_grads.append(d_frames)
        summed = tuple((running + grad_part for running, grad_part in zip(summed, micro_grads)))
    shares = joined_sum(summed)
    frame_total = lax.psum_scatter(
        jnp.stack(frame_grads).astype(jnp.bfloat16), "section", scatter_dimension=2, tiled=True
    ).astype(jnp.float32)
    loss_each = lax.psum(jnp.stack(micro_losses), "section")
    return (loss_each, frame_total) + tuple(shares)


def solution(mesh):
    placed = (
        P("dp", None, "section"),
        P(("section", "dp"), None),
        P(("section", "dp")),
        P(("section", "dp")),
        P(("section", "dp"), None),
        P(("section", "dp")),
        P(("section", "dp")),
        P(("section", "dp"), None),
        P(("section", "dp")),
        P(("section", "dp"), None),
        P(("section", "dp")),
        P(("section", "dp")),
        P(("section", "dp")),
        P(("section", "dp"), None),
        P(("section", "dp")),
        P(("section", "dp"), None),
        P(("section", "dp")),
        P(("section", "dp")),
        P(("section", "dp")),
        P(("section", "dp"), None),
        P(("section", "dp")),
        P(),
        P("dp", None),
        P("dp", None),
        P("dp", None, None),
        P("dp", None, None),
    )
    return jax.shard_map(
        body,
        mesh=mesh,
        in_specs=placed,
        out_specs=(
            P("dp"),
            P("dp", None, "section"),
            P(("section", "dp"), None),
            P(("section", "dp")),
            P(("section", "dp")),
            P(("section", "dp"), None),
            P(("section", "dp")),
            P(("section", "dp")),
            P(("section", "dp"), None),
            P(("section", "dp")),
            P(("section", "dp"), None),
            P(("section", "dp")),
            P(("section", "dp")),
            P(("section", "dp")),
            P(("section", "dp"), None),
            P(("section", "dp")),
            P(("section", "dp"), None),
            P(("section", "dp")),
            P(("section", "dp")),
            P(("section", "dp")),
            P(("section", "dp"), None),
            P(("section", "dp")),
        ),
        check_vma=False,
    )
```

profile of v0, /device:TPU:0, one launch (start us, length us, event | category | flops | bytes accessed | tf_op | source)
XLA Modules:
  0.0 2462.1 jit_solution(8603388275729610141)
XLA Ops:
  22.2 42.8 %all-reduce.27 = (bf16[768]{0:T(1024)(128)(2,1)S(1)}, bf16[512]{0:T(512)(128)(2,1)S(1)}, bf16[512]{0:T(512)(128)(2,1)S(1)}, bf16[768]{0:T(1024)(128)(2,1)S(1)}, ...) all-reduce(bf16[768]{0:T(1024)(128)(2,1)S(1)} %dynamic-update-slice, ...), channel_id=1, replica_groups=mesh['section'=2,'dp'=16] {'section','dp'}, use_global_device_ids=true, to_apply=%add | all-reduce | flops 12032 | bytes 48128
  65.0 45.7 %all_gather.68 = bf16[512,768]{1,0:T(8,128)(2,1)} all-gather(bf16[16,768]{1,0:T(8,128)(2,1)} %param.46), channel_id=1, replica_groups=mesh['section'=2,'dp'=16] {'section','dp'}, dimensions={0}, use_global_device_ids=true | all-gather | bytes 811008 | tf_op jit(solution)/shard_map/all_gather | solution.py:146
  110.7 2.6 fusion.196
  113.3 8.0 conditional.8
  113.3 1.8 reshape_squeeze.9
  115.1 4.3 fusion.170
  119.6 1.7 add_convert_fusion.3
  121.3 2.2 collective-permute-start.1
  123.5 10.9 conditional.6
  124.7 7.8 fusion.168
  132.7 1.7 add_convert_fusion
  134.4 2.2 collective-permute-start
  137.6 38.1 %all_gather.82 = bf16[768,256]{1,0:T(8,128)(2,1)S(1)} all-gather(bf16[24,256]{1,0:T(8,128)(2,1)S(1)} %copy-done.117), channel_id=1, replica_groups=mesh['section'=2,'dp'=16] {'section','dp'}, dimensions={0}, use_global_device_ids=true | all-gather | bytes 405504 | tf_op jit(solution)/shard_map/all_gather | solution.py:161
  175.7 47.7 %all-gather.11.cloned.1.call-done = bf16[768,2304]{1,0:T(8,128)(2,1)} async-done(((bf16[24,2304]{1,0:T(8,128)(2,1)}), bf16[768,2304]{1,0:T(8,128)(2,1)}) %all-gather.11.cloned.1.call-update) | async-done | bytes 3538960 | tf_op jit(solution)/shard_map/all_gather | solution.py:149
  223.4 65.1 %all-gather.15.cloned.1.call-done = bf16[768,3072]{1,0:T(8,128)(2,1)} async-done(((bf16[24,3072]{1,0:T(8,128)(2,1)}), bf16[768,3072]{1,0:T(8,128)(2,1)}) %all-gather.15.cloned.1.call-update) | async-done | bytes 4718608 | tf_op jit(solution)/shard_map/all_gather | solution.py:155
  288.6 65.2 %all-gather.17.cloned.1.call-done = bf16[3072,768]{1,0:T(8,128)(2,1)} async-done(((bf16[96,768]{1,0:T(8,128)(2,1)}), bf16[3072,768]{1,0:T(8,128)(2,1)}) %all-gather.17.cloned.1.call-update) | async-done | bytes 4718608 | tf_op jit(solution)/shard_map/all_gather | solution.py:157
  353.8 27.7 %conditional.9 = (bf16[512,768]{1,0:T(8,128)(2,1)}, f32[768]{0:T(1024)S(1)}, f32[768,2304]{1,0:T(8,128)}, f32[1536]{0:T(1024)S(1)}, f32[768,768]{1,0:T(8,128)}, ...) conditional(s32[]{:T(128)} %convert_element_type.279, () %tuple.76, ...), branch_computations={%region_42.45_spmd, %region_43.78_spmd} | conditional | flops 26351572992 | bytes 588681152 | solution.py:374
  353.9 3.3 broadcast.1077
  357.2 1.6 broadcast.1079
  360.5 4.8 broadcast.1080
  366.0 4.3 broadcast.1082
  381.6 1.3 collective-permute-start.3
  382.9 25.6 %conditional.7 = (bf16[512,768]{1,0:T(8,128)(2,1)}, f32[768]{0:T(1024)S(1)}, f32[768,2304]{1,0:T(8,128)}, f32[1536]{0:T(1024)S(1)}, f32[768,768]{1,0:T(8,128)}, ...) conditional(s32[]{:T(128)} %convert_element_type.279, () %tuple.72, ...), branch_computations={%region_4.0_spmd, %region_5.40_spmd} | conditional | flops 26351572992 | bytes 585593088 | solution.py:374
  383.0 3.3 broadcast.991
  386.3 1.6 broadcast.993
  389.7 4.8 broadcast.994
  395.1 4.3 broadcast.996
  408.5 1.3 collective-permute-start.2
  409.8 549.9 %collective-permute-done.3 = bf16[512,768]{1,0:T(8,128)(2,1)} collective-permute-done((bf16[512,768]{1,0:T(8,128)(2,1)}, bf16[512,768]{1,0:T(8,128)(2,1)}, u32[]{:S(2)}, u32[]{:S(2)}) %collective-permute-start.3) | collective-permute-done | bytes 786464 | tf_op jit(solution)/shard_map/ppermute | solution.py:27
  959.7 21.0 conditional.11
  959.7 1.7 copy.161
  961.4 2.7 fusion.174
  964.1 1.9 multiply_reduce_fusion.6
  966.7 3.2 fusion.45
  974.6 2.2 reshape_squeeze.11
  976.8 2.1 convolution_bitcast_fusion.1
  978.9 1.8 copy.175
  980.7 568.6 %collective-permute-done.2 = bf16[512,768]{1,0:T(8,128)(2,1)} collective-permute-done((bf16[512,768]{1,0:T(8,128)(2,1)}, bf16[512,768]{1,0:T(8,128)(2,1)}, u32[]{:S(2)}, u32[]{:S(2)}) %collective-permute-start.2) | collective-permute-done | bytes 786464 | tf_op jit(solution)/shard_map/ppermute | solution.py:27
  1549.3 19.3 conditional.10
  1549.8 1.6 copy.160
  1551.5 2.7 fusion.172
  1554.2 1.9 multiply_reduce_fusion.3
  1556.7 3.2 fusion.32
  1559.9 1.3 convert_reduce_fusion
  1565.1 1.8 convolution_bitcast_fusion
  1566.8 1.8 copy.173
  1568.7 3.0 pad_maximum_fusion.14
  1571.8 2.4 add.506
  1574.2 3.7 add.491
  1578.0 4.1 add.496
  1582.2 4.0 add.488
  1586.3 8.9 add.494
  1595.2 13.0 add.500
  1608.4 11.2 add.502
  1619.9 5.4 psum.7
  1626.3 40.9 %all-reduce.26 = (f32[512]{0:T(512)S(1)}, f32[512]{0:T(512)S(1)}, f32[768]{0:T(1024)S(1)}, f32[768]{0:T(1024)S(1)}, f32[1536]{0:T(1024)S(1)}, /*index=5*/f32[768...) all-reduce(f32[512]{0:T(512)S(1)} %add.489, ...), channel_id=4, replica_groups=mesh['section'=2,'dp'=16] {'section','dp'}, use_global_device_ids=true, to_apply=%region_97.100.clone | all-reduce | flops 12032 | bytes 96256
  1674.8 2.7 convert_element_type.294
  1677.5 26.1 %reduce-scatter.23.cloned.1.call-done = f32[24,256]{1,0:T(8,128)} async-done(((f32[768,256]{1,0:T(8,128)}), f32[24,256]{1,0:T(8,128)}) %reduce-scatter.23.cloned.1.call-update) | async-done | bytes 24592 | tf_op jit(solution)/shard_map/reduce_scatter | solution.py:108
  1703.6 102.8 %reduce-scatter.13.cloned.1.call-done = f32[16,768]{1,0:T(8,128)} async-done(((f32[512,768]{1,0:T(8,128)}), f32[16,768]{1,0:T(8,128)}) %reduce-scatter.13.cloned.1.call-update) | async-done | bytes 49168 | tf_op jit(solution)/shard_map/reduce_scatter | solution.py:93
  1806.3 104.6 %reduce-scatter.17.cloned.1.call-done = f32[24,768]{1,0:T(8,128)} async-done(((f32[768,768]{1,0:T(8,128)}), f32[24,768]{1,0:T(8,128)}) %reduce-scatter.17.cloned.1.call-update) | async-done | bytes 73744 | tf_op jit(solution)/shard_map/reduce_scatter | solution.py:98
  1910.9 138.6 %reduce-scatter.11.cloned.1.call-done = f32[32,512]{1,0:T(8,128)} async-done(((f32[1024,512]{1,0:T(8,128)}), f32[32,512]{1,0:T(8,128)}) %reduce-scatter.11.cloned.1.call-update) | async-done | bytes 65552 | tf_op jit(solution)/shard_map/reduce_scatter | solution.py:90
  2049.6 122.5 %reduce-scatter.15.cloned.1.call-done = f32[24,2304]{1,0:T(8,128)} async-done(((f32[768,2304]{1,0:T(8,128)}), f32[24,2304]{1,0:T(8,128)}) %reduce-scatter.15.cloned.1.call-update) | async-done | bytes 221200 | tf_op jit(solution)/shard_map/reduce_scatter | solution.py:96
  2172.0 141.3 %reduce-scatter.19.cloned.1.call-done = f32[24,3072]{1,0:T(8,128)} async-done(((f32[768,3072]{1,0:T(8,128)}), f32[24,3072]{1,0:T(8,128)}) %reduce-scatter.19.cloned.1.call-update) | async-done | bytes 294928 | tf_op jit(solution)/shard_map/reduce_scatter | solution.py:102
  2313.4 142.0 %reduce-scatter.21.cloned.1.call-done = f32[96,768]{1,0:T(8,128)} async-done(((f32[3072,768]{1,0:T(8,128)}), f32[96,768]{1,0:T(8,128)}) %reduce-scatter.21.cloned.1.call-update) | async-done | bytes 294928 | tf_op jit(solution)/shard_map/reduce_scatter | solution.py:104
  (255 shorter events, 48.4 us)
Async XLA Ops:
  7.2 103.5 %all-gather.7.cloned.1.call-start = ((), (), s32[]{:S(2)}) async-start(), calls=%async_computation.8 | async-start | bytes 3145728 | tf_op jit(solution)/shard_map/all_gather | solution.py:200
  7.9 105.4 %all-gather.9.cloned.1.call-start = ((), (), s32[]{:S(2)}) async-start(), calls=%async_computation.9 | async-start | bytes 1081344 | tf_op jit(solution)/shard_map/all_gather | solution.py:143
  8.7 167.0 %all-gather.13.cloned.1.call-start = ((), (), s32[]{:S(2)}) async-start(), calls=%async_computation.11 | async-start | bytes 1216512 | tf_op jit(solution)/shard_map/all_gather | solution.py:151
  9.4 214.0 %all-gather.11.cloned.1.call-start = ((), (), s32[]{:S(2)}) async-start(), calls=%async_computation.10 | async-start | bytes 3649536 | tf_op jit(solution)/shard_map/all_gather | solution.py:149
  10.0 278.6 %all-gather.15.cloned.1.call-start = ((), (), s32[]{:S(2)}) async-start(), calls=%async_computation.12 | async-start | bytes 4866048 | tf_op jit(solution)/shard_map/all_gather | solution.py:155
  10.6 343.2 %all-gather.17.cloned.1.call-start = ((), (), s32[]{:S(2)}) async-start(), calls=%async_computation.13 | async-start | bytes 4866048 | tf_op jit(solution)/shard_map/all_gather | solution.py:157
  11.1 1663.7 %reduce-scatter.9.cloned.1.call-start = ((), (), s32[]{:S(2)}) async-start(), calls=%async_computation.14 | async-start | bytes 3145728 | tf_op jit(solution)/shard_map/reduce_scatter | solution.py:386
  64.9 288.8 %copy-start.172 = (bf16[768]{0:T(1024)(128)(2,1)}, bf16[768]{0:T(1024)(128)(2,1)S(1)}, u32[]{:S(2)}) copy-start(bf16[768]{0:T(1024)(128)(2,1)S(1)} %get-tuple-element.731) | copy-start | bytes 4612
  64.9 58.5 %copy-start.67 = (f32[512]{0:T(512)}, f32[512]{0:T(512)S(1)}, u32[]{:S(2)}) copy-start(f32[512]{0:T(512)S(1)} %convert_element_type.281) | copy-start | bytes 6148
  65.0 58.5 %copy-start.98 = (f32[512]{0:T(512)}, f32[512]{0:T(512)S(1)}, u32[]{:S(2)}) copy-start(f32[512]{0:T(512)S(1)} %convert_element_type.282) | copy-start | bytes 6148
  113.3 10.2 copy-start.6
  115.1 4.5 copy-start.49
  121.3 54.4 %collective-permute-start.1 = (bf16[512,768]{1,0:T(8,128)(2,1)}, bf16[512,768]{1,0:T(8,128)(2,1)}, u32[]{:S(2)}, u32[]{:S(2)}) collective-permute-start(bf16[512,768]{1,0:T(8,128)(2,1)} %get-tuple-element.404), channel_id=1, source_target_pairs={{0,16},{1,17},{2,18},{3,19},{4,20},{5,21},{6,22},{7,23},{8,24},{9,... | collective-permute-start | bytes 2359304 | tf_op jit(solution)/shard_map/ppermute | solution.py:27
  123.5 13.3 copy-start.62
  123.5 14.1 copy-start.117
  123.5 230.3 %copy-start.155 = (s32[2,256]{1,0:T(2,128)S(1)}, s32[2,256]{1,0:T(2,128)}, u32[]{:S(2)}) copy-start(s32[2,256]{1,0:T(2,128)} %param.65) | copy-start | bytes 6148
  123.5 230.3 %copy-start.177 = (s32[2,3]{1,0:T(2,128)S(1)}, s32[2,3]{1,0:T(2,128)}, u32[]{:S(2)}) copy-start(s32[2,3]{1,0:T(2,128)} %param.64) | copy-start | bytes 76
  124.7 8.0 copy-start.50
  134.4 3.1 copy-start.30
  134.4 248.5 %collective-permute-start = (bf16[512,768]{1,0:T(8,128)(2,1)}, bf16[512,768]{1,0:T(8,128)(2,1)}, u32[]{:S(2)}, u32[]{:S(2)}) collective-permute-start(bf16[512,768]{1,0:T(8,128)(2,1)} %get-tuple-element.402), channel_id=1, source_target_pairs={{0,16},{1,17},{2,18},{3,19},{4,20},{5,21},{6,22},{7,23},{8,24},{9,... | collective-permute-start | bytes 2359304 | tf_op jit(solution)/shard_map/ppermute | solution.py:27
  136.6 217.1 %copy-start.142 = (f32[768]{0:T(1024)}, f32[768]{0:T(1024)S(1)}, u32[]{:S(2)}) copy-start(f32[768]{0:T(1024)S(1)} %convert_element_type.285) | copy-start | bytes 9220
  136.7 217.1 %copy-start.73 = (f32[768]{0:T(1024)}, f32[768]{0:T(1024)S(1)}, u32[]{:S(2)}) copy-start(f32[768]{0:T(1024)S(1)} %convert_element_type.286) | copy-start | bytes 9220
  136.7 217.1 %copy-start.144 = (f32[768]{0:T(1024)}, f32[768]{0:T(1024)S(1)}, u32[]{:S(2)}) copy-start(f32[768]{0:T(1024)S(1)} %convert_element_type.287) | copy-start | bytes 9220
  136.7 217.1 %copy-start.118 = (f32[3072]{0:T(1024)}, f32[3072]{0:T(1024)S(1)}, u32[]{:S(2)}) copy-start(f32[3072]{0:T(1024)S(1)} %convert_element_type.288) | copy-start | bytes 36868
  136.7 217.1 %copy-start.149 = (f32[768]{0:T(1024)}, f32[768]{0:T(1024)S(1)}, u32[]{:S(2)}) copy-start(f32[768]{0:T(1024)S(1)} %convert_element_type.289) | copy-start | bytes 9220
  136.7 217.1 %copy-start.71 = (f32[768]{0:T(1024)}, f32[768]{0:T(1024)S(1)}, u32[]{:S(2)}) copy-start(f32[768]{0:T(1024)S(1)} %convert_element_type.291) | copy-start | bytes 9220
  136.8 217.0 %copy-start.136 = (f32[256]{0:T(256)}, f32[256]{0:T(256)S(1)}, u32[]{:S(2)}) copy-start(f32[256]{0:T(256)S(1)} %convert_element_type.292) | copy-start | bytes 3076
  137.6 216.3 %copy-start.123 = (f32[2304]{0:T(1024)}, f32[2304]{0:T(1024)S(1)}, u32[]{:S(2)}) copy-start(f32[2304]{0:T(1024)S(1)} %pad_maximum_fusion.15) | copy-start | bytes 27652
  381.6 578.1 %collective-permute-start.3 = (bf16[512,768]{1,0:T(8,128)(2,1)}, bf16[512,768]{1,0:T(8,128)(2,1)}, u32[]{:S(2)}, u32[]{:S(2)}) collective-permute-start(bf16[512,768]{1,0:T(8,128)(2,1)} %get-tuple-element.410), channel_id=1, source_target_pairs={{16,0},{17,1},{18,2},{19,3},{20,4},{21,5},{22,6},{23,7},{24,8},{25... | collective-permute-start | bytes 2359304 | tf_op jit(solution)/shard_map/ppermute | solution.py:27
  382.9 576.8 %copy-start.68 = (f32[512]{0:T(512)S(1)}, f32[512]{0:T(512)}, u32[]{:S(2)}) copy-start(f32[512]{0:T(512)} %copy-done.67) | copy-start | bytes 6148
  408.5 551.2 %copy-start.158 = (f32[256]{0:T(256)}, f32[256]{0:T(256)S(1)}, u32[]{:S(2)}) copy-start(f32[256]{0:T(256)S(1)} %get-tuple-element.450) | copy-start | bytes 3076
  408.5 551.2 %copy-start.109 = (f32[768]{0:T(1024)}, f32[768]{0:T(1024)S(1)}, u32[]{:S(2)}) copy-start(f32[768]{0:T(1024)S(1)} %get-tuple-element.422) | copy-start | bytes 9220
  408.5 1140.8 %collective-permute-start.2 = (bf16[512,768]{1,0:T(8,128)(2,1)}, bf16[512,768]{1,0:T(8,128)(2,1)}, u32[]{:S(2)}, u32[]{:S(2)}) collective-permute-start(bf16[512,768]{1,0:T(8,128)(2,1)} %get-tuple-element.407), channel_id=1, source_target_pairs={{16,0},{17,1},{18,2},{19,3},{20,4},{21,5},{22,6},{23,7},{24,8},{25... | collective-permute-start | bytes 2359304 | tf_op jit(solution)/shard_map/ppermute | solution.py:27
  959.7 589.6 %copy-start.7 = (bf16[1,1024,512]{2,1,0:T(8,128)(2,1)S(1)}, bf16[1,1024,512]{2,1,0:T(8,128)(2,1)}, u32[]{:S(2)}) copy-start(bf16[1,1024,512]{2,1,0:T(8,128)(2,1)} %copy-done.6) | copy-start | bytes 3145732
  959.7 4.4 copy-start.51
  961.4 5.2 copy-start.99
  966.6 6.0 copy-start.170
  1549.8 4.3 copy-start.52
  1551.4 5.2 copy-start.100
  1556.6 6.1 copy-start.171
  1571.7 131.9 %reduce-scatter.23.cloned.1.call-start = ((), (), s32[]{:S(2)}) async-start(), calls=%async_computation.21 | async-start | bytes 811008 | tf_op jit(solution)/shard_map/reduce_scatter | solution.py:108
  1574.2 232.2 %reduce-scatter.13.cloned.1.call-start = ((), (), s32[]{:S(2)}) async-start(), calls=%async_computation.16 | async-start | bytes 1622016 | tf_op jit(solution)/shard_map/reduce_scatter | solution.py:93
  1577.9 333.0 %reduce-scatter.17.cloned.1.call-start = ((), (), s32[]{:S(2)}) async-start(), calls=%async_computation.18 | async-start | bytes 2433024 | tf_op jit(solution)/shard_map/reduce_scatter | solution.py:98
  1582.1 467.4 %reduce-scatter.11.cloned.1.call-start = ((), (), s32[]{:S(2)}) async-start(), calls=%async_computation.15 | async-start | bytes 2162688 | tf_op jit(solution)/shard_map/reduce_scatter | solution.py:90
  1586.2 585.8 %reduce-scatter.15.cloned.1.call-start = ((), (), s32[]{:S(2)}) async-start(), calls=%async_computation.17 | async-start | bytes 7299072 | tf_op jit(solution)/shard_map/reduce_scatter | solution.py:96
  1595.2 718.2 %reduce-scatter.19.cloned.1.call-start = ((), (), s32[]{:S(2)}) async-start(), calls=%async_computation.19 | async-start | bytes 9732096 | tf_op jit(solution)/shard_map/reduce_scatter | solution.py:102
  1608.2 847.1 %reduce-scatter.21.cloned.1.call-start = ((), (), s32[]{:S(2)}) async-start(), calls=%async_computation.20 | async-start | bytes 9732096 | tf_op jit(solution)/shard_map/reduce_scatter | solution.py:104
  1619.6 5.7 copy-start.102
  1619.6 5.7 copy-start.110
  1619.7 5.7 copy-start.83
  1619.7 5.7 copy-start.103
  1619.7 5.7 copy-start.111
  1619.7 5.7 copy-start.104
  1619.7 5.7 copy-start.112
  1619.7 5.7 copy-start.105
  1619.7 5.7 copy-start.113
  1619.7 6.5 copy-start.106
  1619.7 6.5 copy-start.114
  1619.7 6.5 copy-start.107
  1619.7 6.5 copy-start.115
  1619.7 6.5 copy-start.108
  1619.8 6.5 copy-start.116
  1619.8 6.5 copy-start.157
  1619.8 6.5 copy-start.159
  (6 other events, 7.9 us)
Sparse Core Ops, SparseCore 0:
  9.6 36.5 all-gather.6
  49.0 54.0 all-gather.8
  106.0 54.0 all-gather.12
  162.8 60.5 all-gather.10
  226.2 62.3 all-gather.14
  291.3 62.3 all-gather.16
  1571.9 29.7 reduce-scatter.8
  1608.1 95.4 reduce-scatter.22
  1710.2 96.0 reduce-scatter.12
  1812.9 97.9 reduce-scatter.16
  1913.8 135.7 reduce-scatter.10
  2056.6 115.3 reduce-scatter.14
  2178.5 134.7 reduce-scatter.18
  2320.7 134.6 reduce-scatter.20
where the time goes:
time: 2470 us; the launch traced here: 2460 us
  waiting for transfers between devices  2080 us (84%)
  blocking collectives  173 us (7%)
  local copies, waits for them, and re-layouts  78 us (3%)
  other arithmetic  65.6 us (3%)
  matrix products  31 us (1%)
    ppermute x4, waiting for transfers between devices, shifted(): lax.ppermute(value, axis, [(source, source + steps) for source in range(l...  1120 us
    reduce_scatter x1, waiting for transfers between devices, joined_sum(): lax.psum_scatter(grads[14], ('section', 'dp'), scatter_dimension=0, tiled...  142 us
    reduce_scatter x1, waiting for transfers between devices, joined_sum(): lax.psum_scatter(grads[12], ('section', 'dp'), scatter_dimension=0, tiled...  141 us
    reduce_scatter x1, waiting for transfers between devices, joined_sum(): lax.psum_scatter(grads[0], ('section', 'dp'), scatter_dimension=0, tiled=...  139 us
    reduce_scatter x1, waiting for transfers between devices, joined_sum(): lax.psum_scatter(grads[6], ('section', 'dp'), scatter_dimension=0, tiled=...  122 us
    reduce_scatter x1, waiting for transfers between devices, joined_sum(): lax.psum_scatter(grads[8], ('section', 'dp'), scatter_dimension=0, tiled=...  105 us
    reduce_scatter x1, waiting for transfers between devices, joined_sum(): lax.psum_scatter(grads[3], ('section', 'dp'), scatter_dimension=0, tiled=...  103 us
    unnamed x2, blocking collectives  83.6 us
  transfers between devices with their start and end apart: 18, of which 12 were waited for; matrix products, arithmetic and copies ran while one was open for 6% of the time, Pallas kernels for 0%

commit v1 on v0

v1 whole, which is shorter than its diff:
```python
import math

import jax
import jax.numpy as jnp
from jax import lax
from jax.experimental import pallas as pl
from jax.experimental.pallas import tpu as pltpu
from jax.sharding import PartitionSpec as P

D = 768
H = 12
HD = 64
FF = 3072
C = 512
PD = 256
UTTS = 3
FMB = 512
NEG = 100
NMASK = 256
SPARE = 256

BOTH = ("section", "dp")
norm_eps = 1e-05
unit_eps = 1e-06
sharpness = 10.0
masked_score = -1000000000.0
precise = lax.Precision.HIGHEST
low = jnp.bfloat16
full = jnp.float32

VECTORS = (
    ("ln0_gain", C),
    ("ln0_bias", C),
    ("proj0_bias", D),
    ("mask_emb", D),
    ("qv_bias", 2 * D),
    ("out_bias", D),
    ("ln1_gain", D),
    ("ln1_bias", D),
    ("up_bias", FF),
    ("down_bias", D),
    ("ln2_gain", D),
    ("ln2_bias", D),
    ("final_bias", PD),
)
VECTOR_TOTAL = sum(size for _, size in VECTORS)


def plain_dot(left_side, right_side):
    return jnp.dot(left_side, right_side, preferred_element_type=full)


def left_dot(left_side, right_side):
    return lax.dot_general(
        left_side, right_side, (((0,), (0,)), ((), ())), preferred_element_type=full
    )


def right_dot(left_side, right_side):
    return lax.dot_general(
        left_side, right_side, (((1,), (1,)), ((), ())), preferred_element_type=full
    )


def layer_normalize(values, norm_gain, norm_shift):
    center = values - jnp.mean(values, axis=-1, keepdims=True)
    spread = jnp.mean(center * center, axis=-1, keepdims=True)
    return center * lax.rsqrt(spread + norm_eps) * norm_gain + norm_shift


def exact_gelu(values):
    return jax.nn.gelu(values, approximate=False)


def front_norm(conv_out, norm_gain, norm_shift):
    return layer_normalize(exact_gelu(conv_out), norm_gain, norm_shift)


class Links:
    def __init__(self):
        self.per_section = lax.axis_size("dp")
        self.depth = self.per_section // 4
        place = lax.axis_index("dp")
        self.core = place % 2
        self.x = (place // 2) % 2
        self.z = place // 4
        self.y = lax.axis_index("section")

    def move(self, value, where):
        pairs = []
        for y in range(2):
            for z in range(self.depth):
                for x in range(2):
                    for core in range(2):
                        ty, tz, tx, tcore = where(y, z, x, core)
                        pairs.append(
                            (
                                y * self.per_section + z * 4 + x * 2 + core,
                                ty * self.per_section + tz * 4 + tx * 2 + tcore,
                            )
                        )
        return lax.ppermute(value, BOTH, pairs)

    def over_x(self, value):
        return self.move(value, lambda y, z, x, core: (y, z, 1 - x, core))

    def over_y(self, value):
        return self.move(value, lambda y, z, x, core: (1 - y, z, x, core))

    def over_core(self, value):
        return self.move(value, lambda y, z, x, core: (y, z, x, 1 - core))

    def over_z(self, value, steps):
        return self.move(value, lambda y, z, x, core: (y, (z + steps) % self.depth, x, core))


def pick(value, index, axis):
    return lax.squeeze(lax.dynamic_slice_in_dim(value, index, 1, axis), (axis,))


def in_order(index, own, got, axis):
    return jnp.where(
        index == 0, jnp.stack([own, got], axis=axis), jnp.stack([got, own], axis=axis)
    )


def gather_shares(links, share):
    rows, cols = share.shape
    depth = links.depth
    turns = [share] + [links.over_z(share, k) for k in range(1, depth)]
    doubled = jnp.stack([turns[(depth - 1 - i) % depth] for i in range(2 * depth - 1)], 0)
    line = lax.dynamic_slice_in_dim(doubled, depth - 1 - links.z, depth, 0)
    half = cols // 2
    first, second = line[..., :half], line[..., half:]
    first_got, second_got = links.over_x(first), links.over_y(second)
    first = in_order(links.x, first, first_got, 1)
    second = in_order(links.y, second, second_got, 0)
    first_got, second_got = links.over_y(first), links.over_x(second)
    first = in_order(links.y, first, first_got, 0)
    second = in_order(links.x, second, second_got, 2)
    lane = jnp.concatenate([first, second], -1)
    whole = in_order(links.core, lane, links.over_core(lane), 3)
    return whole.reshape(2 * links.per_section, rows, cols)


def sum_shares(links, terms):
    devices, rows, cols = terms.shape
    depth = links.depth
    terms = terms.reshape(2, depth, 2, 2, rows, cols)
    got = links.over_core(pick(terms, 1 - links.core, 3).astype(low))
    lane = pick(terms, links.core, 3) + got.astype(full)
    half = cols // 2
    first, second = lane[..., :half], lane[..., half:]
    first_got = links.over_x(pick(first, 1 - links.x, 2).astype(low))
    second_got = links.over_y(pick(second, 1 - links.y, 0).astype(low))
    first = pick(first, links.x, 2) + first_got.astype(full)
    second = pick(second, links.y, 0) + second_got.astype(full)
    first_got = links.over_y(pick(first, 1 - links.y, 0).astype(low))
    second_got = links.over_x(pick(second, 1 - links.x, 1).astype(low))
    first = pick(first, links.y, 0) + first_got.astype(full)
    second = pick(second, links.x, 1) + second_got.astype(full)
    line = jnp.concatenate([first, second], -1)
    total = pick(line, links.z, 0)
    for k in range(1, depth):
        sent = pick(line, (links.z + k) % depth, 0).astype(low)
        total = total + links.over_z(sent, k).astype(full)
    return total


def vector_maps(devices):
    owner, place = [], []
    start = 0
    for _, size in VECTORS:
        part = size // devices
        for device in range(devices):
            owner += [device] * part
            place += list(range(start, start + part))
        start += part
    return jnp.array(owner, jnp.int32), jnp.array(place, jnp.int32)


def spread_vectors(parts, devices):
    owner, place = vector_maps(devices)
    lanes = (jnp.arange(parts.shape[1], dtype=jnp.int32)[:, None] == place[None, :]).astype(low)
    rows = jnp.arange(devices, dtype=jnp.int32)[:, None] == owner[None, :]
    return jnp.sum(jnp.where(rows, plain_dot(parts, lanes), 0.0), axis=0, keepdims=True)


def split_vectors(vectors, devices, width):
    owner, place = vector_maps(devices)
    lanes = (jnp.arange(width, dtype=jnp.int32)[:, None] == place[None, :]).astype(low)
    rows = jnp.arange(devices, dtype=jnp.int32)[:, None] == owner[None, :]
    return right_dot(jnp.where(rows, vectors.astype(low), 0).astype(low), lanes)


def count_kernel(chosen_ref, count_ref):
    rows = 64
    for block in range(FMB // rows):
        frames = block * rows + lax.broadcasted_iota(jnp.int32, (rows, NMASK), 0)

        def add_one(j, seen):
            return seen + jnp.where(frames == chosen_ref[pl.ds(j, 1), :], 1.0, 0.0)

        seen = lax.fori_loop(0, NEG, add_one, jnp.zeros((rows, NMASK), full), unroll=10)
        count_ref[pl.ds(block * rows, rows), :] = seen.astype(low)


def count_distractors(chosen):
    return pl.pallas_call(
        count_kernel,
        out_shape=jax.ShapeDtypeStruct((FMB, NMASK), low),
        in_specs=[pl.BlockSpec(memory_space=pltpu.VMEM)],
        out_specs=pl.BlockSpec(memory_space=pltpu.VMEM),
        cost_estimate=pl.CostEstimate(flops=2 * FMB * NMASK * NEG, bytes_accessed=400000, transcendentals=0),
    )(chosen.T)


def body(
    features,
    conv_weight,
    ln0_gain,
    ln0_bias,
    proj0_weight,
    proj0_bias,
    mask_emb,
    qkv_weight,
    qv_bias,
    out_weight,
    out_bias,
    ln1_gain,
    ln1_bias,
    up_weight,
    up_bias,
    down_weight,
    down_bias,
    ln2_gain,
    ln2_bias,
    final_weight,
    final_bias,
    codebook,
    lengths,
    mask_pos,
    distractors,
    target_ids,
):
    links = Links()
    section = links.y
    devices = 2 * links.per_section
    rows = C // devices

    own_rows = pick(features, section, 0)
    got_rows = links.over_y(pick(features, 1 - section, 0))
    lens = pick(lengths, section, 0)
    positions = pick(mask_pos, section, 0)
    chosen = pick(distractors, section, 0)
    target_rows = pick(target_ids, section, 0)

    vector_part = jnp.concatenate(
        [
            ln0_gain,
            ln0_bias,
            proj0_bias,
            mask_emb,
            qv_bias,
            out_bias,
            ln1_gain,
            ln1_bias,
            up_bias,
            down_bias,
            ln2_gain,
            ln2_bias,
            final_bias,
        ]
    )
    vector_part = jnp.pad(vector_part, (0, (rows // 2) * SPARE - vector_part.shape[0]))
    misc = jnp.concatenate(
        [
            proj0_weight,
            conv_weight[:rows],
            conv_weight[rows:],
            final_weight[:rows],
            jnp.concatenate([final_weight[rows:], vector_part.reshape(rows // 2, SPARE)], 0),
        ],
        axis=1,
    )
    misc_all = gather_shares(links, misc)
    heads_all = gather_shares(links, jnp.concatenate([qkv_weight, out_weight], axis=1))
    up_all = gather_shares(links, up_weight)
    down_all = gather_shares(links, down_weight)

    proj_full = misc_all[..., :D].reshape(C, D)
    conv_full = jnp.concatenate(
        [misc_all[..., D : D + C], misc_all[..., D + C : D + 2 * C]], axis=1
    ).reshape(2 * C, C)
    last = misc_all[..., D + 2 * C + PD :]
    final_full = jnp.concatenate(
        [misc_all[..., D + 2 * C : D + 2 * C + PD], last[:, : rows // 2]], axis=1
    ).reshape(D, PD)
    vectors = spread_vectors(last[:, rows // 2 :].reshape(devices, -1), devices)
    vec = {}
    start = 0
    for name, size in VECTORS:
        vec[name] = vectors[:, start : start + size]
        start += size
    heads_all = heads_all.reshape(D, 4 * D)
    qkv_full, out_full = heads_all[:, : 3 * D], heads_all[:, 3 * D :]
    up_full = up_all.reshape(D, FF)
    down_full = down_all.reshape(FF, D)

    frame_ids = jnp.arange(FMB, dtype=jnp.int32)
    at_frame = positions[:, None] == frame_ids[None, :]
    is_masked = jnp.any(at_frame, axis=0)
    counts = plain_dot(count_distractors(chosen), at_frame.astype(low))
    own_frame = (frame_ids[:, None] == frame_ids[None, :]) & is_masked[None, :]
    counts = counts + own_frame.astype(full)
    entries = jnp.arange(codebook.shape[1], dtype=jnp.int32)
    targets = jnp.concatenate(
        [
            plain_dot((target_rows[0][:, None] == entries[None, :]).astype(low), codebook[0]),
            plain_dot((target_rows[1][:, None] == entries[None, :]).astype(low), codebook[1]),
        ],
        axis=1,
    )
    targets = targets * lax.rsqrt(jnp.sum(targets * targets, axis=1, keepdims=True) + unit_eps)
    stops = jnp.cumsum(lens)
    segment = jnp.sum(
        (frame_ids[:, None] >= stops[None, : UTTS - 1]).astype(jnp.int32), axis=1
    )
    same_utt = (segment[:, None] == segment[None, :])[None]
    mask_rows = is_masked[:, None]

    own_pairs = own_rows.reshape(FMB, C)
    got_pairs = got_rows.reshape(FMB, C)
    half = C // 2
    taps = conv_full.reshape(2, 2, half, C)
    own_taps = pick(taps, section, 1).reshape(C, C)
    got_taps = pick(taps, 1 - section, 1).reshape(C, C)
    conv_out = plain_dot(own_pairs, own_taps) + plain_dot(got_pairs, got_taps)
    normed, norm_back = jax.vjp(front_norm, conv_out, vec["ln0_gain"], vec["ln0_bias"])
    normed = normed.astype(low)
    encoded = (plain_dot(normed, proj_full) + vec["proj0_bias"]).astype(low)
    inputs = jnp.where(mask_rows, vec["mask_emb"].astype(low), encoded)

    scale = 1.0 / math.sqrt(HD)
    bias_three = jnp.concatenate(
        [vec["qv_bias"][:, :D], jnp.zeros((1, D), full), vec["qv_bias"][:, D:]], axis=1
    )
    qkv_rows = (plain_dot(inputs, qkv_full) + bias_three).astype(low)
    queries = qkv_rows[:, :D].reshape(FMB, H, HD)
    key_rows = qkv_rows[:, D : 2 * D].reshape(FMB, H, HD)
    value_rows = qkv_rows[:, 2 * D :].reshape(FMB, H, HD)
    scores = jnp.einsum("qhd,khd->hqk", queries, key_rows, preferred_element_type=full) * scale
    scores = jnp.where(same_utt, scores, masked_score)
    top_score = jnp.max(scores, axis=-1, keepdims=True)
    exp_scores = jnp.exp(scores - top_score)
    row_total = jnp.sum(exp_scores, axis=-1, keepdims=True)
    attention = exp_scores / row_total
    attention_low = attention.astype(low)
    mixed = (
        jnp.einsum("hqk,khd->qhd", attention_low, value_rows, preferred_element_type=full)
        .reshape(FMB, D)
        .astype(low)
    )
    first, first_back = jax.vjp(
        layer_normalize,
        inputs.astype(full) + plain_dot(mixed, out_full) + vec["out_bias"],
        vec["ln1_gain"],
        vec["ln1_bias"],
    )
    first_low = first.astype(low)
    hidden, gelu_back = jax.vjp(exact_gelu, plain_dot(first_low, up_full) + vec["up_bias"])
    hidden_low = hidden.astype(low)
    second, second_back = jax.vjp(
        layer_normalize,
        first_low.astype(full) + plain_dot(hidden_low, down_full) + vec["down_bias"],
        vec["ln2_gain"],
        vec["ln2_bias"],
    )
    second_low = second.astype(low)
    projected = plain_dot(second_low, final_full) + vec["final_bias"]

    inverse = lax.rsqrt(jnp.sum(projected * projected, axis=1, keepdims=True) + unit_eps)
    unit = projected * inverse
    agreement = sharpness * lax.dot_general(
        targets, unit, (((1,), (1,)), ((), ())), precision=precise, preferred_element_type=full
    )
    drawn = counts > 0
    highest = jnp.max(jnp.where(drawn, agreement, masked_score), axis=0, keepdims=True)
    weights = counts * jnp.exp(jnp.where(drawn, agreement - highest, 0.0))
    weight_total = jnp.sum(weights, axis=0, keepdims=True)
    log_total = highest + jnp.log(jnp.where(is_masked[None, :], weight_total, 1.0))
    own_score = jnp.sum(jnp.where(own_frame, agreement, 0.0), axis=0, keepdims=True)
    loss = jnp.sum(jnp.where(is_masked[None, :], log_total - own_score, 0.0)) / NMASK
    d_agreement = jnp.where(
        is_masked[None, :],
        weights / jnp.where(is_masked[None, :], weight_total, 1.0) - own_frame.astype(full),
        0.0,
    ) * (sharpness / NMASK)
    d_unit = lax.dot_general(
        d_agreement, targets, (((0,), (0,)), ((), ())), precision=precise, preferred_element_type=full
    )
    d_projected = inverse * (d_unit - unit * jnp.sum(d_unit * unit, axis=1, keepdims=True))
    loss_got = links.over_y(loss.reshape(1, 1))
    loss_each = in_order(section, loss.reshape(1, 1), loss_got, 0).reshape(2)

    grad = {}
    d_proj_low = d_projected.astype(low)
    g_final = left_dot(second_low, d_proj_low)
    grad["final_bias"] = jnp.sum(d_proj_low.astype(full), axis=0, keepdims=True)
    d_second, grad["ln2_gain"], grad["ln2_bias"] = second_back(right_dot(d_proj_low, final_full))
    d_ffn_low = d_second.astype(low)
    g_down = left_dot(hidden_low, d_ffn_low)
    down_sum = sum_shares(links, g_down.reshape(devices, FF // devices, D))
    grad["down_bias"] = jnp.sum(d_ffn_low.astype(full), axis=0, keepdims=True)
    (d_hidden,) = gelu_back(right_dot(d_ffn_low, down_full))
    d_pre_low = d_hidden.astype(low)
    g_up = left_dot(first_low, d_pre_low)
    up_sum = sum_shares(links, g_up.reshape(devices, D // devices, FF))
    grad["up_bias"] = jnp.sum(d_pre_low.astype(full), axis=0, keepdims=True)
    d_first, grad["ln1_gain"], grad["ln1_bias"] = first_back(
        right_dot(d_pre_low, up_full) + d_second
    )
    d_attn_low = d_first.astype(low)
    g_out = left_dot(mixed, d_attn_low)
    grad["out_bias"] = jnp.sum(d_attn_low.astype(full), axis=0, keepdims=True)
    d_mixed = right_dot(d_attn_low, out_full).astype(low).reshape(FMB, H, HD)
    d_values = jnp.einsum("hqk,qhd->khd", attention_low, d_mixed, preferred_element_type=full)
    d_attention = jnp.einsum("qhd,khd->hqk", d_mixed, value_rows, preferred_element_type=full)
    d_scores = (
        attention * (d_attention - jnp.sum(attention * d_attention, axis=-1, keepdims=True))
    ).astype(low)
    d_queries = jnp.einsum("hqk,khd->qhd", d_scores, key_rows, preferred_element_type=full) * scale
    d_keys = jnp.einsum("hqk,qhd->khd", d_scores, queries, preferred_element_type=full) * scale
    d_qkv = jnp.concatenate(
        [d_queries.reshape(FMB, D), d_keys.reshape(FMB, D), d_values.reshape(FMB, D)], axis=1
    ).astype(low)
    g_qkv = left_dot(inputs, d_qkv)
    heads_sum = sum_shares(
        links,
        jnp.concatenate([g_qkv, g_out], axis=1).reshape(devices, D // devices, 4 * D),
    )
    qkv_sums = jnp.sum(d_qkv.astype(full), axis=0, keepdims=True)
    grad["qv_bias"] = jnp.concatenate([qkv_sums[:, :D], qkv_sums[:, 2 * D :]], axis=1)
    d_inputs = right_dot(d_qkv, qkv_full) + d_first
    grad["mask_emb"] = jnp.sum(jnp.where(mask_rows, d_inputs, 0.0), axis=0, keepdims=True)
    d_encoded = jnp.where(mask_rows, 0.0, d_inputs).astype(low)
    g_proj = left_dot(normed, d_encoded)
    grad["proj0_bias"] = jnp.sum(d_encoded.astype(full), axis=0, keepdims=True)
    d_conv, grad["ln0_gain"], grad["ln0_bias"] = norm_back(right_dot(d_encoded, proj_full))
    d_conv_low = d_conv.astype(low)
    got_d = links.over_y(right_dot(d_conv_low, got_taps).astype(low).reshape(2 * FMB, half))
    own_d = right_dot(d_conv_low, own_taps).reshape(2 * FMB, half)
    features_grad = in_order(section, own_d, got_d.astype(full), 0)
    own_g = left_dot(own_pairs, d_conv_low).reshape(2, half, C)
    got_g = left_dot(got_pairs, d_conv_low).reshape(2, half, C)
    g_conv = in_order(section, own_g, got_g, 1).reshape(devices, 2 * rows, C)
    g_final = g_final.reshape(devices, D // devices, PD)
    g_vectors = split_vectors(
        jnp.concatenate([grad[name] for name, _ in VECTORS], axis=1),
        devices,
        (rows // 2) * SPARE,
    ).reshape(devices, rows // 2, SPARE)
    misc_sum = sum_shares(
        links,
        jnp.concatenate(
            [
                g_proj.reshape(devices, rows, D),
                g_conv[:, :rows],
                g_conv[:, rows:],
                g_final[:, :rows],
                jnp.concatenate([g_final[:, rows:], g_vectors], axis=1),
            ],
            axis=2,
        ),
    )
    proj_sum = misc_sum[:, :D]
    conv_sum = jnp.concatenate([misc_sum[:, D : D + C], misc_sum[:, D + C : D + 2 * C]], axis=0)
    last = misc_sum[:, D + 2 * C + PD :]
    final_sum = jnp.concatenate(
        [misc_sum[:, D + 2 * C : D + 2 * C + PD], last[: rows // 2]], axis=0
    )
    vector_sum = last[rows // 2 :].reshape(-1)
    share = {}
    start = 0
    for name, size in VECTORS:
        share[name] = vector_sum[start : start + size // devices]
        start += size // devices
    return (
        loss_each,
        features_grad,
        conv_sum,
        share["ln0_gain"],
        share["ln0_bias"],
        proj_sum,
        share["proj0_bias"],
        share["mask_emb"],
        heads_sum[:, : 3 * D],
        share["qv_bias"],
        heads_sum[:, 3 * D :],
        share["out_bias"],
        share["ln1_gain"],
        share["ln1_bias"],
        up_sum,
        share["up_bias"],
        down_sum,
        share["down_bias"],
        share["ln2_gain"],
        share["ln2_bias"],
        final_sum,
        share["final_bias"],
    )


def solution(mesh):
    rows = P(BOTH, None)
    part = P(BOTH)
    weights = (rows, part, part, rows, part, part, rows, part, rows, part, part, part)
    weights += (rows, part, rows, part, part, part, rows, part)
    return jax.shard_map(
        body,
        mesh=mesh,
        in_specs=(P("dp", None, "section"),)
        + weights
        + (P(), P("dp", None), P("dp", None), P("dp", None, None), P("dp", None, None)),
        out_specs=(P("dp"), P("dp", None, "section")) + weights,
        check_vma=False,
    )
```

time: 2470 us -> 535 us (0.22)
  waiting for transfers between devices: 2080 us -> 116 us
  blocking collectives: 173 us -> 0 us
  matrix products: 31 us -> 160 us
  starting transfers between devices: 7.7 us -> 86.5 us
    ppermute x4 -> x67, waiting for transfers between devices: 1120 us -> 116 us  [move(): return lax.ppermute(value, BOTH, pairs)]
    reduce_scatter x8 -> x0, waiting for transfers between devices: 778 us -> none  [the longest x1 142 us: joined_sum(): lax.psum_scatter(grads[14], ('section', 'dp'), scatter_dimension=0, tiled...]
    all_gather x6 -> x0, waiting for transfers between devices: 178 us -> none  [the longest x1 65.2 us: body(): lax.all_gather(down_weight, ('section', 'dp'), axis=0, tiled=True)]
    all_gather x2 -> x0, blocking collectives: 83.8 us -> none  [the longest x1 45.7 us: body(): lax.all_gather(proj0_weight, ('section', 'dp'), axis=0, tiled=True)]
    unnamed x2 -> x0, blocking collectives: 83.6 us -> none
    ppermute x4 -> x67, starting transfers between devices: 6.97 us -> 86.5 us  [move(): return lax.ppermute(value, BOTH, pairs)]
    dot_general x4 -> x19, matrix products: 15.5 us -> 88.2 us  [the longest x12 59.4 us: plain_dot(): return jnp.dot(left_side, right_side, preferred_element_type=full)]
    another operation x41 -> x7, local copies, waits for them, and re-layouts: 51.4 us -> 2.58 us  [the longest x1 2.35 us: in_order(): jnp.stack([own, got], axis=axis)]
  transfers between devices with their start and end apart: 18 -> 67, of which waited for: 12 -> 30; matrix products, arithmetic and copies ran while one was open for 6% -> 34% of each run, Pallas kernels for 0% -> 1%
where the time goes in v1:
time: 535 us; the launch traced here: 527 us
  matrix products  160 us (30%)
  waiting for transfers between devices  116 us (22%)
  starting transfers between devices  86.5 us (16%)
  local copies, waits for them, and re-layouts  83.9 us (16%)
  other arithmetic  70.4 us (13%)
  Pallas kernels  7.11 us (1%)
    ppermute x67, waiting for transfers between devices, move(): return lax.ppermute(value, BOTH, pairs)  116 us
    ppermute x67, starting transfers between devices, move(): return lax.ppermute(value, BOTH, pairs)  86.5 us
    dot_general x12, matrix products, plain_dot(): return jnp.dot(left_side, right_side, preferred_element_type=full)  59.4 us
    dot_general x9, matrix products, right_dot(): lax.dot_general(left_side, right_side, (((1,), (1,)), ((), ())), preferre...  41.4 us
    unnamed x220, local copies, waits for them, and re-layouts  24.7 us
    select_n x28, other arithmetic, in_order(): jnp.where(index == 0, jnp.stack([own, got], axis=axis), jnp.stack([got, o...  22.5 us
    dot_general x8, matrix products, left_dot(): lax.dot_general(left_side, right_side, (((0,), (0,)), ((), ())), preferre...  19.6 us
    convert_element_type x4, local copies, waits for them, and re-layouts, sum_shares(): got = links.over_core(pick(terms, 1 - links.core, 3).astype(low))  13.6 us
  transfers between devices with their start and end apart: 67, of which 30 were waited for; matrix products, arithmetic and copies ran while one was open for 34% of the time, Pallas kernels for 1%

profile of v1, /device:TPU:0, one launch (start us, length us, event | category | flops | bytes accessed | tf_op | source)
XLA Modules:
  0.0 527.1 jit_solution(5565986421880345387)
XLA Ops:
  0.7 8.9 %concatenate.213 = bf16[376]{0:T(512)(128)(2,1)S(1)} concatenate(bf16[16]{0:T(256)(128)(2,1)} %param.32, bf16[16]{0:T(256)(128)(2,1)} %param.33, bf16[24]{0:T(256)(128)(2,1)} %param.35, bf16[24]{0:T(256)(128)(2,1)} %param.36, bf16[48]{0:T(256)(128)(2,1)} %param.38, bf16[24]{0:T(256)(128)(2,1)} %param.40, bf16[24]{0:T(256)(128)(2,1)} %param.41, bf16[24]{0:T(256)(128)(2,1)} %param.42, ...), dimensions={0} | concatenate | bytes 1504 | tf_op jit(solution)/shard_map/concatenate | solution.py:258
  16.2 3.0 collective-permute-start.2
  19.2 2.6 collective-permute-start.1
  28.4 7.1 %shard_map.453 = bf16[512,256]{1,0:T(8,128)(2,1)} custom-call(s32[100,256]{1,0:T(8,128)} %bitcast.505), custom_call_target="tpu_custom_call" | custom-call | flops 26214400 | bytes 400000 | tf_op jit(solution)/shard_map/pallas_call | solution.py:209
  39.8 2.4 convert_add_fusion
  44.3 2.9 collective-permute-start.9
  51.3 4.5 collective-permute-done.17
  55.8 4.2 collective-permute-start.25
  60.0 4.6 collective-permute-done.25
  66.2 4.5 collective-permute-done.26
  70.8 4.8 collective-permute-start.27
  75.6 4.0 collective-permute-done.27
  79.6 2.5 collective-permute-start.19
  83.7 3.0 collective-permute-done.19
  92.4 7.2 %collective-permute-done.5 = bf16[4,16,1152]{2,1,0:T(8,128)(2,1)S(1)} collective-permute-done((bf16[4,16,1152]{2,1,0:T(8,128)(2,1)S(1)}, bf16[4,16,1152]{2,1,0:T(8,128)(2,1)S(1)}, u32[]{:S(2)}, u32[]{:S(2)}) %collective-permute-start.5) | collective-permute-done | bytes 147488 | tf_op jit(solution)/shard_map/ppermute | solution.py:102
  103.6 6.7 %collective-permute-done.22 = bf16[4,24,1536]{2,1,0:T(8,128)(2,1)S(1)} collective-permute-done((bf16[4,24,1536]{2,1,0:T(8,128)(2,1)S(1)}, bf16[4,24,1536]{2,1,0:T(8,128)(2,1)S(1)}, u32[]{:S(2)}, u32[]{:S(2)}) %collective-permute-start.22) | collective-permute-done | bytes 294944 | tf_op jit(solution)/shard_map/ppermute | solution.py:102
  116.9 5.0 collective-permute-done.14
  140.7 4.0 collective-permute-done.31
  148.2 3.1 fusion.178
  157.5 3.7 collective-permute-done.15
  164.3 19.9 %fusion.40 = f32[12032]{0:T(1024)S(1)} fusion(bf16[32,2048]{1,0:T(8,128)(2,1)S(1)} %bitcast.510, s32[12032]{0:T(1024)S(1)} %copy-done.60, s32[12032]{0:T(1024)S(1)} %copy-done.51), kind=kOutput, calls=%fused_computation.126 | convolution fusion | flops 1602842880 | bytes 275456 | tf_op jit(solution)/shard_map/dot_general | solution.py:50
  186.7 7.7 %fusion.190 = (f32[512]{0:T(512)S(1)}, f32[512,512]{1,0:T(8,128)S(1)}, f32[512,512]{1,0:T(8,128)}, f32[512,512]{1,0:T(8,128)}) fusion(f32[512,512]{1,0:T(8,128)S(1)} %fusion.210, bf16[512,512]{1,0:T(8,128)(2,1)S(1)} %copy-done.29, bf16[512,512]{1,0:T(8,128)(2,1)S(1)} %bitcast.465), kind=kOutput, calls=%fused_computation.472 | convolution fusion | flops 285736448 | bytes 5244928 | tf_op jit(solution)/shard_map/dot_general | solution.py:50
  197.0 2.5 copy.142
  207.2 2.3 copy.138
  209.5 10.4 %fusion.206 = (f32[12,512]{1,0:T(8,128)S(1)}, f32[12,512,512]{1,2,0:T(8,128)}) fusion(pred[512,512]{0,1:T(8,128)(4,1)} %broadcast_compare_fusion, bf16[512,12,64]{0,2,1:T(8,128)(2,1)} %bitcast.446, bf16[512,12,64]{0,2,1:T(8,128)(2,1)S(1)} %bitcast.408), kind=kOutput, calls=%fused_computation.487 | convolution fusion | flops 415236608 | bytes 14442496 | tf_op jit(solution)/shard_map/sub | solution.py:355
  219.9 6.1 %fusion.31 = bf16[12,64,512]{2,1,0:T(8,128)(2,1)S(1)} fusion(bf16[512,12,64]{0,2,1:T(8,128)(2,1)} %bitcast.490, f32[12,512,512]{1,2,0:T(8,128)} %get-tuple-element.142, f32[12,512]{1,0:T(8,128)S(1)} %get-tuple-element.141), kind=kOutput, calls=%fused_computation.117 | convolution fusion | flops 409337856 | bytes 14180352 | tf_op jit(solution)/shard_map/hqk,khd->qhd/dot_general | solution.py:360
  228.6 3.1 maximum_select_fusion.2
  232.0 18.3 %multiply_convert_fusion.1 = (bf16[512,3072]{1,0:T(8,128)(2,1)S(1)}, f32[512,3072]{1,0:T(8,128)}, f32[512,3072]{1,0:T(8,128)}) fusion(f32[3072]{0:T(1024)S(1)} %bitcast.521, bf16[768,3072]{1,0:T(8,128)(2,1)S(1)} %bitcast.430, f32[512,768]{1,0:T(8,128)S(1)} %get-tuple-element.144, f32[768]{0:T(1024)S(1)} %get-tuple-element.120, ...), kind=kOutput, calls=%fused_computation.16 | convolution fusion | flops 2521694208 | bytes 22042624 | tf_op jit(solution)/shard_map/dot_general | solution.py:50
  250.3 2.7 fusion.208
  262.4 8.0 %fusion.184 = (bf16[3072]{0:T(1024)(128)(2,1)S(1)}, bf16[512,3072]{1,0:T(8,128)(2,1)S(1)}) fusion(f32[512,3072]{1,0:T(8,128)} %get-tuple-element.58, f32[512,3072]{1,0:T(8,128)} %get-tuple-element.145, f32[3072]{0:T(1024)S(1)} %bitcast.522, bf16[512,768]{1,0:T(8,128)(2,1)S(1)} %get-tuple-element.46, bf16[3072,768]{1,0:T(8,128)(2,1)S(1)} %bitcast.433), kind=kOutput, calls=%fused_computation.467 | convolution fusion | flops 2441081856 | bytes 21252096 | tf_op jit(solution)/shard_map/dot_general | solution.py:60
  270.3 3.1 multiply_reduce_fusion.2
  274.3 3.3 convolution_convert_fusion
  279.5 5.5 %fusion.209 = f32[768,3072]{1,0:T(8,128)} fusion(bf16[512,3072]{1,0:T(8,128)(2,1)S(1)} %copy-done.65, f32[512,768]{1,0:T(8,128)S(1)} %get-tuple-element.144, f32[768]{0:T(1024)S(1)} %get-tuple-element.120, f32[768]{0:T(1024)S(1)} %get-tuple-element.119, f32[512]{0:T(512)S(1)} %fusion.164, f32[512]{0:T(512)S(1)} %broadcast_multiply_fusion.1), kind=kOutput, calls=%fused_computation.490 | convolution fusion | flops 2417885184 | bytes 14166016 | tf_op jit(solution)/shard_map/dot_general | solution.py:54
  285.0 5.0 fusion.214
  290.0 2.3 copy.148
  292.3 7.9 %fusion.34 = bf16[12,64,512]{2,1,0:T(8,128)(2,1)} fusion(bf16[512,12,64]{0,2,1:T(8,128)(2,1)} %bitcast.492, f32[12,512,512]{1,2,0:T(8,128)} %get-tuple-element.142, f32[12,512]{1,0:T(8,128)S(1)} %get-tuple-element.141), kind=kOutput, calls=%fused_computation.118 | convolution fusion | flops 409337856 | bytes 14180352 | tf_op jit(solution)/shard_map/hqk,qhd->khd/dot_general | solution.py:427
  300.2 9.0 %multiply_reduce_fusion = (f32[12,512]{1,0:T(8,128)S(1)}, f32[12,512,512]{1,2,0:T(8,128)}) fusion(f32[12,512,512]{1,2,0:T(8,128)} %get-tuple-element.142, f32[12,512]{1,0:T(8,128)S(1)} %get-tuple-element.141, bf16[512,12,64]{0,2,1:T(8,128)(2,1)S(1)} %bitcast.493, bf16[512,12,64]{0,2,1:T(8,128)(2,1)S(1)} %bitcast.491), kind=kOutput, calls=%fused_computation.8 | convolution fusion | flops 412084224 | bytes 26787840 | tf_op jit(solution)/shard_map/qhd,khd->hqk/dot_general | solution.py:428
  309.2 7.0 %multiply_convert_fusion = bf16[12,512,512]{1,2,0:T(8,128)(2,1)S(1)} fusion(f32[12,512,512]{1,2,0:T(8,128)} %get-tuple-element.157, f32[12,512]{1,0:T(8,128)S(1)} %get-tuple-element.156, f32[12,512,512]{1,2,0:T(8,128)S(1)} %bitcast.402, f32[12,512]{1,0:T(8,128)S(1)} %get-tuple-element.141), kind=kLoop, calls=%fused_computation.7 | loop fusion | flops 12582912 | bytes 31506432 | tf_op jit(solution)/shard_map/convert_element_type | solution.py:431
  321.1 3.4 fusion.186
  333.2 4.9 fusion.175
  338.8 2.9 collective-permute-start.33
  341.7 4.3 fusion.25
  352.8 19.2 %fusion.1 = f32[32,2048]{1,0:T(8,128)S(1)} fusion(s32[12032]{0:T(1024)S(1)} %copy-done.61, bf16[32,12032]{1,0:T(8,128)(2,1)S(1)} %fusion.271), kind=kOutput, calls=%fused_computation.2 | convolution fusion | flops 1601699840 | bytes 1080320 | tf_op jit(solution)/shard_map/dot_general | solution.py:60
  377.9 4.1 fusion.26
  383.2 2.4 stack_reshape.2
  386.1 8.1 %pad_maximum_fusion = f32[768,3072]{1,0:T(8,128)} fusion(f32[768,768]{1,0:T(8,128)S(1)} %fusion.213, f32[768,2304]{1,0:T(8,128)} %fusion.175), kind=kLoop, calls=%fused_computation.13 | loop fusion | flops 2359296 | bytes 18874368 | tf_op jit(solution)/shard_map/concatenate | solution.py:440
  394.2 4.1 fusion.24
  399.6 2.4 fusion.27
  404.2 7.0 %collective-permute-done.36 = bf16[2,4,16,1152]{3,2,1,0:T(8,128)(2,1)S(1)} collective-permute-done((bf16[2,4,16,1152]{3,2,1,0:T(8,128)(2,1)S(1)}, bf16[2,4,16,1152]{3,2,1,0:T(8,128)(2,1)S(1)}, u32[]{:S(2)}, u32[]{:S(2)}) %collective-permute-start.36) | collective-permute-done | bytes 294944 | tf_op jit(solution)/shard_map/ppermute | solution.py:102
  413.3 3.2 collective-permute-done.37
  418.8 3.3 collective-permute-start.42
  430.3 2.8 bitcast_add_fusion.1
  437.0 2.4 bitcast_add_fusion
  442.7 2.6 bitcast_add_fusion.2
  446.3 4.6 collective-permute-done.52
  455.5 7.9 %collective-permute-done.60 = bf16[2,4,96,384]{3,2,1,0:T(8,128)(2,1)S(1)} collective-permute-done((bf16[2,4,96,384]{3,2,1,0:T(8,128)(2,1)S(1)}, bf16[2,4,96,384]{3,2,1,0:T(8,128)(2,1)S(1)}, u32[]{:S(2)}, u32[]{:S(2)}) %collective-permute-start.60) | collective-permute-done | bytes 589856 | tf_op jit(solution)/shard_map/ppermute | solution.py:102
  466.3 9.8 %collective-permute-done.44 = bf16[2,4,24,1536]{3,2,1,0:T(8,128)(2,1)S(1)} collective-permute-done((bf16[2,4,24,1536]{3,2,1,0:T(8,128)(2,1)S(1)}, bf16[2,4,24,1536]{3,2,1,0:T(8,128)(2,1)S(1)}, u32[]{:S(2)}, u32[]{:S(2)}) %collective-permute-start.44) | collective-permute-done | bytes 589856 | tf_op jit(solution)/shard_map/ppermute | solution.py:102
  478.9 4.9 collective-permute-done.53
  487.3 2.8 collective-permute-done.61
  491.3 2.3 collective-permute-start.58
  499.4 11.9 %collective-permute-done.57 = bf16[24,3072]{1,0:T(8,128)(2,1)S(1)} collective-permute-done((bf16[24,3072]{1,0:T(8,128)(2,1)S(1)}, bf16[24,3072]{1,0:T(8,128)(2,1)S(1)}, u32[]{:S(2)}, u32[]{:S(2)}) %collective-permute-start.57) | collective-permute-done | bytes 147488 | tf_op jit(solution)/shard_map/ppermute | solution.py:102
  512.2 4.8 collective-permute-start.66
  517.0 3.4 collective-permute-done.49
  523.2 2.7 collective-permute-done.66
  (526 shorter events, 178.3 us)
Async XLA Ops:
  16.2 33.2 %collective-permute-start.2 = (bf16[16,2304]{1,0:T(8,128)(2,1)}, bf16[16,2304]{1,0:T(8,128)(2,1)S(1)}, u32[]{:S(2)}, u32[]{:S(2)}) collective-permute-start(bf16[16,2304]{1,0:T(8,128)(2,1)} %constant_dynamic-update-slice_fusion), channel_id=1, source_target_pairs={{0,4},{1,5},{2,6},{3,7},{4,8},{5,9},{6,10},{7,11},{8,12},{9,13},{1... | collective-permute-start | bytes 221192 | tf_op jit(solution)/shard_map/ppermute | solution.py:102
  19.2 28.0 %collective-permute-start.1 = (bf16[16,2304]{1,0:T(8,128)(2,1)}, bf16[16,2304]{1,0:T(8,128)(2,1)S(1)}, u32[]{:S(2)}, u32[]{:S(2)}) collective-permute-start(bf16[16,2304]{1,0:T(8,128)(2,1)} %constant_dynamic-update-slice_fusion), channel_id=1, source_target_pairs={{0,8},{1,9},{2,10},{3,11},{4,12},{5,13},{6,14},{7,15},{8,0},{9,1},... | collective-permute-start | bytes 221192 | tf_op jit(solution)/shard_map/ppermute | solution.py:102
  21.8 22.6 %collective-permute-start = (bf16[16,2304]{1,0:T(8,128)(2,1)}, bf16[16,2304]{1,0:T(8,128)(2,1)S(1)}, u32[]{:S(2)}, u32[]{:S(2)}) collective-permute-start(bf16[16,2304]{1,0:T(8,128)(2,1)} %constant_dynamic-update-slice_fusion), channel_id=1, source_target_pairs={{0,12},{1,13},{2,14},{3,15},{4,0},{5,1},{6,2},{7,3},{8,4},{9,5},{1... | collective-permute-start | bytes 221192 | tf_op jit(solution)/shard_map/ppermute | solution.py:102
  24.8 66.7 %collective-permute-start.11 = (bf16[24,3072]{1,0:T(8,128)(2,1)S(1)}, bf16[24,3072]{1,0:T(8,128)(2,1)S(1)}, u32[]{:S(2)}, u32[]{:S(2)}) collective-permute-start(bf16[24,3072]{1,0:T(8,128)(2,1)S(1)} %constant_dynamic-update-slice_fusion.12), channel_id=1, source_target_pairs={{0,4},{1,5},{2,6},{3,7},{4,8},{5,9},{6,10},{7,11},{8,12},{9,13},{1... | collective-permute-start | bytes 442376 | tf_op jit(solution)/shard_map/ppermute | solution.py:102
  25.5 65.4 %collective-permute-start.10 = (bf16[24,3072]{1,0:T(8,128)(2,1)S(1)}, bf16[24,3072]{1,0:T(8,128)(2,1)S(1)}, u32[]{:S(2)}, u32[]{:S(2)}) collective-permute-start(bf16[24,3072]{1,0:T(8,128)(2,1)S(1)} %constant_dynamic-update-slice_fusion.12), channel_id=1, source_target_pairs={{0,8},{1,9},{2,10},{3,11},{4,12},{5,13},{6,14},{7,15},{8,0},{9,1},... | collective-permute-start | bytes 442376 | tf_op jit(solution)/shard_map/ppermute | solution.py:102
  44.3 44.8 %collective-permute-start.9 = (bf16[24,3072]{1,0:T(8,128)(2,1)S(1)}, bf16[24,3072]{1,0:T(8,128)(2,1)S(1)}, u32[]{:S(2)}, u32[]{:S(2)}) collective-permute-start(bf16[24,3072]{1,0:T(8,128)(2,1)S(1)} %constant_dynamic-update-slice_fusion.12), channel_id=1, source_target_pairs={{0,12},{1,13},{2,14},{3,15},{4,0},{5,1},{6,2},{7,3},{8,4},{9,5},{1... | collective-permute-start | bytes 442376 | tf_op jit(solution)/shard_map/ppermute | solution.py:102
  47.2 34.8 %collective-permute-start.18 = (bf16[24,3072]{1,0:T(8,128)(2,1)}, bf16[24,3072]{1,0:T(8,128)(2,1)S(1)}, u32[]{:S(2)}, u32[]{:S(2)}) collective-permute-start(bf16[24,3072]{1,0:T(8,128)(2,1)} %param.43), channel_id=1, source_target_pairs={{0,8},{1,9},{2,10},{3,11},{4,12},{5,13},{6,14},{7,15},{8,0},{9,1},... | collective-permute-start | bytes 442376 | tf_op jit(solution)/shard_map/ppermute | solution.py:102
  49.3 6.5 %collective-permute-start.17 = (bf16[24,3072]{1,0:T(8,128)(2,1)}, bf16[24,3072]{1,0:T(8,128)(2,1)S(1)}, u32[]{:S(2)}, u32[]{:S(2)}) collective-permute-start(bf16[24,3072]{1,0:T(8,128)(2,1)} %param.43), channel_id=1, source_target_pairs={{0,12},{1,13},{2,14},{3,15},{4,0},{5,1},{6,2},{7,3},{8,4},{9,5},{1... | collective-permute-start | bytes 442376 | tf_op jit(solution)/shard_map/ppermute | solution.py:102
  55.8 8.8 %collective-permute-start.25 = (bf16[96,768]{1,0:T(8,128)(2,1)S(1)}, bf16[96,768]{1,0:T(8,128)(2,1)S(1)}, u32[]{:S(2)}, u32[]{:S(2)}) collective-permute-start(bf16[96,768]{1,0:T(8,128)(2,1)S(1)} %copy-done.46), channel_id=1, source_target_pairs={{0,12},{1,13},{2,14},{3,15},{4,0},{5,1},{6,2},{7,3},{8,4},{9,5},{1... | collective-permute-start | bytes 442376 | tf_op jit(solution)/shard_map/ppermute | solution.py:102
  70.8 8.8 %collective-permute-start.27 = (bf16[96,768]{1,0:T(8,128)(2,1)S(1)}, bf16[96,768]{1,0:T(8,128)(2,1)S(1)}, u32[]{:S(2)}, u32[]{:S(2)}) collective-permute-start(bf16[96,768]{1,0:T(8,128)(2,1)S(1)} %copy-done.46), channel_id=1, source_target_pairs={{0,4},{1,5},{2,6},{3,7},{4,8},{5,9},{6,10},{7,11},{8,12},{9,13},{1... | collective-permute-start | bytes 442376 | tf_op jit(solution)/shard_map/ppermute | solution.py:102
  79.6 7.2 %collective-permute-start.19 = (bf16[24,3072]{1,0:T(8,128)(2,1)}, bf16[24,3072]{1,0:T(8,128)(2,1)S(1)}, u32[]{:S(2)}, u32[]{:S(2)}) collective-permute-start(bf16[24,3072]{1,0:T(8,128)(2,1)} %param.43), channel_id=1, source_target_pairs={{0,4},{1,5},{2,6},{3,7},{4,8},{5,9},{6,10},{7,11},{8,12},{9,13},{1... | collective-permute-start | bytes 442376 | tf_op jit(solution)/shard_map/ppermute | solution.py:102
  82.1 55.2 %collective-permute-start.8 = (bf16[1024,256]{1,0:T(8,128)(2,1)}, bf16[1024,256]{1,0:T(8,128)(2,1)S(1)}, u32[]{:S(2)}, u32[]{:S(2)}) collective-permute-start(bf16[1024,256]{1,0:T(8,128)(2,1)} %get-tuple-element.98), channel_id=1, source_target_pairs={{0,16},{1,17},{2,18},{3,19},{4,20},{5,21},{6,22},{7,23},{8,24},{9,... | collective-permute-start | bytes 1572872 | tf_op jit(solution)/shard_map/ppermute | solution.py:102
  86.7 15.2 %collective-permute-start.3 = (bf16[4,16,1152]{2,1,0:T(8,128)(2,1)S(1)}, bf16[4,16,1152]{2,1,0:T(8,128)(2,1)S(1)}, u32[]{:S(2)}, u32[]{:S(2)}) collective-permute-start(bf16[4,16,1152]{2,1,0:T(8,128)(2,1)S(1)} %get-tuple-element.109), channel_id=1, source_target_pairs={{0,2},{1,3},{2,0},{3,1},{4,6},{5,7},{6,4},{7,5},{8,10},{9,11},{10,... | collective-permute-start | bytes 442376 | tf_op jit(solution)/shard_map/ppermute | solution.py:102
  89.2 10.4 %collective-permute-start.5 = (bf16[4,16,1152]{2,1,0:T(8,128)(2,1)S(1)}, bf16[4,16,1152]{2,1,0:T(8,128)(2,1)S(1)}, u32[]{:S(2)}, u32[]{:S(2)}) collective-permute-start(bf16[4,16,1152]{2,1,0:T(8,128)(2,1)S(1)} %get-tuple-element.110), channel_id=1, source_target_pairs={{0,16},{1,17},{2,18},{3,19},{4,20},{5,21},{6,22},{7,23},{8,24},{9,... | collective-permute-start | bytes 442376 | tf_op jit(solution)/shard_map/ppermute | solution.py:102
  90.9 24.6 %collective-permute-start.28 = (bf16[4,96,384]{2,1,0:T(8,128)(2,1)S(1)}, bf16[4,96,384]{2,1,0:T(8,128)(2,1)S(1)}, u32[]{:S(2)}, u32[]{:S(2)}) collective-permute-start(bf16[4,96,384]{2,1,0:T(8,128)(2,1)S(1)} %get-tuple-element.100), channel_id=1, source_target_pairs={{0,2},{1,3},{2,0},{3,1},{4,6},{5,7},{6,4},{7,5},{8,10},{9,11},{10,... | collective-permute-start | bytes 884744 | tf_op jit(solution)/shard_map/ppermute | solution.py:102
  91.5 33.3 %collective-permute-start.30 = (bf16[4,96,384]{2,1,0:T(8,128)(2,1)S(1)}, bf16[4,96,384]{2,1,0:T(8,128)(2,1)S(1)}, u32[]{:S(2)}, u32[]{:S(2)}) collective-permute-start(bf16[4,96,384]{2,1,0:T(8,128)(2,1)S(1)} %get-tuple-element.101), channel_id=1, source_target_pairs={{0,16},{1,17},{2,18},{3,19},{4,20},{5,21},{6,22},{7,23},{8,24},{9,... | collective-permute-start | bytes 884744 | tf_op jit(solution)/shard_map/ppermute | solution.py:102
  99.6 12.5 %collective-permute-start.20 = (bf16[4,24,1536]{2,1,0:T(8,128)(2,1)S(1)}, bf16[4,24,1536]{2,1,0:T(8,128)(2,1)S(1)}, u32[]{:S(2)}, u32[]{:S(2)}) collective-permute-start(bf16[4,24,1536]{2,1,0:T(8,128)(2,1)S(1)} %get-tuple-element.102), channel_id=1, source_target_pairs={{0,2},{1,3},{2,0},{3,1},{4,6},{5,7},{6,4},{7,5},{8,10},{9,11},{10,... | collective-permute-start | bytes 884744 | tf_op jit(solution)/shard_map/ppermute | solution.py:102
  101.9 8.4 %collective-permute-start.22 = (bf16[4,24,1536]{2,1,0:T(8,128)(2,1)S(1)}, bf16[4,24,1536]{2,1,0:T(8,128)(2,1)S(1)}, u32[]{:S(2)}, u32[]{:S(2)}) collective-permute-start(bf16[4,24,1536]{2,1,0:T(8,128)(2,1)S(1)} %get-tuple-element.103), channel_id=1, source_target_pairs={{0,16},{1,17},{2,18},{3,19},{4,20},{5,21},{6,22},{7,23},{8,24},{9,... | collective-permute-start | bytes 884744 | tf_op jit(solution)/shard_map/ppermute | solution.py:102
  110.3 17.9 %collective-permute-start.12 = (bf16[4,24,1536]{2,1,0:T(8,128)(2,1)S(1)}, bf16[4,24,1536]{2,1,0:T(8,128)(2,1)S(1)}, u32[]{:S(2)}, u32[]{:S(2)}) collective-permute-start(bf16[4,24,1536]{2,1,0:T(8,128)(2,1)S(1)} %get-tuple-element.104), channel_id=1, source_target_pairs={{0,2},{1,3},{2,0},{3,1},{4,6},{5,7},{6,4},{7,5},{8,10},{9,11},{10,... | collective-permute-start | bytes 884744 | tf_op jit(solution)/shard_map/ppermute | solution.py:102
  112.1 9.9 %collective-permute-start.14 = (bf16[4,24,1536]{2,1,0:T(8,128)(2,1)S(1)}, bf16[4,24,1536]{2,1,0:T(8,128)(2,1)S(1)}, u32[]{:S(2)}, u32[]{:S(2)}) collective-permute-start(bf16[4,24,1536]{2,1,0:T(8,128)(2,1)S(1)} %get-tuple-element.105), channel_id=1, source_target_pairs={{0,16},{1,17},{2,18},{3,19},{4,20},{5,21},{6,22},{7,23},{8,24},{9,... | collective-permute-start | bytes 884744 | tf_op jit(solution)/shard_map/ppermute | solution.py:102
  115.5 18.0 %collective-permute-start.4 = (bf16[4,2,16,1152]{3,2,0,1:T(8,128)(2,1)S(1)}, bf16[4,2,16,1152]{3,2,0,1:T(8,128)(2,1)S(1)}, u32[]{:S(2)}, u32[]{:S(2)}) collective-permute-start(bf16[4,2,16,1152]{3,2,0,1:T(8,128)(2,1)S(1)} %maximum_select_fusion.25), channel_id=1, source_target_pairs={{0,16},{1,17},{2,18},{3,19},{4,20},{5,21},{6,22},{7,23},{8,24},{9,... | collective-permute-start | bytes 884744 | tf_op jit(solution)/shard_map/ppermute | solution.py:102
  122.0 9.9 %collective-permute-start.6 = (bf16[2,4,16,1152]{3,2,1,0:T(8,128)(2,1)S(1)}, bf16[2,4,16,1152]{3,2,1,0:T(8,128)(2,1)S(1)}, u32[]{:S(2)}, u32[]{:S(2)}) collective-permute-start(bf16[2,4,16,1152]{3,2,1,0:T(8,128)(2,1)S(1)} %maximum_select_fusion.26), channel_id=1, source_target_pairs={{0,2},{1,3},{2,0},{3,1},{4,6},{5,7},{6,4},{7,5},{8,10},{9,11},{10,... | collective-permute-start | bytes 884744 | tf_op jit(solution)/shard_map/ppermute | solution.py:102
  124.9 23.2 %collective-permute-start.29 = (bf16[4,2,96,384]{3,2,0,1:T(8,128)(2,1)}, bf16[4,2,96,384]{3,2,0,1:T(8,128)(2,1)}, u32[]{:S(2)}, u32[]{:S(2)}) collective-permute-start(bf16[4,2,96,384]{3,2,0,1:T(8,128)(2,1)} %maximum_select_fusion.22), channel_id=1, source_target_pairs={{0,16},{1,17},{2,18},{3,19},{4,20},{5,21},{6,22},{7,23},{8,24},{9,... | collective-permute-start | bytes 1769480 | tf_op jit(solution)/shard_map/ppermute | solution.py:102
  128.2 16.6 %collective-permute-start.31 = (bf16[2,4,96,384]{3,2,1,0:T(8,128)(2,1)}, bf16[2,4,96,384]{3,2,1,0:T(8,128)(2,1)}, u32[]{:S(2)}, u32[]{:S(2)}) collective-permute-start(bf16[2,4,96,384]{3,2,1,0:T(8,128)(2,1)} %maximum_select_fusion.23), channel_id=1, source_target_pairs={{0,2},{1,3},{2,0},{3,1},{4,6},{5,7},{6,4},{7,5},{8,10},{9,11},{10,... | collective-permute-start | bytes 1769480 | tf_op jit(solution)/shard_map/ppermute | solution.py:102
  131.9 21.5 %collective-permute-start.21 = (bf16[4,2,24,1536]{3,2,0,1:T(8,128)(2,1)}, bf16[4,2,24,1536]{3,2,0,1:T(8,128)(2,1)}, u32[]{:S(2)}, u32[]{:S(2)}) collective-permute-start(bf16[4,2,24,1536]{3,2,0,1:T(8,128)(2,1)} %maximum_select_fusion.18), channel_id=1, source_target_pairs={{0,16},{1,17},{2,18},{3,19},{4,20},{5,21},{6,22},{7,23},{8,24},{9,... | collective-permute-start | bytes 1769480 | tf_op jit(solution)/shard_map/ppermute | solution.py:102
  133.5 21.5 %collective-permute-start.23 = (bf16[2,4,24,1536]{3,2,1,0:T(8,128)(2,1)}, bf16[2,4,24,1536]{3,2,1,0:T(8,128)(2,1)}, u32[]{:S(2)}, u32[]{:S(2)}) collective-permute-start(bf16[2,4,24,1536]{3,2,1,0:T(8,128)(2,1)} %maximum_select_fusion.20), channel_id=1, source_target_pairs={{0,2},{1,3},{2,0},{3,1},{4,6},{5,7},{6,4},{7,5},{8,10},{9,11},{10,... | collective-permute-start | bytes 1769480 | tf_op jit(solution)/shard_map/ppermute | solution.py:102
  138.0 23.4 %collective-permute-start.13 = (bf16[4,2,24,1536]{3,2,0,1:T(8,128)(2,1)}, bf16[4,2,24,1536]{3,2,0,1:T(8,128)(2,1)}, u32[]{:S(2)}, u32[]{:S(2)}) collective-permute-start(bf16[4,2,24,1536]{3,2,0,1:T(8,128)(2,1)} %maximum_select_fusion.15), channel_id=1, source_target_pairs={{0,16},{1,17},{2,18},{3,19},{4,20},{5,21},{6,22},{7,23},{8,24},{9,... | collective-permute-start | bytes 1769480 | tf_op jit(solution)/shard_map/ppermute | solution.py:102
  144.8 16.5 %collective-permute-start.15 = (bf16[2,4,24,1536]{3,2,1,0:T(8,128)(2,1)}, bf16[2,4,24,1536]{3,2,1,0:T(8,128)(2,1)S(1)}, u32[]{:S(2)}, u32[]{:S(2)}) collective-permute-start(bf16[2,4,24,1536]{3,2,1,0:T(8,128)(2,1)} %maximum_select_fusion.16), channel_id=1, source_target_pairs={{0,2},{1,3},{2,0},{3,1},{4,6},{5,7},{6,4},{7,5},{8,10},{9,11},{10,... | collective-permute-start | bytes 1769480 | tf_op jit(solution)/shard_map/ppermute | solution.py:102
  148.1 15.2 %collective-permute-start.7 = (bf16[2,4,2,16,2304]{4,3,2,1,0:T(8,128)(2,1)}, bf16[2,4,2,16,2304]{4,3,2,1,0:T(8,128)(2,1)S(1)}, u32[]{:S(2)}, u32[]{:S(2)}) collective-permute-start(bf16[2,4,2,16,2304]{4,3,2,1,0:T(8,128)(2,1)} %get-tuple-element.95), channel_id=1, source_target_pairs={{0,1},{1,0},{2,3},{3,2},{4,5},{5,4},{6,7},{7,6},{8,9},{9,8},{10,11... | collective-permute-start | bytes 3538952 | tf_op jit(solution)/shard_map/ppermute | solution.py:102
  153.4 75.1 %collective-permute-start.32 = (bf16[2,4,2,96,768]{4,3,2,1,0:T(8,128)(2,1)}, bf16[2,4,2,96,768]{4,3,2,1,0:T(8,128)(2,1)}, u32[]{:S(2)}, u32[]{:S(2)}) collective-permute-start(bf16[2,4,2,96,768]{4,3,2,1,0:T(8,128)(2,1)} %get-tuple-element.73), channel_id=1, source_target_pairs={{0,1},{1,0},{2,3},{3,2},{4,5},{5,4},{6,7},{7,6},{8,9},{9,8},{10,11... | collective-permute-start | bytes 7077896 | tf_op jit(solution)/shard_map/ppermute | solution.py:102
  157.1 39.0 %collective-permute-start.24 = (bf16[2,4,2,24,3072]{4,3,1,2,0:T(8,128)(2,1)S(1)}, bf16[2,4,2,24,3072]{4,3,1,2,0:T(8,128)(2,1)S(1)}, u32[]{:S(2)}, u32[]{:S(2)}) collective-permute-start(bf16[2,4,2,24,3072]{4,3,1,2,0:T(8,128)(2,1)S(1)} %get-tuple-element.75), channel_id=1, source_target_pairs={{0,1},{1,0},{2,3},{3,2},{4,5},{5,4},{6,7},{7,6},{8,9},{9,8},{10,11... | collective-permute-start | bytes 7077896 | tf_op jit(solution)/shard_map/ppermute | solution.py:102
  163.2 36.3 %collective-permute-start.16 = (bf16[2,4,2,24,3072]{4,3,2,1,0:T(8,128)(2,1)S(1)}, bf16[2,4,2,24,3072]{4,3,2,1,0:T(8,128)(2,1)S(1)}, u32[]{:S(2)}, u32[]{:S(2)}) collective-permute-start(bf16[2,4,2,24,3072]{4,3,2,1,0:T(8,128)(2,1)S(1)} %get-tuple-element.80), channel_id=1, source_target_pairs={{0,1},{1,0},{2,3},{3,2},{4,5},{5,4},{6,7},{7,6},{8,9},{9,8},{10,11... | collective-permute-start | bytes 7077896 | tf_op jit(solution)/shard_map/ppermute | solution.py:102
  338.8 59.5 %collective-permute-start.33 = (f32[1,1]{1,0:T(1,128)}, f32[1,1]{1,0:T(1,128)}, u32[]{:S(2)}, u32[]{:S(2)}) collective-permute-start(f32[1,1]{1,0:T(1,128)} %bitcast.100), channel_id=1, source_target_pairs={{0,16},{1,17},{2,18},{3,19},{4,20},{5,21},{6,22},{7,23},{8,24},{9,... | collective-permute-start | bytes 20 | tf_op jit(solution)/shard_map/ppermute | solution.py:102
  345.9 84.3 %collective-permute-start.51 = (bf16[2,4,2,24,3072]{4,3,1,2,0:T(8,128)(2,1)}, bf16[2,4,2,24,3072]{4,3,1,2,0:T(8,128)(2,1)}, u32[]{:S(2)}, u32[]{:S(2)}) collective-permute-start(bf16[2,4,2,24,3072]{4,3,1,2,0:T(8,128)(2,1)} %fusion.25), channel_id=1, source_target_pairs={{0,1},{1,0},{2,3},{3,2},{4,5},{5,4},{6,7},{7,6},{8,9},{9,8},{10,11... | collective-permute-start | bytes 7077896 | tf_op jit(solution)/shard_map/ppermute | solution.py:102
  377.7 21.9 %collective-permute-start.35 = (bf16[2,4,2,16,2304]{4,3,1,2,0:T(8,128)(2,1)}, bf16[2,4,2,16,2304]{4,3,1,2,0:T(8,128)(2,1)}, u32[]{:S(2)}, u32[]{:S(2)}) collective-permute-start(bf16[2,4,2,16,2304]{4,3,1,2,0:T(8,128)(2,1)} %fusion.41), channel_id=1, source_target_pairs={{0,1},{1,0},{2,3},{3,2},{4,5},{5,4},{6,7},{7,6},{8,9},{9,8},{10,11... | collective-permute-start | bytes 3538952 | tf_op jit(solution)/shard_map/ppermute | solution.py:102
  381.9 55.1 %collective-permute-start.59 = (bf16[2,4,2,96,768]{4,3,1,2,0:T(8,128)(2,1)}, bf16[2,4,2,96,768]{4,3,1,2,0:T(8,128)(2,1)}, u32[]{:S(2)}, u32[]{:S(2)}) collective-permute-start(bf16[2,4,2,96,768]{4,3,1,2,0:T(8,128)(2,1)} %fusion.26), channel_id=1, source_target_pairs={{0,1},{1,0},{2,3},{3,2},{4,5},{5,4},{6,7},{7,6},{8,9},{9,8},{10,11... | collective-permute-start | bytes 7077896 | tf_op jit(solution)/shard_map/ppermute | solution.py:102
  385.6 16.8 %collective-permute-start.34 = (bf16[1024,256]{1,0:T(8,128)(2,1)}, bf16[1024,256]{1,0:T(8,128)(2,1)S(1)}, u32[]{:S(2)}, u32[]{:S(2)}) collective-permute-start(bf16[1024,256]{1,0:T(8,128)(2,1)} %reshape.984), channel_id=1, source_target_pairs={{0,16},{1,17},{2,18},{3,19},{4,20},{5,21},{6,22},{7,23},{8,24},{9,... | collective-permute-start | bytes 1572872 | tf_op jit(solution)/shard_map/ppermute | solution.py:102
  402.3 8.9 %collective-permute-start.36 = (bf16[2,4,16,1152]{3,2,1,0:T(8,128)(2,1)S(1)}, bf16[2,4,16,1152]{3,2,1,0:T(8,128)(2,1)S(1)}, u32[]{:S(2)}, u32[]{:S(2)}) collective-permute-start(bf16[2,4,16,1152]{3,2,1,0:T(8,128)(2,1)S(1)} %fusion.83), channel_id=1, source_target_pairs={{0,2},{1,3},{2,0},{3,1},{4,6},{5,7},{6,4},{7,5},{8,10},{9,11},{10,... | collective-permute-start | bytes 884744 | tf_op jit(solution)/shard_map/ppermute | solution.py:102
  402.6 10.3 %collective-permute-start.38 = (bf16[4,2,16,1152]{3,2,0,1:T(8,128)(2,1)S(1)}, bf16[4,2,16,1152]{3,2,0,1:T(8,128)(2,1)S(1)}, u32[]{:S(2)}, u32[]{:S(2)}) collective-permute-start(bf16[4,2,16,1152]{3,2,0,1:T(8,128)(2,1)S(1)} %fusion.84), channel_id=1, source_target_pairs={{0,16},{1,17},{2,18},{3,19},{4,20},{5,21},{6,22},{7,23},{8,24},{9,... | collective-permute-start | bytes 884744 | tf_op jit(solution)/shard_map/ppermute | solution.py:102
  418.2 6.3 %collective-permute-start.40 = (bf16[16,2304]{1,0:T(8,128)(2,1)S(1)}, bf16[16,2304]{1,0:T(8,128)(2,1)S(1)}, u32[]{:S(2)}, u32[]{:S(2)}) collective-permute-start(bf16[16,2304]{1,0:T(8,128)(2,1)S(1)} %get-tuple-element.106), channel_id=1, source_target_pairs={{0,4},{1,5},{2,6},{3,7},{4,8},{5,9},{6,10},{7,11},{8,12},{9,13},{1... | collective-permute-start | bytes 221192 | tf_op jit(solution)/shard_map/ppermute | solution.py:102
  418.3 6.3 %collective-permute-start.41 = (bf16[16,2304]{1,0:T(8,128)(2,1)S(1)}, bf16[16,2304]{1,0:T(8,128)(2,1)S(1)}, u32[]{:S(2)}, u32[]{:S(2)}) collective-permute-start(bf16[16,2304]{1,0:T(8,128)(2,1)S(1)} %get-tuple-element.107), channel_id=1, source_target_pairs={{0,8},{1,9},{2,10},{3,11},{4,12},{5,13},{6,14},{7,15},{8,0},{9,1},... | collective-permute-start | bytes 221192 | tf_op jit(solution)/shard_map/ppermute | solution.py:102
  418.8 6.5 %collective-permute-start.42 = (bf16[16,2304]{1,0:T(8,128)(2,1)S(1)}, bf16[16,2304]{1,0:T(8,128)(2,1)S(1)}, u32[]{:S(2)}, u32[]{:S(2)}) collective-permute-start(bf16[16,2304]{1,0:T(8,128)(2,1)S(1)} %get-tuple-element.108), channel_id=1, source_target_pairs={{0,12},{1,13},{2,14},{3,15},{4,0},{5,1},{6,2},{7,3},{8,4},{9,5},{1... | collective-permute-start | bytes 221192 | tf_op jit(solution)/shard_map/ppermute | solution.py:102
  424.6 18.1 %collective-permute-start.43 = (bf16[2,4,2,24,3072]{4,3,1,2,0:T(8,128)(2,1)}, bf16[2,4,2,24,3072]{4,3,1,2,0:T(8,128)(2,1)}, u32[]{:S(2)}, u32[]{:S(2)}) collective-permute-start(bf16[2,4,2,24,3072]{4,3,1,2,0:T(8,128)(2,1)} %fusion.24), channel_id=1, source_target_pairs={{0,1},{1,0},{2,3},{3,2},{4,5},{5,4},{6,7},{7,6},{8,9},{9,8},{10,11... | collective-permute-start | bytes 7077896 | tf_op jit(solution)/shard_map/ppermute | solution.py:102
  434.4 16.5 %collective-permute-start.52 = (bf16[2,4,24,1536]{3,2,1,0:T(8,128)(2,1)}, bf16[2,4,24,1536]{3,2,1,0:T(8,128)(2,1)}, u32[]{:S(2)}, u32[]{:S(2)}) collective-permute-start(bf16[2,4,24,1536]{3,2,1,0:T(8,128)(2,1)} %fusion.63), channel_id=1, source_target_pairs={{0,2},{1,3},{2,0},{3,1},{4,6},{5,7},{6,4},{7,5},{8,10},{9,11},{10,... | collective-permute-start | bytes 1769480 | tf_op jit(solution)/shard_map/ppermute | solution.py:102
  435.8 16.9 %collective-permute-start.54 = (bf16[4,2,24,1536]{3,2,0,1:T(8,128)(2,1)}, bf16[4,2,24,1536]{3,2,0,1:T(8,128)(2,1)}, u32[]{:S(2)}, u32[]{:S(2)}) collective-permute-start(bf16[4,2,24,1536]{3,2,0,1:T(8,128)(2,1)} %fusion.64), channel_id=1, source_target_pairs={{0,16},{1,17},{2,18},{3,19},{4,20},{5,21},{6,22},{7,23},{8,24},{9,... | collective-permute-start | bytes 1769480 | tf_op jit(solution)/shard_map/ppermute | solution.py:102
  440.1 23.4 %collective-permute-start.60 = (bf16[2,4,96,384]{3,2,1,0:T(8,128)(2,1)S(1)}, bf16[2,4,96,384]{3,2,1,0:T(8,128)(2,1)S(1)}, u32[]{:S(2)}, u32[]{:S(2)}) collective-permute-start(bf16[2,4,96,384]{3,2,1,0:T(8,128)(2,1)S(1)} %fusion.65), channel_id=1, source_target_pairs={{0,2},{1,3},{2,0},{3,1},{4,6},{5,7},{6,4},{7,5},{8,10},{9,11},{10,... | collective-permute-start | bytes 1769480 | tf_op jit(solution)/shard_map/ppermute | solution.py:102
  441.0 23.9 %collective-permute-start.62 = (bf16[4,2,96,384]{3,2,0,1:T(8,128)(2,1)S(1)}, bf16[4,2,96,384]{3,2,0,1:T(8,128)(2,1)S(1)}, u32[]{:S(2)}, u32[]{:S(2)}) collective-permute-start(bf16[4,2,96,384]{3,2,0,1:T(8,128)(2,1)S(1)} %fusion.66), channel_id=1, source_target_pairs={{0,16},{1,17},{2,18},{3,19},{4,20},{5,21},{6,22},{7,23},{8,24},{9,... | collective-permute-start | bytes 1769480 | tf_op jit(solution)/shard_map/ppermute | solution.py:102
  445.7 30.4 %collective-permute-start.44 = (bf16[2,4,24,1536]{3,2,1,0:T(8,128)(2,1)S(1)}, bf16[2,4,24,1536]{3,2,1,0:T(8,128)(2,1)S(1)}, u32[]{:S(2)}, u32[]{:S(2)}) collective-permute-start(bf16[2,4,24,1536]{3,2,1,0:T(8,128)(2,1)S(1)} %fusion.61), channel_id=1, source_target_pairs={{0,2},{1,3},{2,0},{3,1},{4,6},{5,7},{6,4},{7,5},{8,10},{9,11},{10,... | collective-permute-start | bytes 1769480 | tf_op jit(solution)/shard_map/ppermute | solution.py:102
  450.9 26.6 %collective-permute-start.46 = (bf16[4,2,24,1536]{3,2,0,1:T(8,128)(2,1)S(1)}, bf16[4,2,24,1536]{3,2,0,1:T(8,128)(2,1)S(1)}, u32[]{:S(2)}, u32[]{:S(2)}) collective-permute-start(bf16[4,2,24,1536]{3,2,0,1:T(8,128)(2,1)S(1)} %fusion.62), channel_id=1, source_target_pairs={{0,16},{1,17},{2,18},{3,19},{4,20},{5,21},{6,22},{7,23},{8,24},{9,... | collective-permute-start | bytes 1769480 | tf_op jit(solution)/shard_map/ppermute | solution.py:102
  452.7 31.2 %collective-permute-start.53 = (bf16[4,24,1536]{2,1,0:T(8,128)(2,1)S(1)}, bf16[4,24,1536]{2,1,0:T(8,128)(2,1)S(1)}, u32[]{:S(2)}, u32[]{:S(2)}) collective-permute-start(bf16[4,24,1536]{2,1,0:T(8,128)(2,1)S(1)} %fusion.87), channel_id=1, source_target_pairs={{0,16},{1,17},{2,18},{3,19},{4,20},{5,21},{6,22},{7,23},{8,24},{9,... | collective-permute-start | bytes 884744 | tf_op jit(solution)/shard_map/ppermute | solution.py:102
  463.5 22.0 %collective-permute-start.55 = (bf16[4,24,1536]{2,1,0:T(8,128)(2,1)S(1)}, bf16[4,24,1536]{2,1,0:T(8,128)(2,1)S(1)}, u32[]{:S(2)}, u32[]{:S(2)}) collective-permute-start(bf16[4,24,1536]{2,1,0:T(8,128)(2,1)S(1)} %fusion.88), channel_id=1, source_target_pairs={{0,2},{1,3},{2,0},{3,1},{4,6},{5,7},{6,4},{7,5},{8,10},{9,11},{10,... | collective-permute-start | bytes 884744 | tf_op jit(solution)/shard_map/ppermute | solution.py:102
  464.9 25.3 %collective-permute-start.61 = (bf16[4,96,384]{2,1,0:T(8,128)(2,1)S(1)}, bf16[4,96,384]{2,1,0:T(8,128)(2,1)S(1)}, u32[]{:S(2)}, u32[]{:S(2)}) collective-permute-start(bf16[4,96,384]{2,1,0:T(8,128)(2,1)S(1)} %fusion.89), channel_id=1, source_target_pairs={{0,16},{1,17},{2,18},{3,19},{4,20},{5,21},{6,22},{7,23},{8,24},{9,... | collective-permute-start | bytes 884744 | tf_op jit(solution)/shard_map/ppermute | solution.py:102
  476.1 15.2 %collective-permute-start.63 = (bf16[4,96,384]{2,1,0:T(8,128)(2,1)S(1)}, bf16[4,96,384]{2,1,0:T(8,128)(2,1)S(1)}, u32[]{:S(2)}, u32[]{:S(2)}) collective-permute-start(bf16[4,96,384]{2,1,0:T(8,128)(2,1)S(1)} %fusion.90), channel_id=1, source_target_pairs={{0,2},{1,3},{2,0},{3,1},{4,6},{5,7},{6,4},{7,5},{8,10},{9,11},{10,... | collective-permute-start | bytes 884744 | tf_op jit(solution)/shard_map/ppermute | solution.py:102
  477.5 17.2 %collective-permute-start.45 = (bf16[4,24,1536]{2,1,0:T(8,128)(2,1)S(1)}, bf16[4,24,1536]{2,1,0:T(8,128)(2,1)S(1)}, u32[]{:S(2)}, u32[]{:S(2)}) collective-permute-start(bf16[4,24,1536]{2,1,0:T(8,128)(2,1)S(1)} %fusion.85), channel_id=1, source_target_pairs={{0,16},{1,17},{2,18},{3,19},{4,20},{5,21},{6,22},{7,23},{8,24},{9,... | collective-permute-start | bytes 884744 | tf_op jit(solution)/shard_map/ppermute | solution.py:102
  483.9 10.9 %collective-permute-start.47 = (bf16[4,24,1536]{2,1,0:T(8,128)(2,1)S(1)}, bf16[4,24,1536]{2,1,0:T(8,128)(2,1)S(1)}, u32[]{:S(2)}, u32[]{:S(2)}) collective-permute-start(bf16[4,24,1536]{2,1,0:T(8,128)(2,1)S(1)} %fusion.86), channel_id=1, source_target_pairs={{0,2},{1,3},{2,0},{3,1},{4,6},{5,7},{6,4},{7,5},{8,10},{9,11},{10,... | collective-permute-start | bytes 884744 | tf_op jit(solution)/shard_map/ppermute | solution.py:102
  485.6 11.6 %collective-permute-start.56 = (bf16[24,3072]{1,0:T(8,128)(2,1)S(1)}, bf16[24,3072]{1,0:T(8,128)(2,1)S(1)}, u32[]{:S(2)}, u32[]{:S(2)}) collective-permute-start(bf16[24,3072]{1,0:T(8,128)(2,1)S(1)} %get-tuple-element.88), channel_id=1, source_target_pairs={{0,4},{1,5},{2,6},{3,7},{4,8},{5,9},{6,10},{7,11},{8,12},{9,13},{1... | collective-permute-start | bytes 442376 | tf_op jit(solution)/shard_map/ppermute | solution.py:102
  490.2 21.2 %collective-permute-start.57 = (bf16[24,3072]{1,0:T(8,128)(2,1)S(1)}, bf16[24,3072]{1,0:T(8,128)(2,1)S(1)}, u32[]{:S(2)}, u32[]{:S(2)}) collective-permute-start(bf16[24,3072]{1,0:T(8,128)(2,1)S(1)} %get-tuple-element.89), channel_id=1, source_target_pairs={{0,8},{1,9},{2,10},{3,11},{4,12},{5,13},{6,14},{7,15},{8,0},{9,1},... | collective-permute-start | bytes 442376 | tf_op jit(solution)/shard_map/ppermute | solution.py:102
  491.3 20.1 %collective-permute-start.58 = (bf16[24,3072]{1,0:T(8,128)(2,1)S(1)}, bf16[24,3072]{1,0:T(8,128)(2,1)S(1)}, u32[]{:S(2)}, u32[]{:S(2)}) collective-permute-start(bf16[24,3072]{1,0:T(8,128)(2,1)S(1)} %get-tuple-element.90), channel_id=1, source_target_pairs={{0,12},{1,13},{2,14},{3,15},{4,0},{5,1},{6,2},{7,3},{8,4},{9,5},{1... | collective-permute-start | bytes 442376 | tf_op jit(solution)/shard_map/ppermute | solution.py:102
  494.7 28.4 %collective-permute-start.64 = (bf16[96,768]{1,0:T(8,128)(2,1)S(1)}, bf16[96,768]{1,0:T(8,128)(2,1)S(1)}, u32[]{:S(2)}, u32[]{:S(2)}) collective-permute-start(bf16[96,768]{1,0:T(8,128)(2,1)S(1)} %get-tuple-element.85), channel_id=1, source_target_pairs={{0,4},{1,5},{2,6},{3,7},{4,8},{5,9},{6,10},{7,11},{8,12},{9,13},{1... | collective-permute-start | bytes 442376 | tf_op jit(solution)/shard_map/ppermute | solution.py:102
  494.8 28.3 %collective-permute-start.65 = (bf16[96,768]{1,0:T(8,128)(2,1)S(1)}, bf16[96,768]{1,0:T(8,128)(2,1)S(1)}, u32[]{:S(2)}, u32[]{:S(2)}) collective-permute-start(bf16[96,768]{1,0:T(8,128)(2,1)S(1)} %get-tuple-element.86), channel_id=1, source_target_pairs={{0,8},{1,9},{2,10},{3,11},{4,12},{5,13},{6,14},{7,15},{8,0},{9,1},... | collective-permute-start | bytes 442376 | tf_op jit(solution)/shard_map/ppermute | solution.py:102
  497.2 15.0 %collective-permute-start.48 = (bf16[24,3072]{1,0:T(8,128)(2,1)S(1)}, bf16[24,3072]{1,0:T(8,128)(2,1)S(1)}, u32[]{:S(2)}, u32[]{:S(2)}) collective-permute-start(bf16[24,3072]{1,0:T(8,128)(2,1)S(1)} %get-tuple-element.91), channel_id=1, source_target_pairs={{0,4},{1,5},{2,6},{3,7},{4,8},{5,9},{6,10},{7,11},{8,12},{9,13},{1... | collective-permute-start | bytes 442376 | tf_op jit(solution)/shard_map/ppermute | solution.py:102
  511.4 9.0 %collective-permute-start.49 = (bf16[24,3072]{1,0:T(8,128)(2,1)S(1)}, bf16[24,3072]{1,0:T(8,128)(2,1)S(1)}, u32[]{:S(2)}, u32[]{:S(2)}) collective-permute-start(bf16[24,3072]{1,0:T(8,128)(2,1)S(1)} %get-tuple-element.92), channel_id=1, source_target_pairs={{0,8},{1,9},{2,10},{3,11},{4,12},{5,13},{6,14},{7,15},{8,0},{9,1},... | collective-permute-start | bytes 442376 | tf_op jit(solution)/shard_map/ppermute | solution.py:102
  511.4 10.4 %collective-permute-start.50 = (bf16[24,3072]{1,0:T(8,128)(2,1)S(1)}, bf16[24,3072]{1,0:T(8,128)(2,1)S(1)}, u32[]{:S(2)}, u32[]{:S(2)}) collective-permute-start(bf16[24,3072]{1,0:T(8,128)(2,1)S(1)} %get-tuple-element.93), channel_id=1, source_target_pairs={{0,12},{1,13},{2,14},{3,15},{4,0},{5,1},{6,2},{7,3},{8,4},{9,5},{1... | collective-permute-start | bytes 442376 | tf_op jit(solution)/shard_map/ppermute | solution.py:102
  512.2 13.7 %collective-permute-start.66 = (bf16[96,768]{1,0:T(8,128)(2,1)S(1)}, bf16[96,768]{1,0:T(8,128)(2,1)S(1)}, u32[]{:S(2)}, u32[]{:S(2)}) collective-permute-start(bf16[96,768]{1,0:T(8,128)(2,1)S(1)} %get-tuple-element.87), channel_id=1, source_target_pairs={{0,12},{1,13},{2,14},{3,15},{4,0},{5,1},{6,2},{7,3},{8,4},{9,5},{1... | collective-permute-start | bytes 442376 | tf_op jit(solution)/shard_map/ppermute | solution.py:102
  (89 other events, 510.2 us)

commit v2 on v1

v2 whole, which is shorter than its diff:
```python
import functools
import math

import jax
import jax.numpy as jnp
from jax import lax
from jax.experimental import pallas as pl
from jax.experimental.pallas import tpu as pltpu
from jax.sharding import PartitionSpec as P

D = 768
H = 12
HD = 64
FF = 3072
C = 512
PD = 256
UTTS = 3
PAIR = 2 * HD
FMB = 512
NEG = 100
NMASK = 256
SPARE = 256
SLOTS = 16

SPLIT = ("z", "x", "core")
BOTH = ("section",) + SPLIT
norm_eps = 1e-05
unit_eps = 1e-06
sharpness = 10.0
masked_score = -1000000000.0
precise = lax.Precision.HIGHEST
low = jnp.bfloat16
full = jnp.float32

VECTORS = (
    ("up_bias", FF),
    ("ln0_gain", C),
    ("ln0_bias", C),
    ("proj0_bias", D),
    ("mask_emb", D),
    ("qv_bias", 2 * D),
    ("out_bias", D),
    ("ln1_gain", D),
    ("ln1_bias", D),
    ("down_bias", D),
    ("ln2_gain", D),
    ("ln2_bias", D),
    ("final_bias", PD),
)
VECTOR_TOTAL = sum(size for _, size in VECTORS)
start_of = {name: sum(size for _, size in VECTORS[:i]) for i, (name, _) in enumerate(VECTORS)}
QV_START = start_of["qv_bias"]


def plain_dot(left_side, right_side):
    return jnp.dot(left_side, right_side, preferred_element_type=full)


def left_dot(left_side, right_side):
    return lax.dot_general(
        left_side, right_side, (((0,), (0,)), ((), ())), preferred_element_type=full
    )


def right_dot(left_side, right_side):
    return lax.dot_general(
        left_side, right_side, (((1,), (1,)), ((), ())), preferred_element_type=full
    )


def gelu_and_slope(x):
    size = jnp.abs(x)
    bell = jnp.exp(-0.5 * x * x)
    t = 1.0 / (1.0 + 0.23164189 * size)
    poly = t * (0.127414796 + t * (-0.142248368 + t * (0.7107068705 + t * (-0.7265760135 + t * 0.5307027145))))
    tail = poly * bell
    below = jnp.where(x >= 0, 1.0 - tail, tail)
    return x * below, below + x * (0.3989422804 * bell)


class Links:
    def __init__(self):
        self.depth = lax.axis_size("z")
        self.per_section = 4 * self.depth
        self.core = lax.axis_index("core")
        self.x = lax.axis_index("x")
        self.z = lax.axis_index("z")
        self.y = lax.axis_index("section")
        self.sizes, self.upper = [], []
        size, place = self.depth, self.z
        while size > 1:
            self.sizes.append(size)
            self.upper.append((place >= size // 2).astype(jnp.int32))
            place = jnp.where(place >= size // 2, size - 1 - place, place)
            size //= 2

    def move(self, value, where):
        pairs = []
        for y in range(2):
            for z in range(self.depth):
                for x in range(2):
                    for core in range(2):
                        ty, tz, tx, tcore = where(y, z, x, core)
                        pairs.append(
                            (
                                y * self.per_section + z * 4 + x * 2 + core,
                                ty * self.per_section + tz * 4 + tx * 2 + tcore,
                            )
                        )
        return lax.ppermute(value, BOTH, pairs)

    def over_x(self, value):
        return self.move(value, lambda y, z, x, core: (y, z, 1 - x, core))

    def over_y(self, value):
        return self.move(value, lambda y, z, x, core: (1 - y, z, x, core))

    def over_core(self, value):
        return self.move(value, lambda y, z, x, core: (y, z, x, 1 - core))

    def over_both(self, value):
        return self.move(value, lambda y, z, x, core: (1 - y, z, 1 - x, core))

    def along_z(self, value, steps):
        return self.move(value, lambda y, z, x, core: (y, (z + steps) % self.depth, x, core))

    def over_z(self, value, size):
        def where(y, z, x, core):
            return (y, z - z % size + size - 1 - z % size, x, core)

        return self.move(value, where)


def pick(value, index, axis):
    axis = axis % value.ndim
    return lax.squeeze(lax.dynamic_slice_in_dim(value, index, 1, axis), (axis,))


def in_order(index, own, got, axis):
    axis = axis % own.ndim
    own, got = jnp.expand_dims(own, axis), jnp.expand_dims(got, axis)
    shape = own.shape[:axis] + (2,) + own.shape[axis + 1 :]
    return jnp.where(lax.broadcasted_iota(jnp.int32, shape, axis) == index, own, got)


def in_line(uppers, own, got):
    shape = (own.shape[0], 2) + own.shape[1:]
    turn = (
        lax.broadcasted_iota(jnp.int32, shape, 0) + lax.broadcasted_iota(jnp.int32, shape, 1)
    ) % 2
    line = jnp.where(turn == uppers[-1], jnp.expand_dims(own, 1), jnp.expand_dims(got, 1))
    line = line.reshape((-1,) + own.shape[1:])
    for _ in range(2, len(uppers)):
        line = jnp.concatenate([line[:, 0], jnp.flip(line[:, 1], 0)], axis=0)
    return line


class Gather:
    def __init__(self, links, line, cut, parts=1):
        self.links, self.line, self.cut, self.parts = links, line, cut, parts
        self.got = []

    def start_z(self):
        self.got = [self.links.over_z(self.line, self.links.sizes[0])]

    def start_z_rest(self):
        links = self.links
        for step in range(1, len(links.sizes)):
            self.line = in_order(links.upper[step - 1], self.line, self.got[0], 0)
            self.got = [links.over_z(self.line, links.sizes[step])]

    def start_first(self):
        links = self.links
        line = in_line(links.upper, self.line, self.got[0])
        self.first, self.second = line[..., : self.cut], line[..., self.cut :]
        if self.parts > 1:
            shape = self.second.shape
            self.second = self.second.reshape(shape[:2] + (self.parts, -1)).swapaxes(1, 2)
            self.second = self.second.reshape(shape[0], -1, shape[2] // self.parts)
        self.got = [links.over_x(self.first), links.over_y(self.second)]

    def start_second(self):
        links = self.links
        self.first = in_order(links.x, self.first, self.got[0], -2)
        self.second = in_order(links.y, self.second, self.got[1], -3)
        self.got = [links.over_y(self.first), links.over_x(self.second)]

    def start_core(self):
        links = self.links
        self.lanes = [
            in_order(links.y, self.first, self.got[0], -4),
            in_order(links.x, self.second, self.got[1], -2),
        ]
        self.lanes = lax.optimization_barrier(self.lanes)
        self.got = [links.over_core(lane) for lane in self.lanes]

    def whole(self):
        core = self.links.core
        return [
            in_order(core, own, got, -2).reshape(-1, own.shape[-1])
            for own, got in zip(self.lanes, self.got)
        ]

    def apart(self):
        lanes = [x for pair in zip(self.lanes, self.got) for x in pair]
        return [x.reshape(-1, x.shape[-1]) for x in lanes]


class Line:
    def __init__(self, links, line):
        self.links, self.line = links, line

    def start_z(self):
        self.start_line(self.line)

    def start_line(self, line):
        links = self.links
        for size in links.sizes[:-1]:
            line = jnp.stack([line[: size // 2], jnp.flip(line[size // 2 :], 0)], axis=1)
        self.line = line
        self.got = [links.over_z(pick(line, 1 - links.upper[-1], 0), links.sizes[-1])]

    def start_z_rest(self):
        links = self.links
        for step in range(len(links.sizes) - 2, -1, -1):
            self.line = added(pick(self.line, links.upper[step + 1], 0), self.got[0])
            away = pick(self.line, 1 - links.upper[step], 0)
            self.got = [links.over_z(away, links.sizes[step])]

    def total(self):
        return pick(self.line, self.links.upper[0], 0).astype(full) + self.got[0].astype(full)


class Sum(Line):
    def __init__(self, links, keep, send, cut):
        self.links, self.cut = links, cut
        self.grid = (2, links.depth, 2, -1, keep.shape[-1])
        self.keep, self.send = keep.reshape(self.grid), send
        self.got = []

    def start_core(self):
        self.got = [self.links.over_core(self.send)]

    def start_first(self):
        links = self.links
        lane = added(self.keep, self.got[0].reshape(self.grid))
        self.first, self.second = lane[..., : self.cut], lane[..., self.cut :]
        self.got = [
            links.over_x(pick(self.first, 1 - links.x, -3)),
            links.over_y(pick(self.second, 1 - links.y, -5)),
        ]

    def start_plane(self):
        links = self.links
        lane = added(self.keep, self.got[0].reshape(self.grid))

        def part(y, x):
            return pick(pick(lane, x, -3), y, 0)

        self.line = part(links.y, links.x)
        self.got = [
            links.over_x(part(links.y, 1 - links.x)),
            links.over_y(part(1 - links.y, links.x)),
            links.over_both(part(1 - links.y, 1 - links.x)),
        ]

    def line_of(self):
        links = self.links
        if len(self.got) == 3:
            return total_of(self.line, self.got).astype(low)
        first = added(pick(self.first, links.y, -4), self.got[0])
        second = added(pick(self.second, links.x, -3), self.got[1])
        return jnp.concatenate([first, second], -1)

    def start_straight_z(self):
        links, line = self.links, self.line_of()
        self.line = pick(line, links.z, 0)
        self.got = [
            links.along_z(pick(line, (links.z + k) % links.depth, 0), k)
            for k in range(1, links.depth)
        ]

    def straight_total(self):
        return total_of(self.line, self.got)

    def start_second(self):
        links = self.links
        self.first = added(pick(self.first, links.x, -3), self.got[0])
        self.second = added(pick(self.second, links.y, -5), self.got[1])
        self.got = [
            links.over_y(pick(self.first, 1 - links.y, -4)),
            links.over_x(pick(self.second, 1 - links.x, -3)),
        ]

    def start_z(self):
        self.start_line(self.line_of())


def by_core(links, terms):
    lanes = terms.reshape(links.per_section, 2, -1, terms.shape[-1])
    return [
        pick(lanes, core, 1).reshape(-1, terms.shape[-1]) for core in (links.core, 1 - links.core)
    ]


def total_of(own, others):
    out = own.astype(full)
    for got in others:
        out = out + got.astype(full)
    return out


def added(own, got):
    return (own.astype(full) + got.astype(full)).astype(low)


def after(moves, *values):
    bound = lax.optimization_barrier((tuple(tuple(m.got) for m in moves), values))
    for move, got in zip(moves, bound[0]):
        move.got = list(got)
    return bound[1]


def owner_of(columns, part):
    factor = -(-(1 << 20) // part)
    assert all((n * factor) >> 20 == n // part for n in range(columns))
    lane = lax.broadcasted_iota(jnp.int32, (1, columns), 1)
    return lax.shift_right_logical(lane * factor, 20)


def spread_parts(rows, parts_ref, out_ref):
    start = 0
    devices = C // rows
    slot = (rows // 2) * SPARE // SLOTS
    each_row = SPARE // slot
    shape = (devices, C)
    across = lax.broadcasted_iota(jnp.int32, shape, 1)
    first = lax.broadcasted_iota(jnp.int32, shape, 0) * rows + rows // 2
    held = [
        plain_dot(jnp.where(across == first + k, 1.0, 0.0).astype(low), parts_ref[:, PD:]).astype(low)
        for k in range(rows // 2)
    ]
    for index, (_, size) in enumerate(VECTORS):
        part = size // devices
        owner = owner_of(size, part)
        place = lax.broadcasted_iota(jnp.int32, (1, size), 1) - owner * part
        lanes = jnp.where(lax.broadcasted_iota(jnp.int32, (slot, size), 0) == place, 1.0, 0.0)
        at = lax.broadcasted_iota(jnp.int32, (devices, size), 0) == owner
        begin = (index % each_row) * slot
        mine = held[index // each_row][:, begin : begin + slot]
        out_ref[:, start : start + size] = jnp.sum(
            jnp.where(at, plain_dot(mine, lanes.astype(low)), 0.0), axis=0, keepdims=True
        )
        start += size


def split_kernel(devices, *refs):
    out_ref = refs[-1]
    slot = out_ref.shape[2]
    for index, (_, size) in enumerate(VECTORS):
        part = size // devices
        owner = owner_of(size, part)
        place = lax.broadcasted_iota(jnp.int32, (1, size), 1) - owner * part
        lanes = jnp.where(lax.broadcasted_iota(jnp.int32, (slot, size), 0) == place, 1.0, 0.0)
        lanes = lanes.astype(low)
        rows = lax.broadcasted_iota(jnp.int32, (devices, size), 0) == owner
        values = refs[index][...]
        high = values.astype(low)
        rest = (values - high.astype(full)).astype(low)
        out_ref[index] = right_dot(
            jnp.where(rows, high.astype(full), 0.0).astype(low), lanes
        ) + right_dot(jnp.where(rows, rest.astype(full), 0.0).astype(low), lanes)
    for index in range(len(VECTORS), SLOTS):
        out_ref[index] = jnp.zeros((devices, slot), full)


def split_vectors(vectors, devices, slot):
    return pl.pallas_call(
        functools.partial(split_kernel, devices),
        out_shape=jax.ShapeDtypeStruct((SLOTS, devices, slot), full),
        compiler_params=pltpu.CompilerParams(vmem_limit_bytes=8 * 1024 * 1024),
        name="split_vectors",
    )(*vectors)


def count_kernel(chosen_ref, count_ref):
    rows = 64
    for block in range(FMB // rows):
        frames = block * rows + lax.broadcasted_iota(jnp.int32, (rows, NMASK), 0)

        def add_one(j, seen):
            return seen + jnp.where(frames == chosen_ref[pl.ds(j, 1), :], 1.0, 0.0)

        seen = lax.fori_loop(0, NEG, add_one, jnp.zeros((rows, NMASK), full), unroll=10)
        count_ref[pl.ds(block * rows, rows), :] = seen.astype(low)


def count_distractors(chosen):
    return pl.pallas_call(
        count_kernel,
        out_shape=jax.ShapeDtypeStruct((FMB, NMASK), low),
        in_specs=[pl.BlockSpec(memory_space=pltpu.VMEM)],
        out_specs=pl.BlockSpec(memory_space=pltpu.VMEM),
        cost_estimate=pl.CostEstimate(flops=1, bytes_accessed=1, transcendentals=0),
    )(chosen.T)


def head_lanes(rows, which):
    lane = lax.broadcasted_iota(jnp.int32, (rows, PAIR), 1)
    return (lane < HD) if which == 0 else (lane >= HD)
def fill_mask(row_ref, col_ref, mask_ref):
    mask_ref[...] = jnp.where(col_ref[...] == row_ref[...], 0.0, masked_score)
def spare_lanes(which):
    lane = lax.broadcasted_iota(jnp.int32, (FMB, PAIR), 1)
    return lane - HD if which == 0 else jnp.where(lane >= HD, -1, lane)


def lane_value(spare, columns):
    value = jnp.zeros((FMB, PAIR), full)
    for place, column in columns:
        value = jnp.where(spare == place, column, value)
    return value


def score_sides(q_ref, k_ref, col_ref, which):
    spare = spare_lanes(which)
    segment = col_ref[...]
    same = [(u, jnp.where(segment == u, 1.0, 0.0)) for u in range(UTTS)]
    keys = [(u, 1.0 - value) for u, value in same]
    queries = [(u, masked_score * value) for u, value in same]
    scaled = q_ref[...] * jnp.asarray(1.0 / math.sqrt(HD), low)
    keys = jnp.where(spare < 0, k_ref[...], lane_value(spare, keys).astype(low))
    queries = jnp.where(spare < 0, scaled, lane_value(spare, queries).astype(low))
    return keys, queries


def attention_kernel(col_ref, q_ref, k_ref, v_ref, mixed_ref, log_ref):
    parts, logs = [], []
    for which in range(2):
        keys, queries = score_sides(q_ref, k_ref, col_ref, which)
        scores = right_dot(queries, keys)
        top = jnp.max(scores, axis=1, keepdims=True)
        shares = jnp.exp(scores - top)
        total = jnp.sum(shares, axis=1, keepdims=True)
        parts.append(plain_dot(shares.astype(low), v_ref[...]) * (1.0 / total))
        logs.append(top + jnp.log(total))
    mixed_ref[...] = jnp.where(spare_lanes(0) < 0, parts[0], parts[1]).astype(low)
    log_ref[0] = jnp.concatenate(logs + [jnp.zeros((FMB, 6), full)], 1).T


def attention_forward(qk, values, seg):
    pairs = H // 2

    def spec(first):
        return pl.BlockSpec((FMB, PAIR), lambda i: (0, i + first))

    return pl.pallas_call(
        attention_kernel,
        grid=(pairs,),
        in_specs=[pl.BlockSpec((FMB, 1), lambda i: (0, 0)), spec(0), spec(pairs), spec(0)],
        out_specs=[spec(0), pl.BlockSpec((1, 8, FMB), lambda i: (i, 0, 0))],
        out_shape=[
            jax.ShapeDtypeStruct((FMB, D), low),
            jax.ShapeDtypeStruct((pairs, 8, FMB), full),
        ],
        compiler_params=pltpu.CompilerParams(vmem_limit_bytes=14 * 1024 * 1024),
        cost_estimate=pl.CostEstimate(flops=1, bytes_accessed=1, transcendentals=0),
        name="attention_forward",
    )(seg.reshape(FMB, 1), qk, qk, values)


def attention_back_kernel(row_ref, col_ref, q_ref, k_ref, v_ref, dm_ref, log_ref, out_ref, d_values_ref, mask_ref):
    i = pl.program_id(0)
    @pl.when(i == 0)
    def _():
        fill_mask(row_ref, col_ref, mask_ref)
    queries = q_ref[...] * jnp.asarray(1.0/math.sqrt(HD), low)
    d_mixed = dm_ref[...]
    keys_t = (k_ref[...] * jnp.asarray(1.0/math.sqrt(HD), low)).T
    d_keys = d_values = None
    d_queries = []
    for which in range(2):
        lanes = head_lanes(FMB, which)
        keys = jnp.where(lanes, k_ref[...], 0).astype(low)
        values = jnp.where(lanes, v_ref[...], 0).astype(low)
        shares = jnp.exp(right_dot(keys, queries) + mask_ref[...] - log_ref[0, which:which+1, :])
        d_shares = right_dot(values, d_mixed)
        inner = jnp.sum(shares * d_shares, axis=0, keepdims=True)
        d_scores = (shares * (d_shares - inner)).astype(low)
        dv = plain_dot(shares.astype(low), d_mixed)
        dk = plain_dot(d_scores, queries)
        d_queries.append(plain_dot(keys_t[which*HD:(which+1)*HD], d_scores))
        if which == 0:
            d_values, d_keys = dv, dk
        else:
            d_values, d_keys = jnp.where(lanes, dv, d_values), jnp.where(lanes, dk, d_keys)
    out_ref[:, pl.ds(pl.multiple_of(i*PAIR, PAIR), PAIR)] = jnp.concatenate(d_queries, 0).T.astype(low)
    out_ref[:, pl.ds(pl.multiple_of(D + i*PAIR, PAIR), PAIR)] = d_keys.astype(low)
    d_values_ref[...] = d_values.astype(low)
def attention_backward(qk, values, seg, d_mixed, logs):
    pairs = H//2
    spec = lambda off: pl.BlockSpec((FMB, PAIR), lambda i: (0, i+off))
    return pl.pallas_call(attention_back_kernel, grid=(pairs,),
        in_specs=[pl.BlockSpec((1,FMB), lambda i:(0,0)), pl.BlockSpec((FMB,1), lambda i:(0,0)), spec(0), spec(pairs), spec(0), spec(0), pl.BlockSpec((1,8,FMB), lambda i:(i,0,0))],
        out_specs=[pl.BlockSpec((FMB,2*D), lambda i:(0,0)), spec(0)],
        out_shape=[jax.ShapeDtypeStruct((FMB,2*D),low), jax.ShapeDtypeStruct((FMB,D),low)],
        scratch_shapes=[pltpu.VMEM((FMB,FMB),full)],
        compiler_params=pltpu.CompilerParams(vmem_limit_bytes=56 * 1024 * 1024),
        cost_estimate=pl.CostEstimate(flops=1, bytes_accessed=1, transcendentals=0),
        name="attention_backward")(seg.reshape(1,FMB), seg.reshape(FMB,1), qk, qk, values, d_mixed, logs)


def column_sum(value):
    return jnp.sum(value, axis=0, keepdims=True)
def middle_kernel(each, hidden_ref, slope_ref, blocks_ref, first_ref, final_ref, down_bias_ref, gain_ref, shift_ref, final_bias_ref,
                  targets_ref, counts_ref, masked_ref,
                  second_ref, d_proj_ref, d_ffn_ref, d_pre_ref, loss_ref, g_down_bias_ref, g_gain_ref, g_shift_ref, g_final_bias_ref, g_up_bias_ref,
                  res_ref, inv_ref, proj_ref, down_ref, d_second_ref, held_ref, sem):
    rows = 128
    steps = FMB // rows
    blocks = FF // D
    copy = pltpu.make_async_copy(blocks_ref.at[1], held_ref, sem)
    copy.start()
    copy.wait()
    for r in range(0, D, 2 * each):
        pair = [held_ref[r : r + 2 * each, j * D : (j + 1) * D].astype(full) for j in range(blocks)]
        for k in range(2):
            part = jnp.concatenate([p[k * each : (k + 1) * each] for p in pair], 0).astype(low)
            begin = (r + k * each) * blocks
            down_ref[begin : begin + blocks * each, :] = part
    res_ref[...] = plain_dot(hidden_ref[...], down_ref[...])
    for r in range(steps):
        at = slice(r*rows, (r+1)*rows)
        value = first_ref[at, :].astype(full) + res_ref[at, :] + down_bias_ref[...]
        center = value - jnp.mean(value, axis=1, keepdims=True)
        inverse = lax.rsqrt(jnp.mean(center*center, axis=1, keepdims=True) + norm_eps)
        hat = center * inverse
        res_ref[at, :] = hat
        inv_ref[at, :] = inverse
        second_ref[at, :] = (hat * gain_ref[...] + shift_ref[...]).astype(low)
    proj_ref[...] = plain_dot(second_ref[...], final_ref[...].astype(low)) + final_bias_ref[...]
    loss = jnp.zeros((1, 1), full)
    g_final_bias = jnp.zeros((1, PD), full)
    for r in range(steps):
        at = slice(r*rows, (r+1)*rows)
        value = proj_ref[at, :]
        inverse = lax.rsqrt(jnp.sum(value*value, axis=1, keepdims=True) + unit_eps)
        unit = value * inverse
        agreement = sharpness * lax.dot_general(unit, targets_ref[...], (((1,), (1,)), ((), ())), precision=precise, preferred_element_type=full)
        counts = counts_ref[at, :]
        masked = masked_ref[at, :] > 0
        drawn = counts > 0
        own = (lax.broadcasted_iota(jnp.int32, (rows, FMB), 0) + r*rows) == lax.broadcasted_iota(jnp.int32, (rows, FMB), 1)
        highest = jnp.max(jnp.where(drawn, agreement, masked_score), axis=1, keepdims=True)
        weights = counts * jnp.exp(jnp.where(drawn, agreement - highest, 0.0))
        total = jnp.where(masked, jnp.sum(weights, axis=1, keepdims=True), 1.0)
        own_score = jnp.sum(jnp.where(own, agreement, 0.0), axis=1, keepdims=True)
        loss += column_sum(jnp.where(masked, highest + jnp.log(total) - own_score, 0.0))
        d_agreement = jnp.where(masked, weights * (1.0 / total) - jnp.where(own, 1.0, 0.0), 0.0) * (sharpness / NMASK)
        d_unit = jnp.dot(d_agreement, targets_ref[...], precision=precise, preferred_element_type=full)
        d_proj = (inverse * (d_unit - unit * jnp.sum(d_unit*unit, axis=1, keepdims=True))).astype(low)
        d_proj_ref[at, :] = d_proj
        g_final_bias += column_sum(d_proj.astype(full))
    loss_ref[...] = loss * (1.0 / NMASK)
    g_final_bias_ref[...] = g_final_bias
    d_second_ref[...] = right_dot(d_proj_ref[...], final_ref[...].astype(low))
    g_gain = g_shift = g_down_bias = jnp.zeros((1, D), full)
    for r in range(steps):
        at = slice(r*rows, (r+1)*rows)
        grad = d_second_ref[at, :]
        hat = res_ref[at, :]
        g_gain += column_sum(grad * hat)
        g_shift += column_sum(grad)
        grad = grad * gain_ref[...]
        grad = inv_ref[at, :] * (grad - jnp.mean(grad, axis=1, keepdims=True) - hat * jnp.mean(grad*hat, axis=1, keepdims=True))
        d_ffn_ref[at, :] = grad.astype(low)
        g_down_bias += column_sum(grad.astype(low).astype(full))
    g_gain_ref[...] = g_gain
    g_shift_ref[...] = g_shift
    g_down_bias_ref[...] = g_down_bias
    for j in range(blocks):
        part = right_dot(d_ffn_ref[...], down_ref[j*D:(j+1)*D, :]) * slope_ref[:, j*D:(j+1)*D].astype(full)
        part = part.astype(low)
        d_pre_ref[:, j*D:(j+1)*D] = part
        g_up_bias_ref[:, j*D:(j+1)*D] = column_sum(part.astype(full))
def middle(each, hidden, slope, down, first_low, final, down_bias, gain, shift, final_bias, targets, counts, masked):
    def out(shape, dtype): return jax.ShapeDtypeStruct(shape, dtype)
    return pl.pallas_call(functools.partial(middle_kernel, each),
        grid=(1,),
        in_specs=[pl.BlockSpec(memory_space=pltpu.VMEM)] * 2 + [pl.BlockSpec(memory_space=pltpu.HBM)] + [pl.BlockSpec(memory_space=pltpu.VMEM)] * 9,
        out_specs=[pl.BlockSpec(memory_space=pltpu.VMEM)] * 10,
        out_shape=[out((FMB,D),low), out((FMB,PD),low), out((FMB,D),low), out((FMB,FF),low), out((1,1),full),
                   out((1,D),full), out((1,D),full), out((1,D),full), out((1,PD),full), out((1,FF),full)],
        scratch_shapes=[pltpu.VMEM((FMB,D),full), pltpu.VMEM((FMB,1),full), pltpu.VMEM((FMB,PD),full), pltpu.VMEM((FF,D),low), pltpu.VMEM((FMB,D),full), pltpu.VMEM((D,FF),low), pltpu.SemaphoreType.DMA(())],
        compiler_params=pltpu.CompilerParams(vmem_limit_bytes=34*1024*1024),
        cost_estimate=pl.CostEstimate(flops=1, bytes_accessed=1, transcendentals=0),
        name="middle")(hidden, slope, down, first_low, final, down_bias, gain, shift, final_bias, targets, counts, masked)


def normalized(value):
    center = value - jnp.mean(value, axis=1, keepdims=True)
    inverse = lax.rsqrt(jnp.mean(center * center, axis=1, keepdims=True) + norm_eps)
    return center * inverse, inverse


def normalize_back(grad, hat, inverse):
    shift = jnp.mean(grad, axis=1, keepdims=True)
    return inverse * (grad - shift - hat * jnp.mean(grad * hat, axis=1, keepdims=True))


def vector(ref, name):
    start = 0
    for known, size in VECTORS:
        if known == name:
            return ref[:, start : start + size]
        start += size


def row_steps(rows=128):
    return [slice(r, r + rows) for r in range(0, FMB, rows)]


def join_rows(own_ref, got_ref, whole_ref, core, rows, to=slice(None), at=slice(None)):
    for value in range(2):
        @pl.when(core == value)
        def _():
            for r in range(0, own_ref.shape[0], rows):
                for c, ref in enumerate((own_ref, got_ref)):
                    begin = 2 * r + ((value + c) % 2) * rows
                    part = ref[r : r + rows, at].astype(whole_ref.dtype)
                    whole_ref[begin : begin + rows, to] = part


def front_kernel(
    rows, own_ref, got_ref, left_own_ref, left_got_ref, right_own_ref, right_got_ref, masked_ref,
    place_ref,
    inputs_ref, normed_ref, hat_ref, slope_ref, inverse_ref, taps_ref, proj_ref, vec_ref,
    final_ref, parts_ref, total_ref,
):
    core, section = place_ref[0, 0], place_ref[0, 1]
    half = C // 2
    join_rows(right_own_ref, right_got_ref, taps_ref, core, 2 * rows)
    join_rows(left_own_ref, left_got_ref, proj_ref, core, rows, at=slice(0, D))
    more = slice(D, D + PD + SPARE)
    join_rows(left_own_ref, left_got_ref, parts_ref, core, rows, at=more)
    spread_parts(rows, parts_ref, vec_ref)
    for d in range(C // rows):
        at = slice(d * rows, (d + 1) * rows)
        head, tail = parts_ref[at, :PD], parts_ref[d * rows : d * rows + rows // 2, PD:]
        to = d * (rows + rows // 2)
        final_ref[to : to + rows, :] = head.astype(full)
        final_ref[to + rows : to + rows + rows // 2, :] = tail.astype(full)
    for tap in range(2):
        cols = slice(tap * half, (tap + 1) * half)
        own_taps = taps_ref[pl.ds(pl.multiple_of(tap * C + section * half, half), half), :]
        got_taps = taps_ref[pl.ds(pl.multiple_of(tap * C + (1 - section) * half, half), half), :]
        part = plain_dot(own_ref[:, cols], own_taps) + plain_dot(got_ref[:, cols], got_taps)
        if tap == 0:
            total_ref[...] = part
        else:
            total_ref[...] += part
    for at in row_steps():
        lifted, slope = gelu_and_slope(total_ref[at, :])
        hat, inverse = normalized(lifted)
        slope_ref[at, :] = slope.astype(low)
        hat_ref[at, :] = hat.astype(low)
        inverse_ref[at, :] = inverse
        normed = hat * vector(vec_ref, "ln0_gain") + vector(vec_ref, "ln0_bias")
        normed_ref[at, :] = normed.astype(low)
    for at in row_steps():
        encoded = plain_dot(normed_ref[at, :], proj_ref[...]) + vector(vec_ref, "proj0_bias")
        encoded = jnp.where(masked_ref[at, :] > 0, vector(vec_ref, "mask_emb"), encoded)
        inputs_ref[at, :] = encoded.astype(low)


def first_kernel(
    inputs_ref, mixed_ref, out_ref, vec_ref, first_ref, hat_ref, inverse_ref, total_ref
):
    total_ref[...] = plain_dot(mixed_ref[...], out_ref[:, D:])
    for at in row_steps():
        value = inputs_ref[at, :].astype(full) + total_ref[at, :] + vector(vec_ref, "out_bias")
        hat, inverse = normalized(value)
        hat_ref[at, :] = hat.astype(low)
        inverse_ref[at, :] = inverse
        value = hat * vector(vec_ref, "ln1_gain") + vector(vec_ref, "ln1_bias")
        first_ref[at, :] = value.astype(low)


def first_back_kernel(
    d_pre_ref, up_ref, d_ffn_ref, hat_ref, inverse_ref, out_ref, vec_ref,
    d_attn_ref, d_mixed_ref, g_gain_ref, g_shift_ref, g_out_bias_ref, d_first_ref, held_ref, sems,
):
    part = right_dot(d_pre_ref[...], fetched(up_ref, held_ref, sems))

    @pl.when(pl.program_id(0) == 0)
    def _():
        d_first_ref[...] = d_ffn_ref[...].astype(full) + part

    @pl.when(pl.program_id(0) > 0)
    def _():
        d_first_ref[...] += part

    @pl.when(pl.program_id(0) == pl.num_programs(0) - 1)
    def _():
        g_gain = g_shift = g_out_bias = jnp.zeros((1, D), full)
        for at in row_steps():
            grad = d_first_ref[at, :]
            hat = hat_ref[at, :].astype(full)
            g_gain += column_sum(grad * hat)
            g_shift += column_sum(grad)
            grad = normalize_back(grad * vector(vec_ref, "ln1_gain"), hat, inverse_ref[at, :])
            grad = grad.astype(low)
            d_attn_ref[at, :] = grad
            g_out_bias += column_sum(grad.astype(full))
        g_gain_ref[...] = g_gain
        g_shift_ref[...] = g_shift
        g_out_bias_ref[...] = g_out_bias
        d_mixed_ref[...] = right_dot(d_attn_ref[...], out_ref[:, D:]).astype(low)


def first_backward(d_pre, ffn, d_ffn, hat, inverse, vo, vectors):
    def held(*shape):
        return pl.BlockSpec(shape, lambda i: (0, 0))

    return pl.pallas_call(
        first_back_kernel,
        grid=(FF // D,),
        in_specs=[
            pl.BlockSpec((FMB, D), lambda i: (0, i)),
            pl.BlockSpec(memory_space=pltpu.HBM),
            held(FMB, D),
            held(FMB, D),
            held(FMB, 1),
            held(D, 2 * D),
            held(1, VECTOR_TOTAL),
        ],
        out_specs=[held(FMB, D)] * 2 + [held(1, D)] * 3,
        out_shape=[jax.ShapeDtypeStruct((FMB, D), low)] * 2
        + [jax.ShapeDtypeStruct((1, D), full)] * 3,
        scratch_shapes=[
            pltpu.VMEM((FMB, D), full),
            pltpu.VMEM((FF // D, D, D), low),
            pltpu.SemaphoreType.DMA((FF // D,)),
        ],
        compiler_params=pltpu.CompilerParams(vmem_limit_bytes=28 * 1024 * 1024),
        cost_estimate=pl.CostEstimate(flops=1, bytes_accessed=1, transcendentals=0),
        name="first_backward",
    )(d_pre, ffn, d_ffn, hat, inverse, vo, vectors)


def inputs_back_kernel(
    d_qk_ref, d_values_ref, qk_ref, v_ref, d_attn_ref, masked_ref,
    d_encoded_ref, g_mask_ref, g_proj_bias_ref, g_query_ref, g_value_ref, total_ref,
):
    total_ref[...] = right_dot(d_qk_ref[...], qk_ref[...])
    total_ref[...] += right_dot(d_values_ref[...], v_ref[:, :D])
    g_mask = g_proj_bias = g_query = g_value = jnp.zeros((1, D), full)
    for at in row_steps():
        grad = total_ref[at, :] + d_attn_ref[at, :].astype(full)
        masked = masked_ref[at, :] > 0
        g_mask += column_sum(jnp.where(masked, grad, 0.0))
        grad = jnp.where(masked, 0.0, grad).astype(low)
        d_encoded_ref[at, :] = grad
        g_proj_bias += column_sum(grad.astype(full))
        g_query += column_sum(d_qk_ref[at, :D].astype(full))
        g_value += column_sum(d_values_ref[at, :].astype(full))
    g_mask_ref[...] = g_mask
    g_proj_bias_ref[...] = g_proj_bias
    g_query_ref[...] = g_query
    g_value_ref[...] = g_value


def front_back_kernel(
    d_encoded_ref, proj_ref, hat_ref, slope_ref, inverse_ref, vec_ref,
    d_conv_ref, g_gain_ref, g_shift_ref, total_ref,
):
    total_ref[...] = right_dot(d_encoded_ref[...], proj_ref[...])
    g_gain = g_shift = jnp.zeros((1, C), full)
    for at in row_steps():
        grad = total_ref[at, :]
        hat = hat_ref[at, :].astype(full)
        g_gain += column_sum(grad * hat)
        g_shift += column_sum(grad)
        grad = normalize_back(grad * vector(vec_ref, "ln0_gain"), hat, inverse_ref[at, :])
        d_conv_ref[at, :] = (grad * slope_ref[at, :].astype(full)).astype(low)
    g_gain_ref[...] = g_gain
    g_shift_ref[...] = g_shift


def each_pair(rows, each):
    step = 2 * each if rows % (2 * each) == 0 else each
    return [(slice(r, r + step), slice(2 * r, 2 * r + 2 * step)) for r in range(0, rows, step)]


def join_cores(own_ref, got_ref, whole_ref, core, each, width=512):
    cols = own_ref.shape[1]
    for c in range(0, cols, width):
        at = slice(c, min(c + width, cols))
        for lane, whole in each_pair(own_ref.shape[0], each):
            own, got = own_ref[lane, at].astype(full), got_ref[lane, at].astype(full)
            zero = jnp.where(core == 0, own, got)
            one = jnp.where(core == 0, got, own)
            parts = []
            for r in range(0, own.shape[0], each):
                parts += [zero[r : r + each], one[r : r + each]]
            whole_ref[whole, at] = jnp.concatenate(parts, 0).astype(low)


def split_cores(whole_ref, keep_ref, send_ref, core, each, begin=0, width=384):
    cols = whole_ref.shape[1]
    for c in range(0, cols, width):
        at = slice(c, min(c + width, cols))
        to = slice(begin + at.start, begin + at.stop)
        for lane, whole in each_pair(whole_ref.shape[0] // 2, each):
            zero, one = [], []
            for r in range(whole.start, whole.stop, 2 * each):
                zero.append(whole_ref[r : r + each, at])
                one.append(whole_ref[r + each : r + 2 * each, at])
            zero, one = jnp.concatenate(zero, 0), jnp.concatenate(one, 0)
            keep_ref[lane, to] = jnp.where(core == 0, zero, one).astype(low)
            send_ref[lane, to] = jnp.where(core == 0, one, zero).astype(low)


def qkv_kernel(
    each, inputs_ref, qk_own_ref, qk_got_ref, vo_own_ref, vo_got_ref, vec_ref, core_ref,
    qk_ref, vo_ref, qk_rows_ref, values_ref,
):
    core = core_ref[0, 0]
    join_cores(qk_own_ref, qk_got_ref, qk_ref, core, each)
    join_cores(vo_own_ref, vo_got_ref, vo_ref, core, each)
    bias = vector(vec_ref, "qv_bias")
    rows = plain_dot(inputs_ref[...], qk_ref[:, :D]) + bias[:, :D]
    qk_rows_ref[:, :D] = rows.astype(low)
    qk_rows_ref[:, D:] = plain_dot(inputs_ref[...], qk_ref[:, D:]).astype(low)
    rows = plain_dot(inputs_ref[...], vo_ref[:, :D]) + bias[:, D:]
    values_ref[...] = rows.astype(low)


def lanes_kernel(each, up_ref, up_got_ref, down_ref, down_got_ref, out_ref):
    out_ref[0, 0, 0, :each, :] = added(up_ref[0], up_got_ref[0])
    for j in range(FF // D):
        rows = slice(j * each, (j + 1) * each)
        part = added(down_ref[0, rows, :], down_got_ref[0, rows, :])
        out_ref[0, 0, 0, each:, j * D : (j + 1) * D] = part


def add_lanes(each, depth, up, up_got, down, down_got):
    def where(i):
        return (i // (2 * depth), i % 2, (i // 2) % depth, 0, 0)

    up_rows = pl.BlockSpec((1, each, FF), lambda i: (i, 0, 0))
    down_rows = pl.BlockSpec((1, each * FF // D, D), lambda i: (i, 0, 0))
    up, up_got = [t.reshape(4 * depth, each, FF) for t in (up, up_got)]
    down, down_got = [t.reshape(4 * depth, each * FF // D, D) for t in (down, down_got)]
    return pl.pallas_call(
        functools.partial(lanes_kernel, each),
        grid=(4 * depth,),
        in_specs=[up_rows, up_rows, down_rows, down_rows],
        out_specs=pl.BlockSpec((1, 1, 1, 2 * each, FF), where),
        out_shape=jax.ShapeDtypeStruct((2, 2, depth, 2 * each, FF), low),
        compiler_params=pltpu.CompilerParams(vmem_limit_bytes=8 * 1024 * 1024),
        cost_estimate=pl.CostEstimate(flops=1, bytes_accessed=1, transcendentals=0),
        name="add_lanes",
    )(up, up_got, down, down_got)


def heads_grad_kernel(
    each, inputs_ref, mixed_ref, d_qk_ref, d_values_ref, d_attn_ref, core_ref,
    keep_ref, send_ref, turned_ref, total_ref,
):
    core = core_ref[0, 0]
    turned_ref[...] = inputs_ref[...].T
    for begin, rhs in (
        (0, d_qk_ref[:, :D]),
        (D, d_qk_ref[:, D:]),
        (2 * D, d_values_ref[...]),
        (3 * D, d_attn_ref[...]),
    ):
        if begin == 3 * D:
            turned_ref[...] = mixed_ref[...].T
        total_ref[...] = plain_dot(turned_ref[...], rhs)
        split_cores(total_ref, keep_ref, send_ref, core, each, begin)


def misc_grad_kernel(
    rows, each, normed_ref, d_encoded_ref, second_ref, d_proj_ref, own_ref, got_ref, d_conv_ref,
    vectors_ref, section_ref, terms_ref, final_ref, taps_ref,
):
    section = section_ref[0, 0]
    half = C // 2
    terms_ref[:, :D] = plain_dot(normed_ref[...].T, d_encoded_ref[...]).astype(low)
    final_ref[...] = plain_dot(second_ref[...].T, d_proj_ref[...])
    for d in range(C // rows):
        to = slice(d * rows, d * rows + rows)
        terms_ref[to, D : D + PD] = final_ref[d * each : d * each + rows, :].astype(low)
        last = [final_ref[d * each + rows : (d + 1) * each, :]]
        last.append(vectors_ref[d * (rows // 2) : (d + 1) * (rows // 2), :])
        terms_ref[to, D + PD : D + PD + SPARE] = jnp.concatenate(last, 0).astype(low)
    taps_ref[:C, :] = plain_dot(own_ref[...].T, d_conv_ref[...])
    taps_ref[C:, :] = plain_dot(got_ref[...].T, d_conv_ref[...])
    for tap in range(2):
        for side in range(2):
            for r in range(0, half, 2 * rows):
                at = tap * half + r
                own, got = taps_ref[at : at + 2 * rows, :], taps_ref[C + at : C + at + 2 * rows, :]
                value = jnp.where(section == side, own, got).astype(low)
                d = (tap * C + side * half + r) // (2 * rows)
                begin = D + PD + SPARE
                terms_ref[d * rows : (d + 1) * rows, begin : begin + C] = value[:rows]
                terms_ref[d * rows : (d + 1) * rows, begin + C :] = value[rows:]


def local_kernel(kernel, outs, scratch=(), scalars=0, static=(), far_in=(), far_out=()):
    def call(*args):
        near = len(args) - scalars
        held = [(args[i].shape, args[i].dtype) for i in far_in] + [outs[i] for i in far_out]
        first_held = len(args) + len(outs) + len(scratch)

        def run(*refs):
            refs, held_refs, sems = list(refs[:first_held]), refs[first_held:-2], refs[-2:]
            ins = [
                pltpu.make_async_copy(refs[i], held_refs[k], sems[0].at[k])
                for k, i in enumerate(far_in)
            ]
            ends = [
                pltpu.make_async_copy(
                    held_refs[len(far_in) + k], refs[len(args) + i], sems[1].at[k]
                )
                for k, i in enumerate(far_out)
            ]
            for copy in ins:
                copy.start()
            for copy in ins:
                copy.wait()
            for k, i in enumerate(list(far_in) + [len(args) + i for i in far_out]):
                refs[i] = held_refs[k]
            kernel(*static, *refs)
            for copy in ends:
                copy.start()
            for copy in ends:
                copy.wait()

        def space(index, far):
            return pl.BlockSpec(memory_space=pltpu.HBM if index in far else pltpu.VMEM)

        everything = [(a.shape, a.dtype) for a in args] + list(outs) + list(scratch)
        size = sum(math.prod(shape) * jnp.dtype(dtype).itemsize for shape, dtype in everything)
        return pl.pallas_call(
            run,
            out_shape=[jax.ShapeDtypeStruct(shape, dtype) for shape, dtype in outs],
            in_specs=[space(i, far_in) for i in range(near)]
            + [pl.BlockSpec(memory_space=pltpu.SMEM)] * scalars,
            out_specs=[space(i, far_out) for i in range(len(outs))],
            scratch_shapes=[pltpu.VMEM(shape, dtype) for shape, dtype in list(scratch) + held]
            + [pltpu.SemaphoreType.DMA((max(len(far), 1),)) for far in (far_in, far_out)],
            compiler_params=pltpu.CompilerParams(vmem_limit_bytes=56 * 1024 * 1024 if kernel.__name__ in ('front_kernel',) else size + 4 * 1024 * 1024),
            cost_estimate=pl.CostEstimate(flops=1, bytes_accessed=1, transcendentals=0),
            name=kernel.__name__,
        )(*args)

    return call


def fetched(ffn_ref, held_ref, sems):
    step, width = pl.program_id(0), held_ref.shape[2]

    def copy(k):
        source = ffn_ref.at[0, :, k * width : (k + 1) * width]
        return pltpu.make_async_copy(source, held_ref.at[k], sems.at[k])

    for k in range(held_ref.shape[0]):
        @pl.when(step == 0)
        def _():
            copy(k).start()

    for k in range(held_ref.shape[0]):
        @pl.when(step == k)
        def _():
            copy(k).wait()

    return held_ref[step]


def up_kernel(x_ref, ffn_ref, bias_ref, hidden_ref, slope_ref, pre_ref, held_ref, sems):
    pre_ref[...] = plain_dot(x_ref[...], fetched(ffn_ref, held_ref, sems))
    bias = bias_ref[...]
    rows = 32

    def step(r, carry):
        at = pl.ds(pl.multiple_of(r * rows, rows), rows)
        value, slope = gelu_and_slope(pre_ref[at, :] + bias)
        hidden_ref[at, :] = value.astype(low)
        slope_ref[at, :] = slope.astype(low)
        return carry

    lax.fori_loop(0, FMB // rows, step, 0)


def up_forward(x, ffn, vectors, tile=1024):
    begin = start_of["up_bias"] // tile
    columns = pl.BlockSpec((FMB, tile), lambda i: (0, i))
    return pl.pallas_call(
        up_kernel,
        grid=(FF // tile,),
        in_specs=[
            pl.BlockSpec((FMB, D), lambda i: (0, 0)),
            pl.BlockSpec(memory_space=pltpu.HBM),
            pl.BlockSpec((1, tile), lambda i: (0, begin + i)),
        ],
        out_specs=[columns, columns],
        out_shape=[jax.ShapeDtypeStruct((FMB, FF), low)] * 2,
        scratch_shapes=[
            pltpu.VMEM((FMB, tile), full),
            pltpu.VMEM((FF // tile, D, tile), low),
            pltpu.SemaphoreType.DMA((FF // tile,)),
        ],
        compiler_params=pltpu.CompilerParams(vmem_limit_bytes=22 * 1024 * 1024),
        cost_estimate=pl.CostEstimate(flops=1, bytes_accessed=1, transcendentals=0),
        name="up_forward",
    )(x, ffn, vectors)


def body(
    features,
    conv_weight,
    ln0_gain,
    ln0_bias,
    proj0_weight,
    proj0_bias,
    mask_emb,
    qkv_weight,
    qv_bias,
    out_weight,
    out_bias,
    ln1_gain,
    ln1_bias,
    up_weight,
    up_bias,
    down_weight,
    down_bias,
    ln2_gain,
    ln2_bias,
    final_weight,
    final_bias,
    codebook,
    lengths,
    mask_pos,
    distractors,
    target_ids,
):
    links = Links()
    section = links.y
    core = links.core.reshape(1, 1).astype(jnp.int32)
    place = jnp.stack([links.core, links.y]).reshape(1, 2).astype(jnp.int32)
    devices = 2 * links.per_section
    rows = C // devices

    own_rows = pick(features, section, 0)
    lens = pick(lengths, section, 0)
    positions = pick(mask_pos, section, 0)
    chosen = pick(distractors, section, 0)
    target_rows = pick(target_ids, section, 0)

    each = D // devices
    slot = (rows // 2) * SPARE // SLOTS
    blocks = FF // D
    down_blocks = down_weight.reshape(blocks, each, D).transpose(1, 0, 2).reshape(each, FF)
    ffn_full = lax.all_gather(jnp.stack([up_weight, down_blocks]), BOTH, axis=1, tiled=True)
    heads = Gather(links, jnp.concatenate([qkv_weight, out_weight], axis=1), 2 * D)
    heads.start_z()
    got_rows = links.over_y(pick(features, 1 - section, 0))
    late = (up_bias, proj0_weight, chosen)
    late = after([heads], *late)
    up_bias, proj0_weight, chosen = late
    heads.start_z_rest()
    vector_parts = [
        up_bias,
        ln0_gain,
        ln0_bias,
        proj0_bias,
        mask_emb,
        qv_bias,
        out_bias,
        ln1_gain,
        ln1_bias,
        down_bias,
        ln2_gain,
        ln2_bias,
        final_bias,
    ]
    vector_parts += [vector_parts[0]] * (SLOTS - len(vector_parts))
    vector_part = jnp.stack([jnp.pad(v, (0, slot - v.shape[0])) for v in vector_parts])
    misc = Gather(
        links,
        jnp.concatenate(
            [
                proj0_weight,
                final_weight[:rows],
                jnp.concatenate([final_weight[rows:], vector_part.reshape(rows // 2, SPARE)], 0),
                conv_weight[:rows],
                conv_weight[rows:],
            ],
            axis=1,
        ),
        D + PD + SPARE,
        parts=2,
    )
    misc.start_z()
    drawn = count_distractors(chosen)
    (drawn,) = after([heads, misc], drawn)

    heads.start_first()
    misc.start_z_rest()
    frame_ids = jnp.arange(FMB, dtype=jnp.int32)
    at_frame = positions[:, None] == frame_ids[None, :]
    is_masked = jnp.any(at_frame, axis=0)
    own_frame = (frame_ids[:, None] == frame_ids[None, :]) & is_masked[:, None]
    counts = lax.dot_general(
        at_frame.astype(low), drawn, (((0,), (1,)), ((), ())), preferred_element_type=full
    ) + own_frame.astype(full)
    entries = jnp.arange(codebook.shape[1], dtype=jnp.int32)
    targets = jnp.concatenate(
        [
            plain_dot((target_rows[0][:, None] == entries[None, :]).astype(low), codebook[0]),
            plain_dot((target_rows[1][:, None] == entries[None, :]).astype(low), codebook[1]),
        ],
        axis=1,
    )
    targets = targets * lax.rsqrt(jnp.sum(targets * targets, axis=1, keepdims=True) + unit_eps)
    stops = jnp.cumsum(lens)
    segment = jnp.sum(
        (frame_ids[:, None] >= stops[None, : UTTS - 1]).astype(jnp.int32), axis=1
    )
    masked = is_masked[:, None].astype(full)
    own_pairs = own_rows.reshape(FMB, C)
    counts, targets, got_rows, own_pairs, segment = after(
        [heads, misc], counts, targets, got_rows, own_pairs, segment
    )

    heads.start_second()
    misc.start_first()
    got_pairs = got_rows.reshape(FMB, C)
    (got_pairs,) = after([heads, misc], got_pairs)

    misc.start_second()
    heads.start_core()
    (got_pairs,) = after([misc, heads], got_pairs)

    misc.start_core()
    (got_pairs,) = after([misc], got_pairs)
    half = C // 2
    (
        inputs, normed, hat_zero, conv_slope, inverse_zero, conv_full, proj_full, vectors, final_full
    ) = local_kernel(
        front_kernel,
        [
            ((FMB, D), low),
            ((FMB, C), low),
            ((FMB, C), low),
            ((FMB, C), low),
            ((FMB, 1), full),
            ((2 * C, C), low),
            ((C, D), low),
            ((1, VECTOR_TOTAL), full),
            ((D, PD), full),
        ],
        [((C, PD + SPARE), low), ((FMB, C), full)],
        scalars=1,
        static=(rows,),
        far_in=(0, 1),
        far_out=(1, 2, 3, 4, 5, 6, 8),
    )(own_pairs, got_pairs, *misc.apart(), masked, place)
    taps = conv_full.reshape(2, 2, half, C)
    own_taps = pick(taps, section, 1).reshape(C, C)
    got_taps = pick(taps, 1 - section, 1).reshape(C, C)
    qk_full, vo_full, qk_rows, value_rows = local_kernel(
        qkv_kernel,
        [((D, 2 * D), low), ((D, 2 * D), low), ((FMB, 2 * D), low), ((FMB, D), low)],
        scalars=1,
        static=(each,),
        far_out=(0,),
    )(inputs, *heads.apart(), vectors, core)
    mixed, logs = attention_forward(qk_rows, value_rows, segment)
    first_low, hat_one, inverse_one = local_kernel(
        first_kernel, [((FMB, D), low), ((FMB, D), low), ((FMB, 1), full)], [((FMB, D), full)],
        far_out=(1, 2),
    )(inputs, mixed, vo_full, vectors)
    hidden_low, slope = up_forward(first_low, ffn_full, vectors)
    grad = {}
    (
        second_low,
        d_proj_low,
        d_ffn_low,
        d_pre_low,
        loss,
        grad["down_bias"],
        grad["ln2_gain"],
        grad["ln2_bias"],
        grad["final_bias"],
        grad["up_bias"],
    ) = middle(
        each,
        hidden_low,
        slope,
        ffn_full,
        first_low,
        final_full,
        *[
            vectors[:, start_of[name] : start_of[name] + size]
            for name, size in VECTORS
            if name in ("down_bias", "ln2_gain", "ln2_bias", "final_bias")
        ],
        targets,
        counts,
        masked,
    )

    loss = jnp.where(jnp.arange(2) == section, loss[0], 0.0)
    loss_got = links.over_y(loss)
    g_down = left_dot(hidden_low, d_ffn_low).astype(low)
    down = Sum(links, *by_core(links, g_down), D // 2)
    down.start_core()
    g_up = left_dot(first_low, d_pre_low).astype(low)
    up = Sum(links, *by_core(links, g_up), FF // 2)
    up.start_core()
    d_attn_low, d_mixed, grad["ln1_gain"], grad["ln1_bias"], grad["out_bias"] = (
        first_backward(d_pre_low, ffn_full, d_ffn_low, hat_one, inverse_one, vo_full, vectors)
    )
    d_mixed, d_attn_low, loss_got = after([down, up], d_mixed, d_attn_low, loss_got)

    lanes = add_lanes(
        each, links.depth, up.keep.reshape(-1, FF), up.got[0], down.keep.reshape(-1, D), down.got[0]
    )
    line = lax.psum_scatter(
        lanes.reshape(-1, FF), ("section", "x"), scatter_dimension=0, tiled=True
    ).reshape(links.depth, 2 * each, FF)
    d_qk, d_values = attention_backward(qk_rows, value_rows, segment, d_mixed, logs)
    keep, send = local_kernel(
        heads_grad_kernel,
        [((D // 2, 4 * D), low)] * 2,
        [((D, FMB), low), ((D, D), full)],
        scalars=1,
        static=(each,),
        far_in=(0, 1),
    )(inputs, mixed, d_qk, d_values, d_attn_low, core)

    heads = Sum(links, keep, send, 2 * D)
    heads.start_core()
    d_encoded, grad["mask_emb"], grad["proj0_bias"], g_query, g_value = local_kernel(
        inputs_back_kernel, [((FMB, D), low)] + [((1, D), full)] * 4, [((FMB, D), full)], far_in=(2, 3)
    )(d_qk, d_values, qk_full, vo_full, d_attn_low, masked)
    grad["qv_bias"] = jnp.concatenate([g_query, g_value], axis=1)
    (d_encoded,) = after([heads], d_encoded)

    heads.start_first()
    d_conv_low, grad["ln0_gain"], grad["ln0_bias"] = local_kernel(
        front_back_kernel,
        [((FMB, C), low), ((1, C), full), ((1, C), full)],
        [((FMB, C), full)],
        far_in=(1, 2, 3, 4),
    )(d_encoded, proj_full, hat_zero, conv_slope, inverse_zero, vectors)
    g_vectors = split_vectors([grad[name] for name, _ in VECTORS], devices, slot)
    g_vectors = g_vectors.transpose(1, 0, 2).reshape(devices * (rows // 2), SPARE)
    (terms,) = local_kernel(
        misc_grad_kernel,
        [((C, D + PD + SPARE + 2 * C), low)],
        [((D, PD), full), ((2 * C, C), full)],
        scalars=1,
        static=(rows, each),
        far_in=(0, 2, 3, 4, 5),
    )(
        normed, d_encoded, second_low, d_proj_low, own_pairs, got_pairs, d_conv_low, g_vectors,
        section.reshape(1, 1).astype(jnp.int32),
    )
    misc = Sum(links, *by_core(links, terms), D + PD + SPARE)
    misc.start_core()
    got_d = right_dot(d_conv_low, got_taps).astype(low).reshape(2 * FMB, half)
    own_d = right_dot(d_conv_low, own_taps).reshape(2 * FMB, half)
    own_d, got_d, line = after([misc, heads], own_d, got_d, line)

    heads.start_second()
    misc.start_first()
    ffn = Line(links, line)
    ffn.start_z()
    (got_d,) = after([heads, misc], got_d)

    heads.start_z()
    misc.start_second()
    ffn.start_z_rest()
    (got_d,) = after([heads, misc], got_d)

    heads.start_z_rest()
    misc.start_z()
    got_d = links.over_y(got_d)
    after([misc])
    misc.start_z_rest()
    features_grad = in_order(section, own_d, got_d.astype(full), -2)
    loss_each = loss + loss_got
    ffn_sum, heads_sum, misc_sum = ffn.total(), heads.total(), misc.total()
    up_sum = ffn_sum[:each]
    down_sum = jnp.concatenate(jnp.split(ffn_sum[each:], blocks, axis=1), axis=0)
    qkv_sum, out_sum = heads_sum[:, : 3 * D], heads_sum[:, 3 * D :]
    proj_sum = misc_sum[:, :D]
    left, right = misc_sum[:, D : D + PD + SPARE], misc_sum[:, D + PD + SPARE :]
    conv_sum = jnp.concatenate([right[:, :C], right[:, C:]], axis=0)
    final_sum = jnp.concatenate([left[:, :PD], left[: rows // 2, PD:]], axis=0)
    vector_sum = left[rows // 2 :, PD:].reshape(SLOTS, slot)
    share = {}
    for index, (name, size) in enumerate(VECTORS):
        share[name] = vector_sum[index, : size // devices]
    return (
        loss_each,
        features_grad,
        conv_sum,
        share["ln0_gain"],
        share["ln0_bias"],
        proj_sum,
        share["proj0_bias"],
        share["mask_emb"],
        qkv_sum,
        share["qv_bias"],
        out_sum,
        share["out_bias"],
        share["ln1_gain"],
        share["ln1_bias"],
        up_sum,
        share["up_bias"],
        down_sum,
        share["down_bias"],
        share["ln2_gain"],
        share["ln2_bias"],
        final_sum,
        share["final_bias"],
    )


def solution(mesh):
    grid = mesh.devices.reshape(2, -1, 2, 2)
    rows = P(BOTH, None)
    part = P(BOTH)
    weights = (rows, part, part, rows, part, part, rows, part, rows, part, part, part)
    weights += (rows, part, rows, part, part, part, rows, part)
    batch = [P(SPLIT, *[None] * more) for more in (1, 1, 2, 2)]
    return jax.shard_map(
        body,
        mesh=jax.sharding.Mesh(grid, BOTH),
        in_specs=(P(SPLIT, None, "section"),) + weights + (P(), *batch),
        out_specs=(P(SPLIT), P(SPLIT, None, "section")) + weights,
        check_vma=False,
    )
```

time: 535 us -> 315 us (0.59)
  matrix products: 160 us -> 11.9 us
  Pallas kernels: 7.11 us -> 89.2 us
  waiting for transfers between devices: 116 us -> 66.7 us
  other arithmetic: 70.4 us -> 21.5 us
  starting transfers between devices: 86.5 us -> 51.4 us
  local copies, waits for them, and re-layouts: 83.9 us -> 53.7 us
  between operations: 3.76 us -> 16.1 us
    pallas_call x0 -> x14, Pallas kernels: none -> 82.1 us  [the longest x7 23.6 us: call(): pl.pallas_call(run, out_shape=[jax.ShapeDtypeStruct(shape, dtype) for sha...]
    dot_general x12 -> x2, matrix products: 59.4 us -> 0.62 us  [plain_dot(): return jnp.dot(left_side, right_side, preferred_element_type=full)]
    ppermute x67 -> x37, waiting for transfers between devices: 116 us -> 66.6 us  [move(): return lax.ppermute(value, BOTH, pairs)]
    dot_general x9 -> x2, matrix products: 41.4 us -> 3.82 us  [right_dot(): lax.dot_general(left_side, right_side, (((1,), (1,)), ((), ())), preferre...]
    ppermute x67 -> x37, starting transfers between devices: 86.5 us -> 51.3 us  [move(): return lax.ppermute(value, BOTH, pairs)]
    dot_general x7 -> x1, matrix products: 28.8 us -> 1.42 us  [body(): lax.dot_general(at_frame.astype(low), drawn, (((0,), (1,)), ((), ())), pr...]
    convert_element_type x21 -> x1, local copies, waits for them, and re-layouts: 18.3 us -> 0.86 us  [body(): masked = is_masked[:, None].astype(full)]
    select_n x29 -> x14, other arithmetic: 23.1 us -> 6.81 us  [the longest x11 5.79 us: in_order(): jnp.where(lax.broadcasted_iota(jnp.int32, shape, axis) == index, own, got)]
  transfers between devices with their start and end apart: 67 -> 39, of which waited for: 30 -> 16; matrix products, arithmetic and copies ran while one was open for 34% -> 17% of each run, Pallas kernels for 1% -> 20%
where the time goes in v2:
time: 315 us; the launch traced here: 311 us
  Pallas kernels  89.2 us (28%)
  waiting for transfers between devices  66.7 us (21%)
  local copies, waits for them, and re-layouts  53.7 us (17%)
  starting transfers between devices  51.4 us (16%)
  other arithmetic  21.5 us (7%)
  between operations  16.1 us (5%)
  matrix products  11.9 us (4%)
    ppermute x37, waiting for transfers between devices, move(): return lax.ppermute(value, BOTH, pairs)  66.6 us
    ppermute x37, starting transfers between devices, move(): return lax.ppermute(value, BOTH, pairs)  51.3 us
    unnamed x178, local copies, waits for them, and re-layouts  28.4 us
    pallas_call x7, Pallas kernels, call(): pl.pallas_call(run, out_shape=[jax.ShapeDtypeStruct(shape, dtype) for sha...  23.6 us
    pallas_call x1, Pallas kernels, middle(): pl.pallas_call(functools.partial(middle_kernel, each), grid=(1,), in_spec...  15.7 us
    pallas_call x1, Pallas kernels, attention_backward(): pl.pallas_call(attention_back_kernel, grid=(pairs,), in_specs=[pl.BlockSp...  14.2 us
    pallas_call x1, Pallas kernels, up_forward(): pl.pallas_call(up_kernel, grid=(FF // tile,), in_specs=[pl.BlockSpec((FMB...  10.2 us
    pallas_call x1, Pallas kernels, attention_forward(): pl.pallas_call(attention_kernel, grid=(pairs,), in_specs=[pl.BlockSpec((F...  8.23 us
  transfers between devices with their start and end apart: 39, of which 16 were waited for; matrix products, arithmetic and copies ran while one was open for 17% of the time, Pallas kernels for 20%

profile of v2, /device:TPU:0, one launch (start us, length us, event | category | flops | bytes accessed | tf_op | source)
XLA Modules:
  0.0 310.5 jit_solution(13174501034417803956)
XLA Ops:
  8.5 1.7 pad_maximum_fusion.2
  12.0 5.0 %collective-permute-start = (bf16[24,3072]{1,0:T(8,128)(2,1)S(1)}, bf16[24,3072]{1,0:T(8,128)(2,1)S(1)}, u32[]{:S(2)}, u32[]{:S(2)}) collective-permute-start(bf16[24,3072]{1,0:T(8,128)(2,1)S(1)} %constant_dynamic-update-slice_fusion), channel_id=1, source_target_pairs={{0,12},{1,13},{2,14},{3,15},{4,8},{5,9},{6,10},{7,11},{8,4},{9,5},... | collective-permute-start | bytes 442376 | tf_op jit(solution)/shard_map/ppermute | solution.py:110
  17.1 1.6 collective-permute-start.6
  24.1 2.5 collective-permute-start.2
  26.6 7.1 %shard_map.417 = bf16[512,256]{1,0:T(8,128)(2,1)} custom-call(s32[100,256]{1,0:T(8,128)} %bitcast.272), custom_call_target="tpu_custom_call" | custom-call | flops 1 | bytes 1 | tf_op jit(solution)/shard_map/pallas_call | solution.py:399
  33.8 5.1 %collective-permute-done.2 = bf16[16,2304]{1,0:T(8,128)(2,1)S(1)} collective-permute-done((bf16[16,2304]{1,0:T(8,128)(2,1)S(1)}, bf16[16,2304]{1,0:T(8,128)(2,1)S(1)}, u32[]{:S(2)}, u32[]{:S(2)}) %collective-permute-start.2) | collective-permute-done | bytes 73760 | tf_op jit(solution)/shard_map/ppermute | solution.py:110
  39.7 1.6 collective-permute-start.3
  42.5 1.4 convolution_add_fusion.counts_ref
  44.0 9.1 %collective-permute-done.5 = bf16[2,16,2304]{2,1,0:T(8,128)(2,1)S(1)} collective-permute-done((bf16[2,16,2304]{2,1,0:T(8,128)(2,1)S(1)}, bf16[2,16,2304]{2,1,0:T(8,128)(2,1)S(1)}, u32[]{:S(2)}, u32[]{:S(2)}) %collective-permute-start.5) | collective-permute-done | bytes 147488 | tf_op jit(solution)/shard_map/ppermute | solution.py:110
  54.0 1.7 collective-permute-start.8
  57.2 1.5 collective-permute-start.10
  59.7 9.4 %collective-permute-done.10 = bf16[4,32,512]{2,1,0:T(8,128)(2,1)S(1)} collective-permute-done((bf16[4,32,512]{2,1,0:T(8,128)(2,1)S(1)}, bf16[4,32,512]{2,1,0:T(8,128)(2,1)S(1)}, u32[]{:S(2)}, u32[]{:S(2)}) %collective-permute-start.10) | collective-permute-done | bytes 131104 | tf_op jit(solution)/shard_map/ppermute | solution.py:110
  69.1 3.6 %collective-permute-done.9 = bf16[4,16,1280]{2,1,0:T(8,128)(2,1)S(1)} collective-permute-done((bf16[4,16,1280]{2,1,0:T(8,128)(2,1)S(1)}, bf16[4,16,1280]{2,1,0:T(8,128)(2,1)S(1)}, u32[]{:S(2)}, u32[]{:S(2)}) %collective-permute-start.9) | collective-permute-done | bytes 163872 | tf_op jit(solution)/shard_map/ppermute | solution.py:110
  77.0 1.7 collective-permute-start.12
  78.7 12.8 %collective-permute-done.12 = bf16[2,4,32,512]{3,2,1,0:T(8,128)(2,1)S(1)} collective-permute-done((bf16[2,4,32,512]{3,2,1,0:T(8,128)(2,1)S(1)}, bf16[2,4,32,512]{3,2,1,0:T(8,128)(2,1)S(1)}, u32[]{:S(2)}, u32[]{:S(2)}) %collective-permute-start.12) | collective-permute-done | bytes 262176 | tf_op jit(solution)/shard_map/ppermute | solution.py:110
  91.5 2.6 collective-permute-done.11
  99.5 1.6 collective-permute-done.16
  101.1 9.5 %front_kernel.1 = (bf16[512,768]{1,0:T(8,128)(2,1)}, bf16[512,512]{1,0:T(8,128)(2,1)}, bf16[512,512]{1,0:T(8,128)(2,1)}, bf16[512,512]{1,0:T(8,128)(2,1)}, f32[5...) custom-call(bf16[512,512]{1,0:T(8,128)(2,1)} %reshape_squeeze.18.ref, ...), custom_call_target="tpu_custom_call" | custom-call | flops 1 | bytes 1 | tf_op jit(solution)/shard_map/front_kernel/pallas_call | solution.py:948
  112.6 2.6 qkv_kernel.1
  115.2 1.5 copy-done.27
  116.7 8.2 %attention_forward.1 = (bf16[512,768]{1,0:T(8,128)(2,1)S(1)}, f32[6,8,512]{2,1,0:T(8,128)S(1)}) custom-call(s32[512,1]{1,0:T(8,128)S(1)} %copy.83.col_ref, bf16[512,1536]{1,0:T(8,128)(2,1)S(1)} %get-tuple-element.155.q_ref.k_ref, bf16[512,1536]{1,0:T(8,128)(2,1)S(1)} %get-tuple-element.155.q_ref.k_ref, bf16[512,768]{1,0:T(8,128)(2,1)S(1)} %get-tuple-element.156.v_ref), custom_call_target="tpu_custom_call" | custom-call | flops 1 | bytes 1 | tf_op jit(solution)/shard_map/attention_forward/pallas_call | solution.py:457
  125.8 1.4 first_kernel.1
  128.1 3.7 %copy-done.2 = bf16[2,768,3072]{2,1,0:T(8,128)(2,1)S(1)} copy-done((bf16[2,768,3072]{2,1,0:T(8,128)(2,1)S(1)}, bf16[2,768,3072]{2,1,0:T(8,128)(2,1)}, u32[]{:S(2)}) %copy-start.2) | copy-done | bytes 9437208
  131.8 10.2 %up_forward.1 = (bf16[512,3072]{1,0:T(8,128)(2,1)S(1)}, bf16[512,3072]{1,0:T(8,128)(2,1)S(1)}) custom-call(bf16[512,768]{1,0:T(8,128)(2,1)S(1)} %get-tuple-element.159.x_ref.first_ref, bf16[2,768,3072]{2,1,0:T(8,128)(2,1)S(1)} %copy-done.2, f32[1,12032]{1,0:T(1,128)S(1)} %copy-done.31), custom_call_target="tpu_custom_call" | custom-call | flops 1 | bytes 1 | tf_op jit(solution)/shard_map/up_forward/pallas_call | solution.py:1002
  142.1 15.7 %middle.1 = (bf16[512,768]{1,0:T(8,128)(2,1)S(1)}, bf16[512,256]{1,0:T(8,128)(2,1)S(1)}, bf16[512,768]{1,0:T(8,128)(2,1)S(1)}, bf16[512,3072]{1,0:T(8,128)(2,1)S...) custom-call(bf16[512,3072]{1,0:T(8,128)(2,1)S(1)} %get-tuple-element, ...), custom_call_target="tpu_custom_call" | custom-call | flops 1 | bytes 1 | tf_op jit(solution)/shard_map/middle/pallas_call | solution.py:588
  157.8 2.9 convolution_convert_fusion
  161.4 3.1 %convolution_convert_fusion.1 = bf16[3072,768]{1,0:T(8,128)(2,1)S(1)} fusion(bf16[512,3072]{1,0:T(8,128)(2,1)S(1)} %get-tuple-element.160.hidden_ref, bf16[512,768]{1,0:T(8,128)(2,1)S(1)} %get-tuple-element.166.d_ffn_ref), kind=kOutput, calls=%fused_computation.1 | convolution fusion | flops 2418278400 | bytes 8650752 | tf_op jit(solution)/shard_map/dot_general | solution.py:60
  164.5 1.7 dynamic-slice_bitcast_fusion
  167.5 6.7 %first_backward.1 = (bf16[512,768]{1,0:T(8,128)(2,1)S(1)}, bf16[512,768]{1,0:T(8,128)(2,1)S(1)}, f32[1,768]{1,0:T(1,128)S(1)}, f32[1,768]{1,0:T(1,128)S(1)}, f32[1,768]{1,0:T(1,128)S(1)}) custom-call(bf16[512,3072]{1,0:T(8,128)(2,1)S(1)} %get-tuple-element.167.d_pre_ref, bf16[2,768,3072]{2,1,0:T(8,128)(2,1)S(1)} %bitcast.247, ...), custom_call_target="tpu_custom_call" | custom-call | flops 1 | bytes 1 | tf_op jit(solution)/shard_map/first_backward/pallas_call | solution.py:725
  174.3 1.3 add_lanes.1
  175.7 2.2 copy-done.6
  177.9 14.2 %attention_backward.1 = (bf16[512,1536]{1,0:T(8,128)(2,1)}, bf16[512,768]{1,0:T(8,128)(2,1)}) custom-call(s32[1,512]{1,0:T(1,128)} %bitcast.276, s32[512,1]{1,0:T(8,128)} %copy-done.26, bf16[512,1536]{1,0:T(8,128)(2,1)} %copy-done.3, bf16[512,1536]{1,0:T(8,128)(2,1)} %copy-done.3, bf16[512,768]{1,0:T(8,128)(2,1)} %copy-done.14, bf16[512,768]{1,0:T(8,128)(2,1)} %copy-done.40, ...), custom_call_target="tpu_custom_call" | custom-call | flops 1 | bytes 1 | tf_op jit(solution)/shard_map/attention_backward/pallas_call | solution.py:503
  192.1 1.4 copy-done.9
  194.7 4.2 %heads_grad_kernel.1 = (bf16[384,3072]{1,0:T(8,128)(2,1)S(1)}, bf16[384,3072]{1,0:T(8,128)(2,1)}) custom-call(bf16[512,768]{1,0:T(8,128)(2,1)S(1)} %copy-done.8, bf16[512,768]{1,0:T(8,128)(2,1)S(1)} %copy-done.16, bf16[512,1536]{1,0:T(8,128)(2,1)S(1)} %copy-done.9, bf16[512,768]{1,0:T(8,128)(2,1)S(1)} %copy-done.22, bf16[512,768]{1,0:T(8,128)(2,1)S(1)} %copy-done.20, ...), custom_call_target="tpu_custom_call" | custom-call | flops 1 | bytes 1 | tf_op jit(solution)/shard_map/heads_grad_kernel/pallas_call | solution.py:948
  198.9 1.4 copy-done.24
  200.7 2.5 constant_dynamic-slice_fusion.3
  205.5 1.7 copy-done.28
  207.2 2.8 inputs_back_kernel.1
  210.1 1.4 front_back_kernel.1
  212.5 2.2 split_vectors.1
  218.7 1.6 misc_grad_kernel.1
  222.4 2.5 add_convert_fusion
  226.9 1.5 collective-permute-start.23
  229.3 1.7 collective-permute-start.22
  233.4 2.0 reshape.269
  235.5 2.6 fusion.54
  238.0 2.4 reshape.268
  240.4 6.0 %collective-permute-done.23 = bf16[4,2,24,1536]{3,2,0,1:T(8,128)(2,1)} collective-permute-done((bf16[4,2,24,1536]{3,2,0,1:T(8,128)(2,1)}, bf16[4,2,24,1536]{3,2,0,1:T(8,128)(2,1)}, u32[]{:S(2)}, u32[]{:S(2)}) %collective-permute-start.23) | collective-permute-done | bytes 589856 | tf_op jit(solution)/shard_map/ppermute | solution.py:110
  246.4 1.6 fusion
  248.2 1.5 collective-permute-start.26
  251.8 1.5 collective-permute-start.25
  255.4 1.6 collective-permute-start.35
  257.0 2.0 collective-permute-done.27
  259.0 5.1 %collective-permute-done.25 = bf16[4,24,1536]{2,1,0:T(8,128)(2,1)S(1)} collective-permute-done((bf16[4,24,1536]{2,1,0:T(8,128)(2,1)S(1)}, bf16[4,24,1536]{2,1,0:T(8,128)(2,1)S(1)}, u32[]{:S(2)}, u32[]{:S(2)}) %collective-permute-start.25) | collective-permute-done | bytes 294944 | tf_op jit(solution)/shard_map/ppermute | solution.py:110
  264.2 1.5 collective-permute-start.30
  266.7 1.6 collective-permute-start.28
  268.3 2.7 collective-permute-done.35
  271.2 3.6 %collective-permute-start.36 = (bf16[48,3072]{1,0:T(8,128)(2,1)S(1)}, bf16[48,3072]{1,0:T(8,128)(2,1)S(1)}, u32[]{:S(2)}, u32[]{:S(2)}) collective-permute-start(bf16[48,3072]{1,0:T(8,128)(2,1)S(1)} %dynamic-slice_bitcast_fusion.5), channel_id=1, source_target_pairs={{0,12},{1,13},{2,14},{3,15},{4,8},{5,9},{6,10},{7,11},{8,4},{9,5},... | collective-permute-start | bytes 884744 | tf_op jit(solution)/shard_map/ppermute | solution.py:110
  274.8 1.6 collective-permute-done.28
  276.5 2.5 collective-permute-start.32
  279.2 5.4 %collective-permute-start.34 = (bf16[24,3072]{1,0:T(8,128)(2,1)S(1)}, bf16[24,3072]{1,0:T(8,128)(2,1)S(1)}, u32[]{:S(2)}, u32[]{:S(2)}) collective-permute-start(bf16[24,3072]{1,0:T(8,128)(2,1)S(1)} %dynamic-slice_bitcast_fusion.10), channel_id=1, source_target_pairs={{0,12},{1,13},{2,14},{3,15},{4,8},{5,9},{6,10},{7,11},{8,4},{9,5},... | collective-permute-start | bytes 442376 | tf_op jit(solution)/shard_map/ppermute | solution.py:110
  284.6 2.5 collective-permute-done.32
  287.2 6.0 %collective-permute-start.33 = (bf16[16,2304]{1,0:T(8,128)(2,1)S(1)}, bf16[16,2304]{1,0:T(8,128)(2,1)S(1)}, u32[]{:S(2)}, u32[]{:S(2)}) collective-permute-start(bf16[16,2304]{1,0:T(8,128)(2,1)S(1)} %dynamic-slice_bitcast_fusion.12), channel_id=1, source_target_pairs={{0,12},{1,13},{2,14},{3,15},{4,8},{5,9},{6,10},{7,11},{8,4},{9,5},... | collective-permute-start | bytes 221192 | tf_op jit(solution)/shard_map/ppermute | solution.py:110
  301.7 1.5 broadcast_select_fusion.2
  (346 shorter events, 59.4 us)
Async XLA Ops:
  7.2 13.0 %copy-start = (s32[2,256,100]{1,0,2:T(2,128)S(1)}, s32[2,256,100]{1,0,2:T(2,128)}, u32[]{:S(2)}) copy-start(s32[2,256,100]{1,0,2:T(2,128)} %param.50) | copy-start | bytes 614404
  7.2 9.8 %copy-start.56 = (bf16[2,1024,256]{2,1,0:T(8,128)(2,1)S(1)}, bf16[2,1024,256]{2,1,0:T(8,128)(2,1)}, u32[]{:S(2)}) copy-start(bf16[2,1024,256]{2,1,0:T(8,128)(2,1)} %param.26) | copy-start | bytes 3145732
  7.2 11.6 %copy-start.81 = (s32[2,3]{1,0:T(2,128)S(1)}, s32[2,3]{1,0:T(2,128)}, u32[]{:S(2)}) copy-start(s32[2,3]{1,0:T(2,128)} %param.48) | copy-start | bytes 76
  7.2 11.8 %copy-start.66 = (s32[2,2,512]{2,1,0:T(2,128)S(1)}, s32[2,2,512]{2,1,0:T(2,128)}, u32[]{:S(2)}) copy-start(s32[2,2,512]{2,1,0:T(2,128)} %param.51) | copy-start | bytes 24580
  7.2 11.8 %copy-start.80 = (bf16[2,320,128]{2,1,0:T(8,128)(2,1)S(1)}, bf16[2,320,128]{2,1,0:T(8,128)(2,1)}, u32[]{:S(2)}) copy-start(bf16[2,320,128]{2,1,0:T(8,128)(2,1)} %param.47) | copy-start | bytes 491524
  7.2 120.9 %all-gather.2.cloned.1.call-start = ((), (), s32[]{:S(2)}) async-start(), calls=%async_computation.1 | async-start | bytes 9732096 | tf_op jit(solution)/shard_map/all_gather | solution.py:1068
  10.1 9.8 %copy-start.72 = (bf16[24]{0:T(256)(128)(2,1)S(1)}, bf16[24]{0:T(256)(128)(2,1)}, u32[]{:S(2)}) copy-start(bf16[24]{0:T(256)(128)(2,1)} %param.38) | copy-start | bytes 148
  10.2 9.8 %copy-start.74 = (bf16[24]{0:T(256)(128)(2,1)S(1)}, bf16[24]{0:T(256)(128)(2,1)}, u32[]{:S(2)}) copy-start(bf16[24]{0:T(256)(128)(2,1)} %param.36) | copy-start | bytes 148
  10.2 9.8 %copy-start.75 = (bf16[48]{0:T(256)(128)(2,1)S(1)}, bf16[48]{0:T(256)(128)(2,1)}, u32[]{:S(2)}) copy-start(bf16[48]{0:T(256)(128)(2,1)} %param.34) | copy-start | bytes 292
  10.2 9.8 %copy-start.76 = (bf16[24]{0:T(256)(128)(2,1)S(1)}, bf16[24]{0:T(256)(128)(2,1)}, u32[]{:S(2)}) copy-start(bf16[24]{0:T(256)(128)(2,1)} %param.32) | copy-start | bytes 148
  10.2 9.8 %copy-start.77 = (bf16[24]{0:T(256)(128)(2,1)S(1)}, bf16[24]{0:T(256)(128)(2,1)}, u32[]{:S(2)}) copy-start(bf16[24]{0:T(256)(128)(2,1)} %param.31) | copy-start | bytes 148
  10.2 9.8 %copy-start.78 = (bf16[16]{0:T(256)(128)(2,1)S(1)}, bf16[16]{0:T(256)(128)(2,1)}, u32[]{:S(2)}) copy-start(bf16[16]{0:T(256)(128)(2,1)} %param.29) | copy-start | bytes 100
  10.2 9.8 %copy-start.79 = (bf16[16]{0:T(256)(128)(2,1)S(1)}, bf16[16]{0:T(256)(128)(2,1)}, u32[]{:S(2)}) copy-start(bf16[16]{0:T(256)(128)(2,1)} %param.28) | copy-start | bytes 100
  10.3 236.2 %reduce-scatter.2.cloned.1.call-start = ((), (), s32[]{:S(2)}) async-start(), calls=%async_computation.2 | async-start | bytes 5898240 | tf_op jit(solution)/shard_map/reduce_scatter | solution.py:1234
  12.0 11.1 %collective-permute-start = (bf16[24,3072]{1,0:T(8,128)(2,1)S(1)}, bf16[24,3072]{1,0:T(8,128)(2,1)S(1)}, u32[]{:S(2)}, u32[]{:S(2)}) collective-permute-start(bf16[24,3072]{1,0:T(8,128)(2,1)S(1)} %constant_dynamic-update-slice_fusion), channel_id=1, source_target_pairs={{0,12},{1,13},{2,14},{3,15},{4,8},{5,9},{6,10},{7,11},{8,4},{9,5},... | collective-permute-start | bytes 442376 | tf_op jit(solution)/shard_map/ppermute | solution.py:110
  17.1 26.8 %collective-permute-start.6 = (bf16[1024,256]{1,0:T(8,128)(2,1)S(1)}, bf16[1024,256]{1,0:T(8,128)(2,1)S(1)}, u32[]{:S(2)}, u32[]{:S(2)}) collective-permute-start(bf16[1024,256]{1,0:T(8,128)(2,1)S(1)} %get-tuple-element.241), channel_id=1, source_target_pairs={{0,16},{1,17},{2,18},{3,19},{4,20},{5,21},{6,22},{7,23},{8,24},{9,... | collective-permute-start | bytes 1572872 | tf_op jit(solution)/shard_map/ppermute | solution.py:110
  20.2 79.1 %copy-start.64 = (s32[512]{0:T(512)}, s32[512]{0:T(512)S(1)}, u32[]{:S(2)}) copy-start(s32[512]{0:T(512)S(1)} %fusion.44) | copy-start | bytes 6148
  23.3 16.2 %collective-permute-start.1 = (bf16[2,24,3072]{2,1,0:T(8,128)(2,1)S(1)}, bf16[2,24,3072]{2,1,0:T(8,128)(2,1)S(1)}, u32[]{:S(2)}, u32[]{:S(2)}) collective-permute-start(bf16[2,24,3072]{2,1,0:T(8,128)(2,1)S(1)} %broadcast_select_fusion.8), channel_id=1, source_target_pairs={{0,4},{1,5},{2,6},{3,7},{4,0},{5,1},{6,2},{7,3},{8,12},{9,13},{10,... | collective-permute-start | bytes 884744 | tf_op jit(solution)/shard_map/ppermute | solution.py:110
  24.1 14.8 %collective-permute-start.2 = (bf16[16,2304]{1,0:T(8,128)(2,1)S(1)}, bf16[16,2304]{1,0:T(8,128)(2,1)S(1)}, u32[]{:S(2)}, u32[]{:S(2)}) collective-permute-start(bf16[16,2304]{1,0:T(8,128)(2,1)S(1)} %constant_dynamic-update-slice_fusion.2), channel_id=1, source_target_pairs={{0,12},{1,13},{2,14},{3,15},{4,8},{5,9},{6,10},{7,11},{8,4},{9,5},... | collective-permute-start | bytes 221192 | tf_op jit(solution)/shard_map/ppermute | solution.py:110
  39.7 13.3 %collective-permute-start.3 = (bf16[4,24,1536]{2,1,0:T(8,128)(2,1)S(1)}, bf16[4,24,1536]{2,1,0:T(8,128)(2,1)S(1)}, u32[]{:S(2)}, u32[]{:S(2)}) collective-permute-start(bf16[4,24,1536]{2,1,0:T(8,128)(2,1)S(1)} %get-tuple-element.249), channel_id=1, source_target_pairs={{0,2},{1,3},{2,0},{3,1},{4,6},{5,7},{6,4},{7,5},{8,10},{9,11},{10,... | collective-permute-start | bytes 884744 | tf_op jit(solution)/shard_map/ppermute | solution.py:110
  41.3 12.6 %collective-permute-start.4 = (bf16[4,24,1536]{2,1,0:T(8,128)(2,1)S(1)}, bf16[4,24,1536]{2,1,0:T(8,128)(2,1)S(1)}, u32[]{:S(2)}, u32[]{:S(2)}) collective-permute-start(bf16[4,24,1536]{2,1,0:T(8,128)(2,1)S(1)} %get-tuple-element.248), channel_id=1, source_target_pairs={{0,16},{1,17},{2,18},{3,19},{4,20},{5,21},{6,22},{7,23},{8,24},{9,... | collective-permute-start | bytes 884744 | tf_op jit(solution)/shard_map/ppermute | solution.py:110
  42.2 10.8 %collective-permute-start.5 = (bf16[2,16,2304]{2,1,0:T(8,128)(2,1)S(1)}, bf16[2,16,2304]{2,1,0:T(8,128)(2,1)S(1)}, u32[]{:S(2)}, u32[]{:S(2)}) collective-permute-start(bf16[2,16,2304]{2,1,0:T(8,128)(2,1)S(1)} %broadcast_select_fusion.10), channel_id=1, source_target_pairs={{0,4},{1,5},{2,6},{3,7},{4,0},{5,1},{6,2},{7,3},{8,12},{9,13},{10,... | collective-permute-start | bytes 442376 | tf_op jit(solution)/shard_map/ppermute | solution.py:110
  54.0 18.6 %collective-permute-start.8 = (bf16[2,4,24,1536]{3,2,1,0:T(8,128)(2,1)S(1)}, bf16[2,4,24,1536]{3,2,1,0:T(8,128)(2,1)S(1)}, u32[]{:S(2)}, u32[]{:S(2)}) collective-permute-start(bf16[2,4,24,1536]{3,2,1,0:T(8,128)(2,1)S(1)} %broadcast_select_fusion.4), channel_id=1, source_target_pairs={{0,2},{1,3},{2,0},{3,1},{4,6},{5,7},{6,4},{7,5},{8,10},{9,11},{10,... | collective-permute-start | bytes 1769480 | tf_op jit(solution)/shard_map/ppermute | solution.py:110
  55.9 17.6 %collective-permute-start.7 = (bf16[4,2,24,1536]{3,2,1,0:T(8,128)(2,1)S(1)}, bf16[4,2,24,1536]{3,2,1,0:T(8,128)(2,1)}, u32[]{:S(2)}, u32[]{:S(2)}) collective-permute-start(bf16[4,2,24,1536]{3,2,1,0:T(8,128)(2,1)S(1)} %broadcast_select_fusion.5), channel_id=1, source_target_pairs={{0,16},{1,17},{2,18},{3,19},{4,20},{5,21},{6,22},{7,23},{8,24},{9,... | collective-permute-start | bytes 1769480 | tf_op jit(solution)/shard_map/ppermute | solution.py:110
  56.1 16.6 %collective-permute-start.9 = (bf16[4,16,1280]{2,1,0:T(8,128)(2,1)S(1)}, bf16[4,16,1280]{2,1,0:T(8,128)(2,1)S(1)}, u32[]{:S(2)}, u32[]{:S(2)}) collective-permute-start(bf16[4,16,1280]{2,1,0:T(8,128)(2,1)S(1)} %slice.213), channel_id=1, source_target_pairs={{0,2},{1,3},{2,0},{3,1},{4,6},{5,7},{6,4},{7,5},{8,10},{9,11},{10,... | collective-permute-start | bytes 491528 | tf_op jit(solution)/shard_map/ppermute | solution.py:110
  57.2 11.9 %collective-permute-start.10 = (bf16[4,32,512]{2,1,0:T(8,128)(2,1)S(1)}, bf16[4,32,512]{2,1,0:T(8,128)(2,1)S(1)}, u32[]{:S(2)}, u32[]{:S(2)}) collective-permute-start(bf16[4,32,512]{2,1,0:T(8,128)(2,1)S(1)} %bitcast.269), channel_id=1, source_target_pairs={{0,16},{1,17},{2,18},{3,19},{4,20},{5,21},{6,22},{7,23},{8,24},{9,... | collective-permute-start | bytes 393224 | tf_op jit(solution)/shard_map/ppermute | solution.py:110
  76.1 18.0 %collective-permute-start.13 = (bf16[2,4,2,24,1536]{4,3,2,1,0:T(8,128)(2,1)S(1)}, bf16[2,4,2,24,1536]{4,3,2,1,0:T(8,128)(2,1)S(1)}, u32[]{:S(2)}, u32[]{:S(2)}) collective-permute-start(bf16[2,4,2,24,1536]{4,3,2,1,0:T(8,128)(2,1)S(1)} %broadcast_select_fusion.1), channel_id=1, source_target_pairs={{0,1},{1,0},{2,3},{3,2},{4,5},{5,4},{6,7},{7,6},{8,9},{9,8},{10,11... | collective-permute-start | bytes 3538952 | tf_op jit(solution)/shard_map/ppermute | solution.py:110
  76.2 19.0 %collective-permute-start.14 = (bf16[2,4,2,24,1536]{4,3,2,1,0:T(8,128)(2,1)S(1)}, bf16[2,4,2,24,1536]{4,3,2,1,0:T(8,128)(2,1)S(1)}, u32[]{:S(2)}, u32[]{:S(2)}) collective-permute-start(bf16[2,4,2,24,1536]{4,3,2,1,0:T(8,128)(2,1)S(1)} %broadcast_select_fusion), channel_id=1, source_target_pairs={{0,1},{1,0},{2,3},{3,2},{4,5},{5,4},{6,7},{7,6},{8,9},{9,8},{10,11... | collective-permute-start | bytes 3538952 | tf_op jit(solution)/shard_map/ppermute | solution.py:110
  76.8 17.3 %collective-permute-start.11 = (bf16[4,2,16,1280]{3,2,1,0:T(8,128)(2,1)S(1)}, bf16[4,2,16,1280]{3,2,1,0:T(8,128)(2,1)S(1)}, u32[]{:S(2)}, u32[]{:S(2)}) collective-permute-start(bf16[4,2,16,1280]{3,2,1,0:T(8,128)(2,1)S(1)} %broadcast_select_fusion.7), channel_id=1, source_target_pairs={{0,16},{1,17},{2,18},{3,19},{4,20},{5,21},{6,22},{7,23},{8,24},{9,... | collective-permute-start | bytes 983048 | tf_op jit(solution)/shard_map/ppermute | solution.py:110
  77.0 14.5 %collective-permute-start.12 = (bf16[2,4,32,512]{3,2,1,0:T(8,128)(2,1)S(1)}, bf16[2,4,32,512]{3,2,1,0:T(8,128)(2,1)S(1)}, u32[]{:S(2)}, u32[]{:S(2)}) collective-permute-start(bf16[2,4,32,512]{3,2,1,0:T(8,128)(2,1)S(1)} %broadcast_select_fusion.9), channel_id=1, source_target_pairs={{0,2},{1,3},{2,0},{3,1},{4,6},{5,7},{6,4},{7,5},{8,10},{9,11},{10,... | collective-permute-start | bytes 786440 | tf_op jit(solution)/shard_map/ppermute | solution.py:110
  97.3 3.8 %collective-permute-start.15 = (bf16[2,4,2,16,1280]{4,3,2,1,0:T(8,128)(2,1)S(1)}, bf16[2,4,2,16,1280]{4,3,2,1,0:T(8,128)(2,1)}, u32[]{:S(2)}, u32[]{:S(2)}) collective-permute-start(bf16[2,4,2,16,1280]{4,3,2,1,0:T(8,128)(2,1)S(1)} %broadcast_select_fusion.3), channel_id=1, source_target_pairs={{0,1},{1,0},{2,3},{3,2},{4,5},{5,4},{6,7},{7,6},{8,9},{9,8},{10,11... | collective-permute-start | bytes 1966088 | tf_op jit(solution)/shard_map/ppermute | solution.py:110
  97.4 3.7 %collective-permute-start.16 = (bf16[2,4,2,32,512]{4,3,2,1,0:T(8,128)(2,1)}, bf16[2,4,2,32,512]{4,3,2,1,0:T(8,128)(2,1)}, u32[]{:S(2)}, u32[]{:S(2)}) collective-permute-start(bf16[2,4,2,32,512]{4,3,2,1,0:T(8,128)(2,1)} %broadcast_select_fusion.6), channel_id=1, source_target_pairs={{0,1},{1,0},{2,3},{3,2},{4,5},{5,4},{6,7},{7,6},{8,9},{9,8},{10,11... | collective-permute-start | bytes 1572872 | tf_op jit(solution)/shard_map/ppermute | solution.py:110
  99.5 17.2 %copy-start.26 = (s32[512,1]{1,0:T(8,128)}, s32[512,1]{1,0:T(8,128)S(1)}, u32[]{:S(2)}) copy-start(s32[512,1]{1,0:T(8,128)S(1)} %copy.83.col_ref) | copy-start | bytes 6148
  99.5 11.2 %copy-start.33 = (bf16[2,4,2,24,1536]{4,3,2,1,0:T(8,128)(2,1)S(1)}, bf16[2,4,2,24,1536]{4,3,2,1,0:T(8,128)(2,1)}, u32[]{:S(2)}) copy-start(bf16[2,4,2,24,1536]{4,3,2,1,0:T(8,128)(2,1)} %copy-done.32) | copy-start | bytes 3538948
  99.5 11.2 %copy-start.35 = (bf16[2,4,2,24,1536]{4,3,2,1,0:T(8,128)(2,1)S(1)}, bf16[2,4,2,24,1536]{4,3,2,1,0:T(8,128)(2,1)}, u32[]{:S(2)}) copy-start(bf16[2,4,2,24,1536]{4,3,2,1,0:T(8,128)(2,1)} %copy-done.34) | copy-start | bytes 3538948
  125.8 16.2 %copy-start.50 = (f32[6,8,512]{2,1,0:T(8,128)}, f32[6,8,512]{2,1,0:T(8,128)S(1)}, u32[]{:S(2)}) copy-start(f32[6,8,512]{2,1,0:T(8,128)S(1)} %get-tuple-element.175.log_ref) | copy-start | bytes 294916
  131.8 10.2 %copy-start.13 = (f32[512,1]{1,0:T(8,128)S(1)}, f32[512,1]{1,0:T(8,128)}, u32[]{:S(2)}) copy-start(f32[512,1]{1,0:T(8,128)} %copy.82.refs_6_.masked_ref.refs_5_) | copy-start | bytes 6148
  131.8 10.2 %copy-start.29 = (f32[512,256]{1,0:T(8,128)S(1)}, f32[512,256]{1,0:T(8,128)}, u32[]{:S(2)}) copy-start(f32[512,256]{1,0:T(8,128)} %fusion.20.targets_ref) | copy-start | bytes 1572868
  131.8 10.2 %copy-start.36 = (f32[512,512]{1,0:T(8,128)S(1)}, f32[512,512]{1,0:T(8,128)}, u32[]{:S(2)}) copy-start(f32[512,512]{1,0:T(8,128)} %convolution_add_fusion.counts_ref) | copy-start | bytes 3145732
  131.8 10.2 %copy-start.39 = (f32[768,256]{1,0:T(8,128)S(1)}, f32[768,256]{1,0:T(8,128)}, u32[]{:S(2)}) copy-start(f32[768,256]{1,0:T(8,128)} %get-tuple-element.162.final_ref) | copy-start | bytes 2359300
  161.1 13.2 %collective-permute-start.18 = (bf16[384,3072]{1,0:T(8,128)(2,1)S(1)}, bf16[384,3072]{1,0:T(8,128)(2,1)S(1)}, u32[]{:S(2)}, u32[]{:S(2)}) collective-permute-start(bf16[384,3072]{1,0:T(8,128)(2,1)S(1)} %bitcast.262), channel_id=1, source_target_pairs={{0,1},{1,0},{2,3},{3,2},{4,5},{5,4},{6,7},{7,6},{8,9},{9,8},{10,11... | collective-permute-start | bytes 7077896 | tf_op jit(solution)/shard_map/ppermute | solution.py:110
  166.3 8.0 %collective-permute-start.17 = (bf16[1536,768]{1,0:T(8,128)(2,1)}, bf16[1536,768]{1,0:T(8,128)(2,1)S(1)}, u32[]{:S(2)}, u32[]{:S(2)}) collective-permute-start(bf16[1536,768]{1,0:T(8,128)(2,1)} %bitcast.263), channel_id=1, source_target_pairs={{0,1},{1,0},{2,3},{3,2},{4,5},{5,4},{6,7},{7,6},{8,9},{9,8},{10,11... | collective-permute-start | bytes 7077896 | tf_op jit(solution)/shard_map/ppermute | solution.py:110
  167.3 7.0 %collective-permute-start.19 = (f32[2]{0:T(128)S(1)}, f32[2]{0:T(128)S(1)}, u32[]{:S(2)}, u32[]{:S(2)}) collective-permute-start(f32[2]{0:T(128)S(1)} %broadcast_select_fusion.11), channel_id=1, source_target_pairs={{0,16},{1,17},{2,18},{3,19},{4,20},{5,21},{6,22},{7,23},{8,24},{9,... | collective-permute-start | bytes 32 | tf_op jit(solution)/shard_map/ppermute | solution.py:110
  177.9 14.2 %copy-start.8 = (bf16[512,768]{1,0:T(8,128)(2,1)S(1)}, bf16[512,768]{1,0:T(8,128)(2,1)}, u32[]{:S(2)}) copy-start(bf16[512,768]{1,0:T(8,128)(2,1)} %get-tuple-element.150.refs_0_) | copy-start | bytes 2359300
  177.9 14.2 %copy-start.16 = (bf16[512,768]{1,0:T(8,128)(2,1)S(1)}, bf16[512,768]{1,0:T(8,128)(2,1)}, u32[]{:S(2)}) copy-start(bf16[512,768]{1,0:T(8,128)(2,1)} %copy-done.15) | copy-start | bytes 2359300
  177.9 14.2 %copy-start.20 = (bf16[512,768]{1,0:T(8,128)(2,1)S(1)}, bf16[512,768]{1,0:T(8,128)(2,1)}, u32[]{:S(2)}) copy-start(bf16[512,768]{1,0:T(8,128)(2,1)} %copy-done.19) | copy-start | bytes 2359300
  200.3 9.8 %collective-permute-start.20 = (bf16[384,3072]{1,0:T(8,128)(2,1)}, bf16[384,3072]{1,0:T(8,128)(2,1)}, u32[]{:S(2)}, u32[]{:S(2)}) collective-permute-start(bf16[384,3072]{1,0:T(8,128)(2,1)} %get-tuple-element.179), channel_id=1, source_target_pairs={{0,1},{1,0},{2,3},{3,2},{4,5},{5,4},{6,7},{7,6},{8,9},{9,8},{10,11... | collective-permute-start | bytes 7077896 | tf_op jit(solution)/shard_map/ppermute | solution.py:110
  221.5 24.9 %collective-permute-start.21 = (bf16[256,2304]{1,0:T(8,128)(2,1)}, bf16[256,2304]{1,0:T(8,128)(2,1)}, u32[]{:S(2)}, u32[]{:S(2)}) collective-permute-start(bf16[256,2304]{1,0:T(8,128)(2,1)} %bitcast.56), channel_id=1, source_target_pairs={{0,1},{1,0},{2,3},{3,2},{4,5},{5,4},{6,7},{7,6},{8,9},{9,8},{10,11... | collective-permute-start | bytes 3538952 | tf_op jit(solution)/shard_map/ppermute | solution.py:110
  226.9 19.5 %collective-permute-start.23 = (bf16[4,2,24,1536]{3,2,0,1:T(8,128)(2,1)}, bf16[4,2,24,1536]{3,2,0,1:T(8,128)(2,1)}, u32[]{:S(2)}, u32[]{:S(2)}) collective-permute-start(bf16[4,2,24,1536]{3,2,0,1:T(8,128)(2,1)} %bitcast.242), channel_id=1, source_target_pairs={{0,16},{1,17},{2,18},{3,19},{4,20},{5,21},{6,22},{7,23},{8,24},{9,... | collective-permute-start | bytes 1769480 | tf_op jit(solution)/shard_map/ppermute | solution.py:110
  229.3 17.1 %collective-permute-start.22 = (bf16[2,4,24,1536]{3,2,1,0:T(8,128)(2,1)}, bf16[2,4,24,1536]{3,2,1,0:T(8,128)(2,1)}, u32[]{:S(2)}, u32[]{:S(2)}) collective-permute-start(bf16[2,4,24,1536]{3,2,1,0:T(8,128)(2,1)} %dynamic-slice_bitcast_fusion.2), channel_id=1, source_target_pairs={{0,2},{1,3},{2,0},{3,1},{4,6},{5,7},{6,4},{7,5},{8,10},{9,11},{10,... | collective-permute-start | bytes 1769480 | tf_op jit(solution)/shard_map/ppermute | solution.py:110
  248.2 15.9 %collective-permute-start.26 = (bf16[2,4,16,1280]{3,2,1,0:T(8,128)(2,1)S(1)}, bf16[2,4,16,1280]{3,2,1,0:T(8,128)(2,1)S(1)}, u32[]{:S(2)}, u32[]{:S(2)}) collective-permute-start(bf16[2,4,16,1280]{3,2,1,0:T(8,128)(2,1)S(1)} %dynamic-slice_bitcast_fusion.4), channel_id=1, source_target_pairs={{0,2},{1,3},{2,0},{3,1},{4,6},{5,7},{6,4},{7,5},{8,10},{9,11},{10,... | collective-permute-start | bytes 983048 | tf_op jit(solution)/shard_map/ppermute | solution.py:110
  249.8 9.2 %collective-permute-start.27 = (bf16[4,2,16,1024]{3,2,1,0:T(8,128)(2,1)S(1)}, bf16[4,2,16,1024]{3,2,1,0:T(8,128)(2,1)S(1)}, u32[]{:S(2)}, u32[]{:S(2)}) collective-permute-start(bf16[4,2,16,1024]{3,2,1,0:T(8,128)(2,1)S(1)} %dynamic-slice_bitcast_fusion.8), channel_id=1, source_target_pairs={{0,16},{1,17},{2,18},{3,19},{4,20},{5,21},{6,22},{7,23},{8,24},{9,... | collective-permute-start | bytes 786440 | tf_op jit(solution)/shard_map/ppermute | solution.py:110
  251.8 12.3 %collective-permute-start.25 = (bf16[4,24,1536]{2,1,0:T(8,128)(2,1)S(1)}, bf16[4,24,1536]{2,1,0:T(8,128)(2,1)S(1)}, u32[]{:S(2)}, u32[]{:S(2)}) collective-permute-start(bf16[4,24,1536]{2,1,0:T(8,128)(2,1)S(1)} %dynamic-slice_bitcast_fusion.6), channel_id=1, source_target_pairs={{0,2},{1,3},{2,0},{3,1},{4,6},{5,7},{6,4},{7,5},{8,10},{9,11},{10,... | collective-permute-start | bytes 884744 | tf_op jit(solution)/shard_map/ppermute | solution.py:110
  254.6 9.5 %collective-permute-start.24 = (bf16[4,24,1536]{2,1,0:T(8,128)(2,1)S(1)}, bf16[4,24,1536]{2,1,0:T(8,128)(2,1)S(1)}, u32[]{:S(2)}, u32[]{:S(2)}) collective-permute-start(bf16[4,24,1536]{2,1,0:T(8,128)(2,1)S(1)} %dynamic-slice_bitcast_fusion.7), channel_id=1, source_target_pairs={{0,16},{1,17},{2,18},{3,19},{4,20},{5,21},{6,22},{7,23},{8,24},{9,... | collective-permute-start | bytes 884744 | tf_op jit(solution)/shard_map/ppermute | solution.py:110
  255.4 15.6 %collective-permute-start.35 = (bf16[2,48,3072]{2,1,0:T(8,128)(2,1)S(1)}, bf16[2,48,3072]{2,1,0:T(8,128)(2,1)S(1)}, u32[]{:S(2)}, u32[]{:S(2)}) collective-permute-start(bf16[2,48,3072]{2,1,0:T(8,128)(2,1)S(1)} %fusion.10), channel_id=1, source_target_pairs={{0,4},{1,5},{2,6},{3,7},{4,0},{5,1},{6,2},{7,3},{8,12},{9,13},{10,... | collective-permute-start | bytes 1769480 | tf_op jit(solution)/shard_map/ppermute | solution.py:110
  264.2 10.6 %collective-permute-start.30 = (bf16[4,16,1024]{2,1,0:T(8,128)(2,1)S(1)}, bf16[4,16,1024]{2,1,0:T(8,128)(2,1)S(1)}, u32[]{:S(2)}, u32[]{:S(2)}) collective-permute-start(bf16[4,16,1024]{2,1,0:T(8,128)(2,1)S(1)} %dynamic-slice_bitcast_fusion.11), channel_id=1, source_target_pairs={{0,2},{1,3},{2,0},{3,1},{4,6},{5,7},{6,4},{7,5},{8,10},{9,11},{10,... | collective-permute-start | bytes 393224 | tf_op jit(solution)/shard_map/ppermute | solution.py:110
  265.8 9.0 %collective-permute-start.29 = (bf16[4,16,1280]{2,1,0:T(8,128)(2,1)S(1)}, bf16[4,16,1280]{2,1,0:T(8,128)(2,1)S(1)}, u32[]{:S(2)}, u32[]{:S(2)}) collective-permute-start(bf16[4,16,1280]{2,1,0:T(8,128)(2,1)S(1)} %dynamic-slice_bitcast_fusion.9), channel_id=1, source_target_pairs={{0,16},{1,17},{2,18},{3,19},{4,20},{5,21},{6,22},{7,23},{8,24},{9,... | collective-permute-start | bytes 491528 | tf_op jit(solution)/shard_map/ppermute | solution.py:110
  266.7 9.6 %collective-permute-start.28 = (bf16[2,24,3072]{2,1,0:T(8,128)(2,1)S(1)}, bf16[2,24,3072]{2,1,0:T(8,128)(2,1)S(1)}, u32[]{:S(2)}, u32[]{:S(2)}) collective-permute-start(bf16[2,24,3072]{2,1,0:T(8,128)(2,1)S(1)} %fusion.29), channel_id=1, source_target_pairs={{0,4},{1,5},{2,6},{3,7},{4,0},{5,1},{6,2},{7,3},{8,12},{9,13},{10,... | collective-permute-start | bytes 884744 | tf_op jit(solution)/shard_map/ppermute | solution.py:110
  271.1 13.5 %copy-start.58 = (bf16[1024,256]{1,0:T(8,128)(2,1)S(1)}, bf16[1024,256]{1,0:T(8,128)(2,1)}, u32[]{:S(2)}) copy-start(bf16[1024,256]{1,0:T(8,128)(2,1)} %reshape.269) | copy-start | bytes 1572868
  271.2 28.8 %collective-permute-start.36 = (bf16[48,3072]{1,0:T(8,128)(2,1)S(1)}, bf16[48,3072]{1,0:T(8,128)(2,1)S(1)}, u32[]{:S(2)}, u32[]{:S(2)}) collective-permute-start(bf16[48,3072]{1,0:T(8,128)(2,1)S(1)} %dynamic-slice_bitcast_fusion.5), channel_id=1, source_target_pairs={{0,12},{1,13},{2,14},{3,15},{4,8},{5,9},{6,10},{7,11},{8,4},{9,5},... | collective-permute-start | bytes 884744 | tf_op jit(solution)/shard_map/ppermute | solution.py:110
  276.5 10.6 %collective-permute-start.32 = (bf16[2,16,2304]{2,1,0:T(8,128)(2,1)S(1)}, bf16[2,16,2304]{2,1,0:T(8,128)(2,1)S(1)}, u32[]{:S(2)}, u32[]{:S(2)}) collective-permute-start(bf16[2,16,2304]{2,1,0:T(8,128)(2,1)S(1)} %fusion.37), channel_id=1, source_target_pairs={{0,4},{1,5},{2,6},{3,7},{4,0},{5,1},{6,2},{7,3},{8,12},{9,13},{10,... | collective-permute-start | bytes 442376 | tf_op jit(solution)/shard_map/ppermute | solution.py:110
  279.2 14.0 %collective-permute-start.34 = (bf16[24,3072]{1,0:T(8,128)(2,1)S(1)}, bf16[24,3072]{1,0:T(8,128)(2,1)S(1)}, u32[]{:S(2)}, u32[]{:S(2)}) collective-permute-start(bf16[24,3072]{1,0:T(8,128)(2,1)S(1)} %dynamic-slice_bitcast_fusion.10), channel_id=1, source_target_pairs={{0,12},{1,13},{2,14},{3,15},{4,8},{5,9},{6,10},{7,11},{8,4},{9,5},... | collective-permute-start | bytes 442376 | tf_op jit(solution)/shard_map/ppermute | solution.py:110
  284.6 17.0 %collective-permute-start.31 = (bf16[1024,256]{1,0:T(8,128)(2,1)S(1)}, bf16[1024,256]{1,0:T(8,128)(2,1)S(1)}, u32[]{:S(2)}, u32[]{:S(2)}) collective-permute-start(bf16[1024,256]{1,0:T(8,128)(2,1)S(1)} %copy-done.58), channel_id=1, source_target_pairs={{0,16},{1,17},{2,18},{3,19},{4,20},{5,21},{6,22},{7,23},{8,24},{9,... | collective-permute-start | bytes 1572872 | tf_op jit(solution)/shard_map/ppermute | solution.py:110
  287.2 8.3 %collective-permute-start.33 = (bf16[16,2304]{1,0:T(8,128)(2,1)S(1)}, bf16[16,2304]{1,0:T(8,128)(2,1)S(1)}, u32[]{:S(2)}, u32[]{:S(2)}) collective-permute-start(bf16[16,2304]{1,0:T(8,128)(2,1)S(1)} %dynamic-slice_bitcast_fusion.12), channel_id=1, source_target_pairs={{0,12},{1,13},{2,14},{3,15},{4,8},{5,9},{6,10},{7,11},{8,4},{9,5},... | collective-permute-start | bytes 221192 | tf_op jit(solution)/shard_map/ppermute | solution.py:110
  (62 other events, 244.9 us)
Sparse Core Ops, SparseCore 0:
  11.6 100.1 all-gather.1
  178.0 60.7 reduce-scatter.1

commit v3 on v2

--- a/solution.py
+++ b/solution.py
@@ -984,16 +984,10 @@
 def up_kernel(x_ref, ffn_ref, bias_ref, hidden_ref, slope_ref, pre_ref, held_ref, sems):
     pre_ref[...] = plain_dot(x_ref[...], fetched(ffn_ref, held_ref, sems))
     bias = bias_ref[...]
-    rows = 32
-
-    def step(r, carry):
-        at = pl.ds(pl.multiple_of(r * rows, rows), rows)
+    for at in row_steps(64):
         value, slope = gelu_and_slope(pre_ref[at, :] + bias)
         hidden_ref[at, :] = value.astype(low)
         slope_ref[at, :] = slope.astype(low)
-        return carry
-
-    lax.fori_loop(0, FMB // rows, step, 0)
 
 
 def up_forward(x, ffn, vectors, tile=1024):
@@ -1144,10 +1138,7 @@
 
     misc.start_second()
     heads.start_core()
-    (got_pairs,) = after([misc, heads], got_pairs)
-
     misc.start_core()
-    (got_pairs,) = after([misc], got_pairs)
     half = C // 2
     (
         inputs, normed, hat_zero, conv_slope, inverse_zero, conv_full, proj_full, vectors, final_full
@@ -1283,15 +1274,15 @@
     ffn = Line(links, line)
     ffn.start_z()
     (got_d,) = after([heads, misc], got_d)
+    got_d = links.over_y(got_d)
 
     heads.start_z()
     misc.start_second()
     ffn.start_z_rest()
-    (got_d,) = after([heads, misc], got_d)
+    after([heads, misc])
 
     heads.start_z_rest()
     misc.start_z()
-    got_d = links.over_y(got_d)
     after([misc])
     misc.start_z_rest()
     features_grad = in_order(section, own_d, got_d.astype(full), -2)

time: 315 us -> 311 us (0.987)
  waiting for transfers between devices: 66.7 us -> 61.1 us
    ppermute x37, waiting for transfers between devices: 66.6 us -> 61.1 us  [move(): return lax.ppermute(value, BOTH, pairs)]
    unnamed x178 -> x172, local copies, waits for them, and re-layouts: 28.4 us -> 26.7 us
  transfers between devices with their start and end apart: 39 -> 39, of which waited for: 16 -> 18; matrix products, arithmetic and copies ran while one was open for 17% -> 17% of each run, Pallas kernels for 20% -> 21%
where the time goes in v3:
time: 311 us; the launch traced here: 306 us
  Pallas kernels  89.8 us (29%)
  waiting for transfers between devices  61.1 us (20%)
  local copies, waits for them, and re-layouts  54.3 us (17%)
  starting transfers between devices  52.1 us (17%)
  other arithmetic  20.5 us (7%)
  between operations  16.1 us (5%)
  matrix products  11.9 us (4%)
    ppermute x37, waiting for transfers between devices, move(): return lax.ppermute(value, BOTH, pairs)  61.1 us
    ppermute x37, starting transfers between devices, move(): return lax.ppermute(value, BOTH, pairs)  52.1 us
    unnamed x172, local copies, waits for them, and re-layouts  26.7 us
    pallas_call x7, Pallas kernels, call(): pl.pallas_call(run, out_shape=[jax.ShapeDtypeStruct(shape, dtype) for sha...  25.2 us
    pallas_call x1, Pallas kernels, middle(): pl.pallas_call(functools.partial(middle_kernel, each), grid=(1,), in_spec...  15.7 us
    pallas_call x1, Pallas kernels, attention_backward(): pl.pallas_call(attention_back_kernel, grid=(pairs,), in_specs=[pl.BlockSp...  14.1 us
    pallas_call x1, Pallas kernels, up_forward(): pl.pallas_call(up_kernel, grid=(FF // tile,), in_specs=[pl.BlockSpec((FMB...  9.19 us
    pallas_call x1, Pallas kernels, attention_forward(): pl.pallas_call(attention_kernel, grid=(pairs,), in_specs=[pl.BlockSpec((F...  8.24 us
  transfers between devices with their start and end apart: 39, of which 18 were waited for; matrix products, arithmetic and copies ran while one was open for 17% of the time, Pallas kernels for 21%

profile of v3, /device:TPU:0, one launch (start us, length us, event | category | flops | bytes accessed | tf_op | source)
XLA Modules:
  0.0 305.9 jit_solution(2457860313737528136)
XLA Ops:
  8.5 1.7 pad_maximum_fusion.2
  12.0 5.0 %collective-permute-start = (bf16[24,3072]{1,0:T(8,128)(2,1)S(1)}, bf16[24,3072]{1,0:T(8,128)(2,1)S(1)}, u32[]{:S(2)}, u32[]{:S(2)}) collective-permute-start(bf16[24,3072]{1,0:T(8,128)(2,1)S(1)} %constant_dynamic-update-slice_fusion), channel_id=1, source_target_pairs={{0,12},{1,13},{2,14},{3,15},{4,8},{5,9},{6,10},{7,11},{8,4},{9,5},... | collective-permute-start | bytes 442376 | tf_op jit(solution)/shard_map/ppermute | solution.py:110
  17.1 1.6 collective-permute-start.6
  24.1 2.5 collective-permute-start.2
  26.6 7.1 %shard_map.417 = bf16[512,256]{1,0:T(8,128)(2,1)} custom-call(s32[100,256]{1,0:T(8,128)} %bitcast.270), custom_call_target="tpu_custom_call" | custom-call | flops 1 | bytes 1 | tf_op jit(solution)/shard_map/pallas_call | solution.py:399
  33.8 5.1 %collective-permute-done.2 = bf16[16,2304]{1,0:T(8,128)(2,1)S(1)} collective-permute-done((bf16[16,2304]{1,0:T(8,128)(2,1)S(1)}, bf16[16,2304]{1,0:T(8,128)(2,1)S(1)}, u32[]{:S(2)}, u32[]{:S(2)}) %collective-permute-start.2) | collective-permute-done | bytes 73760 | tf_op jit(solution)/shard_map/ppermute | solution.py:110
  39.8 1.6 collective-permute-start.3
  42.6 1.4 convolution_add_fusion.counts_ref
  44.0 9.0 %collective-permute-done.5 = bf16[2,16,2304]{2,1,0:T(8,128)(2,1)S(1)} collective-permute-done((bf16[2,16,2304]{2,1,0:T(8,128)(2,1)S(1)}, bf16[2,16,2304]{2,1,0:T(8,128)(2,1)S(1)}, u32[]{:S(2)}, u32[]{:S(2)}) %collective-permute-start.5) | collective-permute-done | bytes 147488 | tf_op jit(solution)/shard_map/ppermute | solution.py:110
  54.0 1.7 collective-permute-start.8
  57.3 1.4 collective-permute-start.10
  58.7 2.0 reshape.248.refs_1_.refs_5_
  60.7 8.4 %collective-permute-done.10 = bf16[4,32,512]{2,1,0:T(8,128)(2,1)S(1)} collective-permute-done((bf16[4,32,512]{2,1,0:T(8,128)(2,1)S(1)}, bf16[4,32,512]{2,1,0:T(8,128)(2,1)S(1)}, u32[]{:S(2)}, u32[]{:S(2)}) %collective-permute-start.10) | collective-permute-done | bytes 131104 | tf_op jit(solution)/shard_map/ppermute | solution.py:110
  69.1 3.7 %collective-permute-done.9 = bf16[4,16,1280]{2,1,0:T(8,128)(2,1)S(1)} collective-permute-done((bf16[4,16,1280]{2,1,0:T(8,128)(2,1)S(1)}, bf16[4,16,1280]{2,1,0:T(8,128)(2,1)S(1)}, u32[]{:S(2)}, u32[]{:S(2)}) %collective-permute-start.9) | collective-permute-done | bytes 163872 | tf_op jit(solution)/shard_map/ppermute | solution.py:110
  72.9 1.6 collective-permute-start.12
  74.7 1.3 broadcast_select_fusion
  76.8 10.0 %collective-permute-done.12 = bf16[2,4,32,512]{3,2,1,0:T(8,128)(2,1)S(1)} collective-permute-done((bf16[2,4,32,512]{3,2,1,0:T(8,128)(2,1)S(1)}, bf16[2,4,32,512]{3,2,1,0:T(8,128)(2,1)S(1)}, u32[]{:S(2)}, u32[]{:S(2)}) %collective-permute-start.12) | collective-permute-done | bytes 262176 | tf_op jit(solution)/shard_map/ppermute | solution.py:110
  87.8 3.4 %collective-permute-done.11 = bf16[4,2,16,1280]{3,2,1,0:T(8,128)(2,1)S(1)} collective-permute-done((bf16[4,2,16,1280]{3,2,1,0:T(8,128)(2,1)S(1)}, bf16[4,2,16,1280]{3,2,1,0:T(8,128)(2,1)S(1)}, u32[]{:S(2)}, u32[]{:S(2)}) %collective-permute-start.11) | collective-permute-done | bytes 327712 | tf_op jit(solution)/shard_map/ppermute | solution.py:110
  94.6 9.6 %front_kernel.1 = (bf16[512,768]{1,0:T(8,128)(2,1)}, bf16[512,512]{1,0:T(8,128)(2,1)}, bf16[512,512]{1,0:T(8,128)(2,1)}, bf16[512,512]{1,0:T(8,128)(2,1)}, f32[5...) custom-call(bf16[512,512]{1,0:T(8,128)(2,1)} %reshape_squeeze.18.ref, ...), custom_call_target="tpu_custom_call" | custom-call | flops 1 | bytes 1 | tf_op jit(solution)/shard_map/front_kernel/pallas_call | solution.py:948
  107.5 4.2 %qkv_kernel.1 = (bf16[768,1536]{1,0:T(8,128)(2,1)S(1)}, bf16[768,1536]{1,0:T(8,128)(2,1)S(1)}, bf16[512,1536]{1,0:T(8,128)(2,1)S(1)}, bf16[512,768]{1,0:T(8,128)(2,1)S(1)}) custom-call(bf16[512,768]{1,0:T(8,128)(2,1)S(1)} %copy-done.7, bf16[384,1536]{1,0:T(8,128)(2,1)S(1)} %bitcast.251, bf16[384,1536]{1,0:T(8,128)(2,1)} %bitcast.40.refs_2_, ...), custom_call_target="tpu_custom_call" | custom-call | flops 1 | bytes 1 | tf_op jit(solution)/shard_map/qkv_kernel/pallas_call | solution.py:948
  111.8 1.5 copy-done.27
  113.2 8.2 %attention_forward.1 = (bf16[512,768]{1,0:T(8,128)(2,1)S(1)}, f32[6,8,512]{2,1,0:T(8,128)S(1)}) custom-call(s32[512,1]{1,0:T(8,128)S(1)} %copy.83.col_ref, bf16[512,1536]{1,0:T(8,128)(2,1)S(1)} %get-tuple-element.138.q_ref.k_ref, bf16[512,1536]{1,0:T(8,128)(2,1)S(1)} %get-tuple-element.138.q_ref.k_ref, bf16[512,768]{1,0:T(8,128)(2,1)S(1)} %get-tuple-element.139.v_ref), custom_call_target="tpu_custom_call" | custom-call | flops 1 | bytes 1 | tf_op jit(solution)/shard_map/attention_forward/pallas_call | solution.py:457
  122.4 1.4 first_kernel.1
  125.6 3.7 %copy-done.2 = bf16[2,768,3072]{2,1,0:T(8,128)(2,1)S(1)} copy-done((bf16[2,768,3072]{2,1,0:T(8,128)(2,1)S(1)}, bf16[2,768,3072]{2,1,0:T(8,128)(2,1)}, u32[]{:S(2)}) %copy-start.2) | copy-done | bytes 9437208
  129.3 9.2 %up_forward.1 = (bf16[512,3072]{1,0:T(8,128)(2,1)S(1)}, bf16[512,3072]{1,0:T(8,128)(2,1)S(1)}) custom-call(bf16[512,768]{1,0:T(8,128)(2,1)S(1)} %get-tuple-element.142.x_ref.first_ref, bf16[2,768,3072]{2,1,0:T(8,128)(2,1)S(1)} %copy-done.2, f32[1,12032]{1,0:T(1,128)S(1)} %copy-done.31), custom_call_target="tpu_custom_call" | custom-call | flops 1 | bytes 1 | tf_op jit(solution)/shard_map/up_forward/pallas_call | solution.py:996
  138.5 15.7 %middle.1 = (bf16[512,768]{1,0:T(8,128)(2,1)S(1)}, bf16[512,256]{1,0:T(8,128)(2,1)S(1)}, bf16[512,768]{1,0:T(8,128)(2,1)S(1)}, bf16[512,3072]{1,0:T(8,128)(2,1)S...) custom-call(bf16[512,3072]{1,0:T(8,128)(2,1)S(1)} %get-tuple-element, ...), custom_call_target="tpu_custom_call" | custom-call | flops 1 | bytes 1 | tf_op jit(solution)/shard_map/middle/pallas_call | solution.py:588
  154.3 2.9 convolution_convert_fusion
  157.7 3.1 %convolution_convert_fusion.1 = bf16[3072,768]{1,0:T(8,128)(2,1)S(1)} fusion(bf16[512,3072]{1,0:T(8,128)(2,1)S(1)} %get-tuple-element.143.hidden_ref, bf16[512,768]{1,0:T(8,128)(2,1)S(1)} %get-tuple-element.149.d_ffn_ref), kind=kOutput, calls=%fused_computation.1 | convolution fusion | flops 2418278400 | bytes 8650752 | tf_op jit(solution)/shard_map/dot_general | solution.py:60
  160.9 1.7 dynamic-slice_bitcast_fusion
  164.1 6.7 %first_backward.1 = (bf16[512,768]{1,0:T(8,128)(2,1)S(1)}, bf16[512,768]{1,0:T(8,128)(2,1)S(1)}, f32[1,768]{1,0:T(1,128)S(1)}, f32[1,768]{1,0:T(1,128)S(1)}, f32[1,768]{1,0:T(1,128)S(1)}) custom-call(bf16[512,3072]{1,0:T(8,128)(2,1)S(1)} %get-tuple-element.150.d_pre_ref, bf16[2,768,3072]{2,1,0:T(8,128)(2,1)S(1)} %bitcast.247, ...), custom_call_target="tpu_custom_call" | custom-call | flops 1 | bytes 1 | tf_op jit(solution)/shard_map/first_backward/pallas_call | solution.py:725
  170.9 1.3 add_lanes.1
  172.3 2.2 copy-done.6
  174.5 14.1 %attention_backward.1 = (bf16[512,1536]{1,0:T(8,128)(2,1)}, bf16[512,768]{1,0:T(8,128)(2,1)}) custom-call(s32[1,512]{1,0:T(1,128)} %bitcast.274, s32[512,1]{1,0:T(8,128)} %copy-done.26, bf16[512,1536]{1,0:T(8,128)(2,1)} %copy-done.3, bf16[512,1536]{1,0:T(8,128)(2,1)} %copy-done.3, bf16[512,768]{1,0:T(8,128)(2,1)} %copy-done.14, bf16[512,768]{1,0:T(8,128)(2,1)} %copy-done.36, ...), custom_call_target="tpu_custom_call" | custom-call | flops 1 | bytes 1 | tf_op jit(solution)/shard_map/attention_backward/pallas_call | solution.py:503
  188.7 1.4 copy-done.9
  191.3 4.2 %heads_grad_kernel.1 = (bf16[384,3072]{1,0:T(8,128)(2,1)S(1)}, bf16[384,3072]{1,0:T(8,128)(2,1)}) custom-call(bf16[512,768]{1,0:T(8,128)(2,1)S(1)} %copy-done.8, bf16[512,768]{1,0:T(8,128)(2,1)S(1)} %copy-done.16, bf16[512,1536]{1,0:T(8,128)(2,1)S(1)} %copy-done.9, bf16[512,768]{1,0:T(8,128)(2,1)S(1)} %copy-done.22, bf16[512,768]{1,0:T(8,128)(2,1)S(1)} %copy-done.20, ...), custom_call_target="tpu_custom_call" | custom-call | flops 1 | bytes 1 | tf_op jit(solution)/shard_map/heads_grad_kernel/pallas_call | solution.py:948
  195.5 1.4 copy-done.24
  197.3 2.4 constant_dynamic-slice_fusion.3
  201.9 1.7 copy-done.28
  203.7 2.8 inputs_back_kernel.1
  206.6 1.4 front_back_kernel.1
  209.0 2.2 split_vectors.1
  215.3 1.6 misc_grad_kernel.1
  219.0 2.5 add_convert_fusion
  223.6 1.4 collective-permute-start.23
  229.1 2.0 reshape.269
  231.1 2.6 fusion.54
  233.7 2.4 reshape.268
  236.0 5.5 %collective-permute-done.23 = bf16[4,2,24,1536]{3,2,0,1:T(8,128)(2,1)} collective-permute-done((bf16[4,2,24,1536]{3,2,0,1:T(8,128)(2,1)}, bf16[4,2,24,1536]{3,2,0,1:T(8,128)(2,1)}, u32[]{:S(2)}, u32[]{:S(2)}) %collective-permute-start.23) | collective-permute-done | bytes 589856 | tf_op jit(solution)/shard_map/ppermute | solution.py:110
  241.8 1.6 fusion
  245.6 1.3 fusion.2
  246.9 1.5 collective-permute-start.25
  250.8 1.3 collective-permute-start.35
  252.1 2.1 collective-permute-done.27
  254.2 5.1 %collective-permute-done.25 = bf16[4,24,1536]{2,1,0:T(8,128)(2,1)S(1)} collective-permute-done((bf16[4,24,1536]{2,1,0:T(8,128)(2,1)S(1)}, bf16[4,24,1536]{2,1,0:T(8,128)(2,1)S(1)}, u32[]{:S(2)}, u32[]{:S(2)}) %collective-permute-start.25) | collective-permute-done | bytes 294944 | tf_op jit(solution)/shard_map/ppermute | solution.py:110
  259.4 1.6 collective-permute-start.31
  262.1 1.5 collective-permute-start.29
  263.6 1.6 collective-permute-start.28
  266.1 4.0 %collective-permute-start.36 = (bf16[48,3072]{1,0:T(8,128)(2,1)S(1)}, bf16[48,3072]{1,0:T(8,128)(2,1)S(1)}, u32[]{:S(2)}, u32[]{:S(2)}) collective-permute-start(bf16[48,3072]{1,0:T(8,128)(2,1)S(1)} %dynamic-slice_bitcast_fusion.5), channel_id=1, source_target_pairs={{0,12},{1,13},{2,14},{3,15},{4,8},{5,9},{6,10},{7,11},{8,4},{9,5},... | collective-permute-start | bytes 884744 | tf_op jit(solution)/shard_map/ppermute | solution.py:110
  270.1 1.3 collective-permute-done.29
  271.6 2.5 collective-permute-start.32
  274.2 5.7 %collective-permute-start.34 = (bf16[24,3072]{1,0:T(8,128)(2,1)S(1)}, bf16[24,3072]{1,0:T(8,128)(2,1)S(1)}, u32[]{:S(2)}, u32[]{:S(2)}) collective-permute-start(bf16[24,3072]{1,0:T(8,128)(2,1)S(1)} %dynamic-slice_bitcast_fusion.10), channel_id=1, source_target_pairs={{0,12},{1,13},{2,14},{3,15},{4,8},{5,9},{6,10},{7,11},{8,4},{9,5},... | collective-permute-start | bytes 442376 | tf_op jit(solution)/shard_map/ppermute | solution.py:110
  280.0 2.7 collective-permute-done.32
  282.7 5.8 %collective-permute-start.33 = (bf16[16,2304]{1,0:T(8,128)(2,1)S(1)}, bf16[16,2304]{1,0:T(8,128)(2,1)S(1)}, u32[]{:S(2)}, u32[]{:S(2)}) collective-permute-start(bf16[16,2304]{1,0:T(8,128)(2,1)S(1)} %dynamic-slice_bitcast_fusion.12), channel_id=1, source_target_pairs={{0,12},{1,13},{2,14},{3,15},{4,8},{5,9},{6,10},{7,11},{8,4},{9,5},... | collective-permute-start | bytes 221192 | tf_op jit(solution)/shard_map/ppermute | solution.py:110
  295.5 1.5 broadcast_select_fusion.2
  (340 shorter events, 58.6 us)
Async XLA Ops:
  7.2 13.0 %copy-start = (s32[2,256,100]{1,0,2:T(2,128)S(1)}, s32[2,256,100]{1,0,2:T(2,128)}, u32[]{:S(2)}) copy-start(s32[2,256,100]{1,0,2:T(2,128)} %param.50) | copy-start | bytes 614404
  7.2 9.8 %copy-start.52 = (bf16[2,1024,256]{2,1,0:T(8,128)(2,1)S(1)}, bf16[2,1024,256]{2,1,0:T(8,128)(2,1)}, u32[]{:S(2)}) copy-start(bf16[2,1024,256]{2,1,0:T(8,128)(2,1)} %param.26) | copy-start | bytes 3145732
  7.2 11.6 %copy-start.78 = (s32[2,3]{1,0:T(2,128)S(1)}, s32[2,3]{1,0:T(2,128)}, u32[]{:S(2)}) copy-start(s32[2,3]{1,0:T(2,128)} %param.48) | copy-start | bytes 76
  7.2 11.8 %copy-start.63 = (s32[2,2,512]{2,1,0:T(2,128)S(1)}, s32[2,2,512]{2,1,0:T(2,128)}, u32[]{:S(2)}) copy-start(s32[2,2,512]{2,1,0:T(2,128)} %param.51) | copy-start | bytes 24580
  7.2 11.8 %copy-start.77 = (bf16[2,320,128]{2,1,0:T(8,128)(2,1)S(1)}, bf16[2,320,128]{2,1,0:T(8,128)(2,1)}, u32[]{:S(2)}) copy-start(bf16[2,320,128]{2,1,0:T(8,128)(2,1)} %param.47) | copy-start | bytes 491524
  7.2 118.3 %all-gather.2.cloned.1.call-start = ((), (), s32[]{:S(2)}) async-start(), calls=%async_computation.1 | async-start | bytes 9732096 | tf_op jit(solution)/shard_map/all_gather | solution.py:1062
  10.1 9.8 %copy-start.65 = (bf16[8]{0:T(256)(128)(2,1)S(1)}, bf16[8]{0:T(256)(128)(2,1)}, u32[]{:S(2)}) copy-start(bf16[8]{0:T(256)(128)(2,1)} %param.46) | copy-start | bytes 52
  10.1 9.8 %copy-start.66 = (bf16[24]{0:T(256)(128)(2,1)S(1)}, bf16[24]{0:T(256)(128)(2,1)}, u32[]{:S(2)}) copy-start(bf16[24]{0:T(256)(128)(2,1)} %param.44) | copy-start | bytes 148
  10.1 9.8 %copy-start.67 = (bf16[24]{0:T(256)(128)(2,1)S(1)}, bf16[24]{0:T(256)(128)(2,1)}, u32[]{:S(2)}) copy-start(bf16[24]{0:T(256)(128)(2,1)} %param.43) | copy-start | bytes 148
  10.1 9.8 %copy-start.68 = (bf16[24]{0:T(256)(128)(2,1)S(1)}, bf16[24]{0:T(256)(128)(2,1)}, u32[]{:S(2)}) copy-start(bf16[24]{0:T(256)(128)(2,1)} %param.42) | copy-start | bytes 148
  10.1 9.8 %copy-start.69 = (bf16[24]{0:T(256)(128)(2,1)S(1)}, bf16[24]{0:T(256)(128)(2,1)}, u32[]{:S(2)}) copy-start(bf16[24]{0:T(256)(128)(2,1)} %param.38) | copy-start | bytes 148
  10.1 9.8 %copy-start.70 = (bf16[24]{0:T(256)(128)(2,1)S(1)}, bf16[24]{0:T(256)(128)(2,1)}, u32[]{:S(2)}) copy-start(bf16[24]{0:T(256)(128)(2,1)} %param.37) | copy-start | bytes 148
  10.2 9.8 %copy-start.71 = (bf16[24]{0:T(256)(128)(2,1)S(1)}, bf16[24]{0:T(256)(128)(2,1)}, u32[]{:S(2)}) copy-start(bf16[24]{0:T(256)(128)(2,1)} %param.36) | copy-start | bytes 148
  10.2 9.8 %copy-start.72 = (bf16[48]{0:T(256)(128)(2,1)S(1)}, bf16[48]{0:T(256)(128)(2,1)}, u32[]{:S(2)}) copy-start(bf16[48]{0:T(256)(128)(2,1)} %param.34) | copy-start | bytes 292
  10.2 9.8 %copy-start.73 = (bf16[24]{0:T(256)(128)(2,1)S(1)}, bf16[24]{0:T(256)(128)(2,1)}, u32[]{:S(2)}) copy-start(bf16[24]{0:T(256)(128)(2,1)} %param.32) | copy-start | bytes 148
  10.2 9.8 %copy-start.74 = (bf16[24]{0:T(256)(128)(2,1)S(1)}, bf16[24]{0:T(256)(128)(2,1)}, u32[]{:S(2)}) copy-start(bf16[24]{0:T(256)(128)(2,1)} %param.31) | copy-start | bytes 148
  10.2 9.8 %copy-start.75 = (bf16[16]{0:T(256)(128)(2,1)S(1)}, bf16[16]{0:T(256)(128)(2,1)}, u32[]{:S(2)}) copy-start(bf16[16]{0:T(256)(128)(2,1)} %param.29) | copy-start | bytes 100
  10.2 9.8 %copy-start.76 = (bf16[16]{0:T(256)(128)(2,1)S(1)}, bf16[16]{0:T(256)(128)(2,1)}, u32[]{:S(2)}) copy-start(bf16[16]{0:T(256)(128)(2,1)} %param.28) | copy-start | bytes 100
  10.3 231.6 %reduce-scatter.2.cloned.1.call-start = ((), (), s32[]{:S(2)}) async-start(), calls=%async_computation.2 | async-start | bytes 5898240 | tf_op jit(solution)/shard_map/reduce_scatter | solution.py:1225
  12.0 11.1 %collective-permute-start = (bf16[24,3072]{1,0:T(8,128)(2,1)S(1)}, bf16[24,3072]{1,0:T(8,128)(2,1)S(1)}, u32[]{:S(2)}, u32[]{:S(2)}) collective-permute-start(bf16[24,3072]{1,0:T(8,128)(2,1)S(1)} %constant_dynamic-update-slice_fusion), channel_id=1, source_target_pairs={{0,12},{1,13},{2,14},{3,15},{4,8},{5,9},{6,10},{7,11},{8,4},{9,5},... | collective-permute-start | bytes 442376 | tf_op jit(solution)/shard_map/ppermute | solution.py:110
  17.1 26.8 %collective-permute-start.6 = (bf16[1024,256]{1,0:T(8,128)(2,1)S(1)}, bf16[1024,256]{1,0:T(8,128)(2,1)S(1)}, u32[]{:S(2)}, u32[]{:S(2)}) collective-permute-start(bf16[1024,256]{1,0:T(8,128)(2,1)S(1)} %get-tuple-element.223), channel_id=1, source_target_pairs={{0,16},{1,17},{2,18},{3,19},{4,20},{5,21},{6,22},{7,23},{8,24},{9,... | collective-permute-start | bytes 1572872 | tf_op jit(solution)/shard_map/ppermute | solution.py:110
  20.2 73.2 %copy-start.61 = (s32[512]{0:T(512)}, s32[512]{0:T(512)S(1)}, u32[]{:S(2)}) copy-start(s32[512]{0:T(512)S(1)} %fusion.44) | copy-start | bytes 6148
  23.3 16.2 %collective-permute-start.1 = (bf16[2,24,3072]{2,1,0:T(8,128)(2,1)S(1)}, bf16[2,24,3072]{2,1,0:T(8,128)(2,1)S(1)}, u32[]{:S(2)}, u32[]{:S(2)}) collective-permute-start(bf16[2,24,3072]{2,1,0:T(8,128)(2,1)S(1)} %broadcast_select_fusion.8), channel_id=1, source_target_pairs={{0,4},{1,5},{2,6},{3,7},{4,0},{5,1},{6,2},{7,3},{8,12},{9,13},{10,... | collective-permute-start | bytes 884744 | tf_op jit(solution)/shard_map/ppermute | solution.py:110
  24.1 14.8 %collective-permute-start.2 = (bf16[16,2304]{1,0:T(8,128)(2,1)S(1)}, bf16[16,2304]{1,0:T(8,128)(2,1)S(1)}, u32[]{:S(2)}, u32[]{:S(2)}) collective-permute-start(bf16[16,2304]{1,0:T(8,128)(2,1)S(1)} %constant_dynamic-update-slice_fusion.2), channel_id=1, source_target_pairs={{0,12},{1,13},{2,14},{3,15},{4,8},{5,9},{6,10},{7,11},{8,4},{9,5},... | collective-permute-start | bytes 221192 | tf_op jit(solution)/shard_map/ppermute | solution.py:110
  39.8 13.3 %collective-permute-start.3 = (bf16[4,24,1536]{2,1,0:T(8,128)(2,1)S(1)}, bf16[4,24,1536]{2,1,0:T(8,128)(2,1)S(1)}, u32[]{:S(2)}, u32[]{:S(2)}) collective-permute-start(bf16[4,24,1536]{2,1,0:T(8,128)(2,1)S(1)} %get-tuple-element.231), channel_id=1, source_target_pairs={{0,2},{1,3},{2,0},{3,1},{4,6},{5,7},{6,4},{7,5},{8,10},{9,11},{10,... | collective-permute-start | bytes 884744 | tf_op jit(solution)/shard_map/ppermute | solution.py:110
  41.3 12.6 %collective-permute-start.4 = (bf16[4,24,1536]{2,1,0:T(8,128)(2,1)S(1)}, bf16[4,24,1536]{2,1,0:T(8,128)(2,1)S(1)}, u32[]{:S(2)}, u32[]{:S(2)}) collective-permute-start(bf16[4,24,1536]{2,1,0:T(8,128)(2,1)S(1)} %get-tuple-element.230), channel_id=1, source_target_pairs={{0,16},{1,17},{2,18},{3,19},{4,20},{5,21},{6,22},{7,23},{8,24},{9,... | collective-permute-start | bytes 884744 | tf_op jit(solution)/shard_map/ppermute | solution.py:110
  42.2 10.7 %collective-permute-start.5 = (bf16[2,16,2304]{2,1,0:T(8,128)(2,1)S(1)}, bf16[2,16,2304]{2,1,0:T(8,128)(2,1)S(1)}, u32[]{:S(2)}, u32[]{:S(2)}) collective-permute-start(bf16[2,16,2304]{2,1,0:T(8,128)(2,1)S(1)} %broadcast_select_fusion.10), channel_id=1, source_target_pairs={{0,4},{1,5},{2,6},{3,7},{4,0},{5,1},{6,2},{7,3},{8,12},{9,13},{10,... | collective-permute-start | bytes 442376 | tf_op jit(solution)/shard_map/ppermute | solution.py:110
  44.0 9.9 %copy-start.57 = (bf16[1024,256]{1,0:T(8,128)(2,1)}, bf16[1024,256]{1,0:T(8,128)(2,1)S(1)}, u32[]{:S(2)}) copy-start(bf16[1024,256]{1,0:T(8,128)(2,1)S(1)} %collective-permute-done.6) | copy-start | bytes 1572868
  54.0 18.8 %collective-permute-start.8 = (bf16[2,4,24,1536]{3,2,1,0:T(8,128)(2,1)S(1)}, bf16[2,4,24,1536]{3,2,1,0:T(8,128)(2,1)S(1)}, u32[]{:S(2)}, u32[]{:S(2)}) collective-permute-start(bf16[2,4,24,1536]{3,2,1,0:T(8,128)(2,1)S(1)} %broadcast_select_fusion.4), channel_id=1, source_target_pairs={{0,2},{1,3},{2,0},{3,1},{4,6},{5,7},{6,4},{7,5},{8,10},{9,11},{10,... | collective-permute-start | bytes 1769480 | tf_op jit(solution)/shard_map/ppermute | solution.py:110
  55.9 16.9 %collective-permute-start.7 = (bf16[4,2,24,1536]{3,2,1,0:T(8,128)(2,1)S(1)}, bf16[4,2,24,1536]{3,2,1,0:T(8,128)(2,1)S(1)}, u32[]{:S(2)}, u32[]{:S(2)}) collective-permute-start(bf16[4,2,24,1536]{3,2,1,0:T(8,128)(2,1)S(1)} %broadcast_select_fusion.5), channel_id=1, source_target_pairs={{0,16},{1,17},{2,18},{3,19},{4,20},{5,21},{6,22},{7,23},{8,24},{9,... | collective-permute-start | bytes 1769480 | tf_op jit(solution)/shard_map/ppermute | solution.py:110
  56.1 16.7 %collective-permute-start.9 = (bf16[4,16,1280]{2,1,0:T(8,128)(2,1)S(1)}, bf16[4,16,1280]{2,1,0:T(8,128)(2,1)S(1)}, u32[]{:S(2)}, u32[]{:S(2)}) collective-permute-start(bf16[4,16,1280]{2,1,0:T(8,128)(2,1)S(1)} %slice.213), channel_id=1, source_target_pairs={{0,2},{1,3},{2,0},{3,1},{4,6},{5,7},{6,4},{7,5},{8,10},{9,11},{10,... | collective-permute-start | bytes 491528 | tf_op jit(solution)/shard_map/ppermute | solution.py:110
  57.3 11.8 %collective-permute-start.10 = (bf16[4,32,512]{2,1,0:T(8,128)(2,1)S(1)}, bf16[4,32,512]{2,1,0:T(8,128)(2,1)S(1)}, u32[]{:S(2)}, u32[]{:S(2)}) collective-permute-start(bf16[4,32,512]{2,1,0:T(8,128)(2,1)S(1)} %bitcast.267), channel_id=1, source_target_pairs={{0,16},{1,17},{2,18},{3,19},{4,20},{5,21},{6,22},{7,23},{8,24},{9,... | collective-permute-start | bytes 393224 | tf_op jit(solution)/shard_map/ppermute | solution.py:110
  72.9 13.9 %collective-permute-start.12 = (bf16[2,4,32,512]{3,2,1,0:T(8,128)(2,1)S(1)}, bf16[2,4,32,512]{3,2,1,0:T(8,128)(2,1)S(1)}, u32[]{:S(2)}, u32[]{:S(2)}) collective-permute-start(bf16[2,4,32,512]{3,2,1,0:T(8,128)(2,1)S(1)} %broadcast_select_fusion.9), channel_id=1, source_target_pairs={{0,2},{1,3},{2,0},{3,1},{4,6},{5,7},{6,4},{7,5},{8,10},{9,11},{10,... | collective-permute-start | bytes 786440 | tf_op jit(solution)/shard_map/ppermute | solution.py:110
  74.6 16.6 %collective-permute-start.11 = (bf16[4,2,16,1280]{3,2,1,0:T(8,128)(2,1)S(1)}, bf16[4,2,16,1280]{3,2,1,0:T(8,128)(2,1)S(1)}, u32[]{:S(2)}, u32[]{:S(2)}) collective-permute-start(bf16[4,2,16,1280]{3,2,1,0:T(8,128)(2,1)S(1)} %broadcast_select_fusion.7), channel_id=1, source_target_pairs={{0,16},{1,17},{2,18},{3,19},{4,20},{5,21},{6,22},{7,23},{8,24},{9,... | collective-permute-start | bytes 983048 | tf_op jit(solution)/shard_map/ppermute | solution.py:110
  76.2 29.3 %collective-permute-start.15 = (bf16[2,4,2,24,1536]{4,3,2,1,0:T(8,128)(2,1)S(1)}, bf16[2,4,2,24,1536]{4,3,2,1,0:T(8,128)(2,1)}, u32[]{:S(2)}, u32[]{:S(2)}) collective-permute-start(bf16[2,4,2,24,1536]{4,3,2,1,0:T(8,128)(2,1)S(1)} %broadcast_select_fusion.1), channel_id=1, source_target_pairs={{0,1},{1,0},{2,3},{3,2},{4,5},{5,4},{6,7},{7,6},{8,9},{9,8},{10,11... | collective-permute-start | bytes 3538952 | tf_op jit(solution)/shard_map/ppermute | solution.py:110
  76.3 29.3 %collective-permute-start.16 = (bf16[2,4,2,24,1536]{4,3,2,1,0:T(8,128)(2,1)S(1)}, bf16[2,4,2,24,1536]{4,3,2,1,0:T(8,128)(2,1)}, u32[]{:S(2)}, u32[]{:S(2)}) collective-permute-start(bf16[2,4,2,24,1536]{4,3,2,1,0:T(8,128)(2,1)S(1)} %broadcast_select_fusion), channel_id=1, source_target_pairs={{0,1},{1,0},{2,3},{3,2},{4,5},{5,4},{6,7},{7,6},{8,9},{9,8},{10,11... | collective-permute-start | bytes 3538952 | tf_op jit(solution)/shard_map/ppermute | solution.py:110
  91.3 3.3 %collective-permute-start.13 = (bf16[2,4,2,16,1280]{4,3,2,1,0:T(8,128)(2,1)S(1)}, bf16[2,4,2,16,1280]{4,3,2,1,0:T(8,128)(2,1)}, u32[]{:S(2)}, u32[]{:S(2)}) collective-permute-start(bf16[2,4,2,16,1280]{4,3,2,1,0:T(8,128)(2,1)S(1)} %broadcast_select_fusion.3), channel_id=1, source_target_pairs={{0,1},{1,0},{2,3},{3,2},{4,5},{5,4},{6,7},{7,6},{8,9},{9,8},{10,11... | collective-permute-start | bytes 1966088 | tf_op jit(solution)/shard_map/ppermute | solution.py:110
  91.4 3.2 %collective-permute-start.14 = (bf16[2,4,2,32,512]{4,3,2,1,0:T(8,128)(2,1)}, bf16[2,4,2,32,512]{4,3,2,1,0:T(8,128)(2,1)}, u32[]{:S(2)}, u32[]{:S(2)}) collective-permute-start(bf16[2,4,2,32,512]{4,3,2,1,0:T(8,128)(2,1)} %broadcast_select_fusion.6), channel_id=1, source_target_pairs={{0,1},{1,0},{2,3},{3,2},{4,5},{5,4},{6,7},{7,6},{8,9},{9,8},{10,11... | collective-permute-start | bytes 1572872 | tf_op jit(solution)/shard_map/ppermute | solution.py:110
  93.5 19.7 %copy-start.26 = (s32[512,1]{1,0:T(8,128)}, s32[512,1]{1,0:T(8,128)S(1)}, u32[]{:S(2)}) copy-start(s32[512,1]{1,0:T(8,128)S(1)} %copy.83.col_ref) | copy-start | bytes 6148
  122.4 16.1 %copy-start.46 = (f32[6,8,512]{2,1,0:T(8,128)}, f32[6,8,512]{2,1,0:T(8,128)S(1)}, u32[]{:S(2)}) copy-start(f32[6,8,512]{2,1,0:T(8,128)S(1)} %get-tuple-element.158.log_ref) | copy-start | bytes 294916
  157.6 13.3 %collective-permute-start.18 = (bf16[384,3072]{1,0:T(8,128)(2,1)S(1)}, bf16[384,3072]{1,0:T(8,128)(2,1)S(1)}, u32[]{:S(2)}, u32[]{:S(2)}) collective-permute-start(bf16[384,3072]{1,0:T(8,128)(2,1)S(1)} %bitcast.260), channel_id=1, source_target_pairs={{0,1},{1,0},{2,3},{3,2},{4,5},{5,4},{6,7},{7,6},{8,9},{9,8},{10,11... | collective-permute-start | bytes 7077896 | tf_op jit(solution)/shard_map/ppermute | solution.py:110
  162.6 8.2 %collective-permute-start.17 = (bf16[1536,768]{1,0:T(8,128)(2,1)}, bf16[1536,768]{1,0:T(8,128)(2,1)S(1)}, u32[]{:S(2)}, u32[]{:S(2)}) collective-permute-start(bf16[1536,768]{1,0:T(8,128)(2,1)} %bitcast.261), channel_id=1, source_target_pairs={{0,1},{1,0},{2,3},{3,2},{4,5},{5,4},{6,7},{7,6},{8,9},{9,8},{10,11... | collective-permute-start | bytes 7077896 | tf_op jit(solution)/shard_map/ppermute | solution.py:110
  163.8 7.1 %collective-permute-start.19 = (f32[2]{0:T(128)S(1)}, f32[2]{0:T(128)S(1)}, u32[]{:S(2)}, u32[]{:S(2)}) collective-permute-start(f32[2]{0:T(128)S(1)} %broadcast_select_fusion.11), channel_id=1, source_target_pairs={{0,16},{1,17},{2,18},{3,19},{4,20},{5,21},{6,22},{7,23},{8,24},{9,... | collective-permute-start | bytes 32 | tf_op jit(solution)/shard_map/ppermute | solution.py:110
  174.5 14.2 %copy-start.8 = (bf16[512,768]{1,0:T(8,128)(2,1)S(1)}, bf16[512,768]{1,0:T(8,128)(2,1)}, u32[]{:S(2)}) copy-start(bf16[512,768]{1,0:T(8,128)(2,1)} %get-tuple-element.131.refs_0_) | copy-start | bytes 2359300
  174.5 14.2 %copy-start.16 = (bf16[512,768]{1,0:T(8,128)(2,1)S(1)}, bf16[512,768]{1,0:T(8,128)(2,1)}, u32[]{:S(2)}) copy-start(bf16[512,768]{1,0:T(8,128)(2,1)} %copy-done.15) | copy-start | bytes 2359300
  174.5 14.2 %copy-start.20 = (bf16[512,768]{1,0:T(8,128)(2,1)S(1)}, bf16[512,768]{1,0:T(8,128)(2,1)}, u32[]{:S(2)}) copy-start(bf16[512,768]{1,0:T(8,128)(2,1)} %copy-done.19) | copy-start | bytes 2359300
  196.9 9.7 %collective-permute-start.20 = (bf16[384,3072]{1,0:T(8,128)(2,1)}, bf16[384,3072]{1,0:T(8,128)(2,1)}, u32[]{:S(2)}, u32[]{:S(2)}) collective-permute-start(bf16[384,3072]{1,0:T(8,128)(2,1)} %get-tuple-element.162), channel_id=1, source_target_pairs={{0,1},{1,0},{2,3},{3,2},{4,5},{5,4},{6,7},{7,6},{8,9},{9,8},{10,11... | collective-permute-start | bytes 7077896 | tf_op jit(solution)/shard_map/ppermute | solution.py:110
  218.1 23.7 %collective-permute-start.21 = (bf16[256,2304]{1,0:T(8,128)(2,1)}, bf16[256,2304]{1,0:T(8,128)(2,1)}, u32[]{:S(2)}, u32[]{:S(2)}) collective-permute-start(bf16[256,2304]{1,0:T(8,128)(2,1)} %bitcast.56), channel_id=1, source_target_pairs={{0,1},{1,0},{2,3},{3,2},{4,5},{5,4},{6,7},{7,6},{8,9},{9,8},{10,11... | collective-permute-start | bytes 3538952 | tf_op jit(solution)/shard_map/ppermute | solution.py:110
  223.6 18.0 %collective-permute-start.23 = (bf16[4,2,24,1536]{3,2,0,1:T(8,128)(2,1)}, bf16[4,2,24,1536]{3,2,0,1:T(8,128)(2,1)}, u32[]{:S(2)}, u32[]{:S(2)}) collective-permute-start(bf16[4,2,24,1536]{3,2,0,1:T(8,128)(2,1)} %bitcast.242), channel_id=1, source_target_pairs={{0,16},{1,17},{2,18},{3,19},{4,20},{5,21},{6,22},{7,23},{8,24},{9,... | collective-permute-start | bytes 1769480 | tf_op jit(solution)/shard_map/ppermute | solution.py:110
  225.9 15.9 %collective-permute-start.22 = (bf16[2,4,24,1536]{3,2,1,0:T(8,128)(2,1)}, bf16[2,4,24,1536]{3,2,1,0:T(8,128)(2,1)}, u32[]{:S(2)}, u32[]{:S(2)}) collective-permute-start(bf16[2,4,24,1536]{3,2,1,0:T(8,128)(2,1)} %dynamic-slice_bitcast_fusion.2), channel_id=1, source_target_pairs={{0,2},{1,3},{2,0},{3,1},{4,6},{5,7},{6,4},{7,5},{8,10},{9,11},{10,... | collective-permute-start | bytes 1769480 | tf_op jit(solution)/shard_map/ppermute | solution.py:110
  243.7 15.7 %collective-permute-start.26 = (bf16[2,4,16,1280]{3,2,1,0:T(8,128)(2,1)S(1)}, bf16[2,4,16,1280]{3,2,1,0:T(8,128)(2,1)S(1)}, u32[]{:S(2)}, u32[]{:S(2)}) collective-permute-start(bf16[2,4,16,1280]{3,2,1,0:T(8,128)(2,1)S(1)} %dynamic-slice_bitcast_fusion.4), channel_id=1, source_target_pairs={{0,2},{1,3},{2,0},{3,1},{4,6},{5,7},{6,4},{7,5},{8,10},{9,11},{10,... | collective-permute-start | bytes 983048 | tf_op jit(solution)/shard_map/ppermute | solution.py:110
  244.9 9.3 %collective-permute-start.27 = (bf16[4,2,16,1024]{3,2,1,0:T(8,128)(2,1)S(1)}, bf16[4,2,16,1024]{3,2,1,0:T(8,128)(2,1)S(1)}, u32[]{:S(2)}, u32[]{:S(2)}) collective-permute-start(bf16[4,2,16,1024]{3,2,1,0:T(8,128)(2,1)S(1)} %dynamic-slice_bitcast_fusion.8), channel_id=1, source_target_pairs={{0,16},{1,17},{2,18},{3,19},{4,20},{5,21},{6,22},{7,23},{8,24},{9,... | collective-permute-start | bytes 786440 | tf_op jit(solution)/shard_map/ppermute | solution.py:110
  246.9 12.4 %collective-permute-start.25 = (bf16[4,24,1536]{2,1,0:T(8,128)(2,1)S(1)}, bf16[4,24,1536]{2,1,0:T(8,128)(2,1)S(1)}, u32[]{:S(2)}, u32[]{:S(2)}) collective-permute-start(bf16[4,24,1536]{2,1,0:T(8,128)(2,1)S(1)} %dynamic-slice_bitcast_fusion.6), channel_id=1, source_target_pairs={{0,2},{1,3},{2,0},{3,1},{4,6},{5,7},{6,4},{7,5},{8,10},{9,11},{10,... | collective-permute-start | bytes 884744 | tf_op jit(solution)/shard_map/ppermute | solution.py:110
  249.7 9.6 %collective-permute-start.24 = (bf16[4,24,1536]{2,1,0:T(8,128)(2,1)S(1)}, bf16[4,24,1536]{2,1,0:T(8,128)(2,1)S(1)}, u32[]{:S(2)}, u32[]{:S(2)}) collective-permute-start(bf16[4,24,1536]{2,1,0:T(8,128)(2,1)S(1)} %dynamic-slice_bitcast_fusion.7), channel_id=1, source_target_pairs={{0,16},{1,17},{2,18},{3,19},{4,20},{5,21},{6,22},{7,23},{8,24},{9,... | collective-permute-start | bytes 884744 | tf_op jit(solution)/shard_map/ppermute | solution.py:110
  250.8 15.1 %collective-permute-start.35 = (bf16[2,48,3072]{2,1,0:T(8,128)(2,1)S(1)}, bf16[2,48,3072]{2,1,0:T(8,128)(2,1)S(1)}, u32[]{:S(2)}, u32[]{:S(2)}) collective-permute-start(bf16[2,48,3072]{2,1,0:T(8,128)(2,1)S(1)} %fusion.10), channel_id=1, source_target_pairs={{0,4},{1,5},{2,6},{3,7},{4,0},{5,1},{6,2},{7,3},{8,12},{9,13},{10,... | collective-permute-start | bytes 1769480 | tf_op jit(solution)/shard_map/ppermute | solution.py:110
  259.4 10.6 %collective-permute-start.31 = (bf16[4,16,1024]{2,1,0:T(8,128)(2,1)S(1)}, bf16[4,16,1024]{2,1,0:T(8,128)(2,1)S(1)}, u32[]{:S(2)}, u32[]{:S(2)}) collective-permute-start(bf16[4,16,1024]{2,1,0:T(8,128)(2,1)S(1)} %dynamic-slice_bitcast_fusion.11), channel_id=1, source_target_pairs={{0,2},{1,3},{2,0},{3,1},{4,6},{5,7},{6,4},{7,5},{8,10},{9,11},{10,... | collective-permute-start | bytes 393224 | tf_op jit(solution)/shard_map/ppermute | solution.py:110
  261.2 8.9 %collective-permute-start.30 = (bf16[4,16,1280]{2,1,0:T(8,128)(2,1)S(1)}, bf16[4,16,1280]{2,1,0:T(8,128)(2,1)S(1)}, u32[]{:S(2)}, u32[]{:S(2)}) collective-permute-start(bf16[4,16,1280]{2,1,0:T(8,128)(2,1)S(1)} %dynamic-slice_bitcast_fusion.9), channel_id=1, source_target_pairs={{0,16},{1,17},{2,18},{3,19},{4,20},{5,21},{6,22},{7,23},{8,24},{9,... | collective-permute-start | bytes 491528 | tf_op jit(solution)/shard_map/ppermute | solution.py:110
  262.1 9.3 %collective-permute-start.29 = (bf16[2,24,3072]{2,1,0:T(8,128)(2,1)S(1)}, bf16[2,24,3072]{2,1,0:T(8,128)(2,1)S(1)}, u32[]{:S(2)}, u32[]{:S(2)}) collective-permute-start(bf16[2,24,3072]{2,1,0:T(8,128)(2,1)S(1)} %fusion.29), channel_id=1, source_target_pairs={{0,4},{1,5},{2,6},{3,7},{4,0},{5,1},{6,2},{7,3},{8,12},{9,13},{10,... | collective-permute-start | bytes 884744 | tf_op jit(solution)/shard_map/ppermute | solution.py:110
  263.6 31.8 %collective-permute-start.28 = (bf16[1024,256]{1,0:T(8,128)(2,1)S(1)}, bf16[1024,256]{1,0:T(8,128)(2,1)S(1)}, u32[]{:S(2)}, u32[]{:S(2)}) collective-permute-start(bf16[1024,256]{1,0:T(8,128)(2,1)S(1)} %copy-done.56), channel_id=1, source_target_pairs={{0,16},{1,17},{2,18},{3,19},{4,20},{5,21},{6,22},{7,23},{8,24},{9,... | collective-permute-start | bytes 1572872 | tf_op jit(solution)/shard_map/ppermute | solution.py:110
  266.1 30.9 %collective-permute-start.36 = (bf16[48,3072]{1,0:T(8,128)(2,1)S(1)}, bf16[48,3072]{1,0:T(8,128)(2,1)S(1)}, u32[]{:S(2)}, u32[]{:S(2)}) collective-permute-start(bf16[48,3072]{1,0:T(8,128)(2,1)S(1)} %dynamic-slice_bitcast_fusion.5), channel_id=1, source_target_pairs={{0,12},{1,13},{2,14},{3,15},{4,8},{5,9},{6,10},{7,11},{8,4},{9,5},... | collective-permute-start | bytes 884744 | tf_op jit(solution)/shard_map/ppermute | solution.py:110
  271.6 11.1 %collective-permute-start.32 = (bf16[2,16,2304]{2,1,0:T(8,128)(2,1)S(1)}, bf16[2,16,2304]{2,1,0:T(8,128)(2,1)S(1)}, u32[]{:S(2)}, u32[]{:S(2)}) collective-permute-start(bf16[2,16,2304]{2,1,0:T(8,128)(2,1)S(1)} %fusion.37), channel_id=1, source_target_pairs={{0,4},{1,5},{2,6},{3,7},{4,0},{5,1},{6,2},{7,3},{8,12},{9,13},{10,... | collective-permute-start | bytes 442376 | tf_op jit(solution)/shard_map/ppermute | solution.py:110
  274.2 21.2 %copy-start.47 = (f32[1024,256]{1,0:T(8,128)S(1)}, f32[1024,256]{1,0:T(8,128)}, u32[]{:S(2)}) copy-start(f32[1024,256]{1,0:T(8,128)} %reshape.268) | copy-start | bytes 3145732
  274.2 14.3 %collective-permute-start.34 = (bf16[24,3072]{1,0:T(8,128)(2,1)S(1)}, bf16[24,3072]{1,0:T(8,128)(2,1)S(1)}, u32[]{:S(2)}, u32[]{:S(2)}) collective-permute-start(bf16[24,3072]{1,0:T(8,128)(2,1)S(1)} %dynamic-slice_bitcast_fusion.10), channel_id=1, source_target_pairs={{0,12},{1,13},{2,14},{3,15},{4,8},{5,9},{6,10},{7,11},{8,4},{9,5},... | collective-permute-start | bytes 442376 | tf_op jit(solution)/shard_map/ppermute | solution.py:110
  282.7 8.1 %collective-permute-start.33 = (bf16[16,2304]{1,0:T(8,128)(2,1)S(1)}, bf16[16,2304]{1,0:T(8,128)(2,1)S(1)}, u32[]{:S(2)}, u32[]{:S(2)}) collective-permute-start(bf16[16,2304]{1,0:T(8,128)(2,1)S(1)} %dynamic-slice_bitcast_fusion.12), channel_id=1, source_target_pairs={{0,12},{1,13},{2,14},{3,15},{4,8},{5,9},{6,10},{7,11},{8,4},{9,5},... | collective-permute-start | bytes 221192 | tf_op jit(solution)/shard_map/ppermute | solution.py:110
  (59 other events, 229.8 us)
Sparse Core Ops, SparseCore 0:
  11.6 97.4 all-gather.1
  174.6 57.7 reduce-scatter.1
